TPU v7x, 256 devices: a whole 4x4x8 slice. The times are simulated.
256 devices in a mesh: dp: 16 (over y, x), mp: 16 (over z, core).
Axes of the slice: x: 4, y: 4, z: 8, core: 2. Of those that a mesh axis runs over, the one named last changes fastest.
Arguments:
- output_cotangent: bfloat16 [16384, 8192], P(('dp', 'mp')), may hold values from -6 to 6
- acts: bfloat16 [16384, 8192], P('dp', 'mp'), may hold values from -6 to 6
- output_weight: bfloat16 [8192, 8192], P('mp'), may hold values from -0.0625 to 0.0625
- adapter_down_weight: bfloat16 [64, 8192, 16], P('dp', 'mp'), may hold values from -0.0625 to 0.0625
- adapter_up_weight: bfloat16 [64, 16, 8192], P('dp', None, 'mp'), may hold values from -0.0625 to 0.0625
- counts: int32 [64], replicated, may hold values from 1 to 4224, as said below
- block_tenant_map: int32 [128], replicated, may hold values from 0 to 63, as said below
- owner: int32 [64], replicated, may hold values from 0 to 63, each once
Outputs:
- input_gradient: bfloat16 [16384, 8192], P('dp', 'mp')
- grad_down: float32 [64, 8192, 16], P('dp', 'mp')
- grad_up: float32 [64, 16, 8192], P('dp', None, 'mp')
Inputs may be any that keep to these rules, and one draw needn't show every extreme that they name: Each tenant's blocks stand together in block_tenant_map, and every tenant has one block or more. `counts`: A tenant with n blocks has a count from 128 * (n - 1) + 1 to 128 * n.
All inputs are finite; a program needn't handle non-finite values.
Results may differ from a plain program's by a relative error of at most 0.0034.
Values may be sent and summed in bfloat16 or wider, within the bound.
No kernel may reach another device: no remote copies, remote signals or barrier semaphores. Data moves between devices by JAX's collectives and lax.ppermute only.
A program may use at most 128 MiB of HBM per device.

v0:
```python
import jax
import jax.numpy as jnp
from jax import lax
from jax.sharding import PartitionSpec as P

BLOCK = 128


adapter_scale = 2.0


def per_device(
    output_cotangent,
    acts,
    output_weight,
    adapter_down_weight,
    adapter_up_weight,
    counts,
    block_tenant_map,
    owner,
):
    gathered = lax.all_gather(output_cotangent, "mp", axis=0, tiled=True)
    row_block_values, width = gathered.shape
    nblk_loc = row_block_values // BLOCK
    resident_features = acts.shape[1]
    resident_columns = adapter_up_weight.shape[2]
    slot_count = owner.shape[0]
    nblocks = block_tenant_map.shape[0]
    group = lax.axis_index("dp")
    column_idx = lax.axis_index("mp")
    first_block = group * nblk_loc
    local_map = lax.dynamic_slice_in_dim(block_tenant_map, first_block, nblk_loc)
    global_ids = jnp.arange(nblocks, dtype=jnp.int32)
    local_ids = first_block + jnp.arange(nblk_loc, dtype=jnp.int32)
    same = (local_map[:, None] == block_tenant_map[None, :]) & (
        global_ids[None, :] < local_ids[:, None]
    )
    before = jnp.sum(same.astype(jnp.int32), axis=1)
    tenant_ids = jnp.arange(slot_count, dtype=jnp.int32)
    hit = local_map[:, None] == tenant_ids[None, :]
    limit = jnp.sum(jnp.where(hit, counts[None, :], 0), axis=1)
    slot_blk = jnp.sum(jnp.where(hit, owner[None, :], 0), axis=1)
    within = jnp.arange(BLOCK, dtype=jnp.int32)
    valid = before[:, None] * BLOCK + within[None, :] < limit[:, None]
    blocks_out = gathered.reshape(nblk_loc, BLOCK, width)
    masked_rows = jnp.where(valid[:, :, None], blocks_out, jnp.zeros_like(blocks_out))
    all_down, all_up = (
        lax.all_gather(adapter_down_weight, "dp", axis=0, tiled=True),
        lax.all_gather(adapter_up_weight, "dp", axis=0, tiled=True),
    )
    picker = (slot_blk[:, None] == tenant_ids[None, :]).astype(jnp.bfloat16)
    down_factor = jnp.einsum(
        "ns,shr->nhr", picker, all_down, preferred_element_type=jnp.float32
    ).astype(jnp.bfloat16)
    up_factor = jnp.einsum(
        "ns,srd->nrd", picker, all_up, preferred_element_type=jnp.float32
    ).astype(jnp.bfloat16)
    my_cols = lax.dynamic_slice_in_dim(
        masked_rows, column_idx * resident_columns, resident_columns, 2
    )
    activation_block = acts.reshape(nblk_loc, BLOCK, resident_features)
    low_part = jnp.einsum(
        "nbh,nhr->nbr", activation_block, down_factor, preferred_element_type=jnp.float32
    )
    back_part = jnp.einsum("nbd,nrd->nbr", my_cols, up_factor, preferred_element_type=jnp.float32)
    low_sum, back_sum = lax.psum((low_part, back_part), "mp")
    reduced_product = low_sum.astype(jnp.bfloat16)
    backward_term = back_sum.astype(jnp.bfloat16)
    frozen_term = lax.dot_general(
        masked_rows.reshape(row_block_values, width),
        output_weight,
        (((1,), (1,)), ((), ())),
        preferred_element_type=jnp.float32,
    )
    adapter_extra = jnp.einsum(
        "nbr,nhr->nbh", backward_term, down_factor, preferred_element_type=jnp.float32
    )
    input_gradient = (
        frozen_term + adapter_scale * adapter_extra.reshape(row_block_values, resident_features)
    ).astype(jnp.bfloat16)
    down_factor_block = adapter_scale * jnp.einsum(
        "fay,fat->fyt", activation_block, backward_term, preferred_element_type=jnp.float32
    )
    up_factor_block = adapter_scale * jnp.einsum(
        "wqk,wqj->wkj", reduced_product, my_cols, preferred_element_type=jnp.float32
    )
    resident_count = adapter_down_weight.shape[0]
    every_down, every_up, every_slot = (
        lax.all_gather(down_factor_block, "dp", axis=0, tiled=True),
        lax.all_gather(up_factor_block, "dp", axis=0, tiled=True),
        lax.all_gather(slot_blk, "dp", axis=0, tiled=True),
    )
    mine = group * resident_count + jnp.arange(resident_count, dtype=jnp.int32)
    select = (every_slot[None, :] == mine[:, None]).astype(jnp.float32)
    grad_down = jnp.einsum("mn,nhr->mhr", select, every_down, precision=lax.Precision.HIGHEST)
    grad_up = jnp.einsum("mn,nrd->mrd", select, every_up, precision=lax.Precision.HIGHEST)
    return (input_gradient, grad_down, grad_up)


def solution(mesh):
    in_specs = (
        P(("dp", "mp"), None),
        P("dp", "mp"),
        P("mp", None),
        P("dp", "mp", None),
        P("dp", None, "mp"),
        P(),
        P(),
        P(),
    )
    out_specs = (P("dp", "mp"), P("dp", "mp", None), P("dp", None, "mp"))
    return jax.shard_map(
        per_device, mesh=mesh, in_specs=in_specs, out_specs=out_specs, check_vma=False
    )
```

profile of v0, /device:TPU:1, one launch (start us, length us, event | category | flops | bytes accessed | tf_op | source)
XLA Modules:
  0.0 387.7 jit_solution(11326872808633132440)
XLA Ops:
  7.2 0.7 all-gather.10.cloned.1.call-update
  7.9 0.0 all-gather.8.cloned.1.call-start
  8.0 0.7 all-gather.8.cloned.1.call-update
  8.7 0.0 all-gather.6.cloned.1.call-start
  8.7 0.7 all-gather.6.cloned.1.call-update
  9.4 0.0 all-gather.14.cloned.1.call-start
  9.5 0.7 dynamic_slice.6
  10.2 0.9 select_reduce_fusion.1
  11.1 0.8 convert_reduce_fusion
  11.9 0.1 fusion.42
  12.0 48.6 %all-gather.10.cloned.1.call-done = bf16[64,512,16]{1,2,0:T(8,128)(2,1)} async-done(((bf16[4,512,16]{1,2,0:T(8,128)(2,1)}), bf16[64,512,16]{1,2,0:T(8,128)(2,1)}) %all-gather.10.cloned.1.call-update) | async-done | bytes 1048592 | tf_op jit(solution)/shard_map/all_gather | solution.py:48
  60.6 2.4 convolution_convert_fusion
  63.0 0.4 convolution_bitcast_fusion
  63.4 46.7 %all-gather.8.cloned.1.call-done = bf16[64,16,512]{2,1,0:T(8,128)(2,1)} async-done(((bf16[4,16,512]{2,1,0:T(8,128)(2,1)}), bf16[64,16,512]{2,1,0:T(8,128)(2,1)}) %all-gather.8.cloned.1.call-update) | async-done | bytes 1048592 | tf_op jit(solution)/shard_map/all_gather | solution.py:49
  110.1 2.4 convolution_convert_fusion.1
  112.5 96.0 %all-gather.6.cloned.1.call-done = bf16[1024,8192]{1,0:T(8,128)(2,1)} async-done(((bf16[64,8192]{1,0:T(8,128)(2,1)}), bf16[1024,8192]{1,0:T(8,128)(2,1)}) %all-gather.6.cloned.1.call-update) | async-done | bytes 16777232 | tf_op jit(solution)/shard_map/all_gather | solution.py:22
  208.5 1.7 fusion.14
  210.2 44.4 %all-reduce.3 = (bf16[8,128,16]{1,2,0:T(8,128)(2,1)S(1)}, bf16[8,128,16]{1,2,0:T(8,128)(2,1)S(1)}) all-reduce(f32[8,128,16]{1,2,0:T(8,128)S(1)} %fusion.14, f32[8,128,16]{1,2,0:T(8,128)S(1)} %convolution_bitcast_fusion), channel_id=1, replica_groups=mesh['dp'=16,'mp'=16] {'mp'}, use_global_device_ids=true, to_apply=%region_3.4 | all-reduce | flops 32768 | bytes 196608 | tf_op jit(solution)/shard_map/psum | solution.py:66
  254.6 2.3 convolution_multiply_fusion.1
  256.9 0.0 all-gather.12.cloned.1.call-start
  256.9 1.0 fusion.11
  257.9 0.6 dynamic-slice
  259.2 0.2 dynamic-update-slice
  259.4 12.5 %all-reduce = s32[128]{0:T(128)S(1)} all-reduce(s32[128]{0:T(128)S(1)} %dynamic-update-slice), channel_id=1, replica_groups=mesh['dp'=16,'mp'=16] {'dp'}, use_global_device_ids=true, to_apply=%add | all-reduce | flops 128 | bytes 1024
  271.9 0.5 convolution_multiply_fusion
  272.4 16.0 %fusion.8 = bf16[1024,512]{1,0:T(8,128)(2,1)} fusion(f32[8,128,512]{2,1,0:T(8,128)S(1)} %convolution_multiply_fusion, bf16[512,8192]{1,0:T(8,128)(2,1)} %param.10, bf16[1024,8192]{1,0:T(8,128)(2,1)} %all-gather.6.cloned.1.call-done, pred[1024]{0:T(1024)(128)(4,1)S(1)} %get-tuple-element.19), kind=kOutput, calls=%fused_computation.9 | convolution fusion | flops 8599371776 | bytes 28312576 | tf_op jit(solution)/shard_map/dot_general | solution.py:69
  288.3 27.7 %all-gather.14.cloned.1.call-done = f32[128,16,512]{2,1,0:T(8,128)} async-done(((f32[8,16,512]{2,1,0:T(8,128)}), f32[128,16,512]{2,1,0:T(8,128)}) %all-gather.14.cloned.1.call-update) | async-done | bytes 4194320 | tf_op jit(solution)/shard_map/all_gather | solution.py:90
  316.1 5.8 %fusion.4 = f32[4,16,512]{2,0,1:T(4,128)S(1)} fusion(f32[128,16,512]{2,1,0:T(8,128)} %all-gather.14.cloned.1.call-done, s32[128]{0:T(128)S(1)} %all-reduce, s32[4]{0:T(128)S(1)} %iota_add_fusion), kind=kOutput, calls=%fused_computation.4 | convolution fusion | flops 50332160 | bytes 4325904 | tf_op jit(solution)/shard_map/mn,nrd->mrd/dot_general | solution.py:96
  321.9 0.7 copy.36
  322.6 52.1 %all-gather.12.cloned.1.call-done = f32[128,512,16]{1,2,0:T(8,128)} async-done(((f32[8,512,16]{1,2,0:T(8,128)}), f32[128,512,16]{1,2,0:T(8,128)}) %all-gather.12.cloned.1.call-update) | async-done | bytes 4194320 | tf_op jit(solution)/shard_map/all_gather | solution.py:89
  374.7 5.8 %fusion.6 = f32[4,512,16]{1,0,2:T(4,128)S(1)} fusion(f32[128,512,16]{1,2,0:T(8,128)} %all-gather.12.cloned.1.call-done, s32[128]{0:T(128)S(1)} %all-reduce, s32[4]{0:T(128)S(1)} %iota_add_fusion), kind=kOutput, calls=%fused_computation.6 | convolution fusion | flops 50332160 | bytes 4325904 | tf_op jit(solution)/shard_map/mn,nhr->mhr/dot_general | solution.py:95
  380.5 0.7 copy.35
  (11 shorter events, 0.1 us)
Async XLA Ops:
  7.2 55.8 %copy-start = (bf16[1024,512]{1,0:T(8,128)(2,1)S(1)}, bf16[1024,512]{1,0:T(8,128)(2,1)}, u32[]{:S(2)}) copy-start(bf16[1024,512]{1,0:T(8,128)(2,1)} %param.9) | copy-start | bytes 3145732
  7.2 53.4 %all-gather.10.cloned.1.call-start = ((), (), s32[]{:S(2)}) async-start(), calls=%async_computation.2 | async-start | bytes 1114112 | tf_op jit(solution)/shard_map/all_gather | solution.py:48
  7.9 102.1 %all-gather.8.cloned.1.call-start = ((), (), s32[]{:S(2)}) async-start(), calls=%async_computation.1 | async-start | bytes 1114112 | tf_op jit(solution)/shard_map/all_gather | solution.py:49
  8.7 199.8 %all-gather.6.cloned.1.call-start = ((), (), s32[]{:S(2)}) async-start(), calls=%async_computation | async-start | bytes 17825792 | tf_op jit(solution)/shard_map/all_gather | solution.py:22
  9.4 306.7 %all-gather.14.cloned.1.call-start = ((), (), s32[]{:S(2)}) async-start(), calls=%async_computation.4 | async-start | bytes 4456448 | tf_op jit(solution)/shard_map/all_gather | solution.py:90
  63.0 194.9 %copy-start.1 = (u32[256]{0:T(256)S(1)}, u32[256]{0:T(256)}, u32[]{:S(2)}) copy-start(u32[256]{0:T(256)} %constant.31) | copy-start | bytes 3076
  256.9 117.8 %all-gather.12.cloned.1.call-start = ((), (), s32[]{:S(2)}) async-start(), calls=%async_computation.3 | async-start | bytes 4456448 | tf_op jit(solution)/shard_map/all_gather | solution.py:89
Sparse Core Ops, SparseCore 0:
  10.4 50.0 all-gather.9
  63.0 47.0 all-gather.7
  111.9 96.5 all-gather.5
  257.0 59.0 all-gather.13
  318.4 56.2 all-gather.11
where the time goes:
time: 388 us
  waiting for transfers between devices  273 us (70%)
  blocking collectives  56.9 us (15%)
  matrix products  38.1 us (10%)
  between operations  14.5 us (4%)
    all_gather x1, waiting for transfers between devices, per_device(): gathered = lax.all_gather(output_cotangent, 'mp', axis=0, tiled=True)  96 us
    all_gather x1, waiting for transfers between devices, per_device(): lax.all_gather(down_factor_block, 'dp', axis=0, tiled=True)  52.1 us
    all_gather x1, waiting for transfers between devices, per_device(): lax.all_gather(adapter_down_weight, 'dp', axis=0, tiled=True)  48.6 us
    all_gather x1, waiting for transfers between devices, per_device(): lax.all_gather(adapter_up_weight, 'dp', axis=0, tiled=True)  46.7 us
    psum x1, blocking collectives, per_device(): low_sum, back_sum = lax.psum((low_part, back_part), 'mp')  44.4 us
    all_gather x1, waiting for transfers between devices, per_device(): lax.all_gather(up_factor_block, 'dp', axis=0, tiled=True)  27.7 us
    dot_general x1, matrix products, per_device(): lax.dot_general(masked_rows.reshape(row_block_values, width), output_weig...  16 us
    unnamed x1, blocking collectives  12.5 us
  transfers between devices with their start and end apart: 5, of which 5 were waited for; matrix products, arithmetic and copies ran while one was open for 8% of the time, Pallas kernels for 0%

commit v1 on v0

v1 whole, which is shorter than its diff:
```python
import jax
import jax.numpy as jnp
from jax import lax
from jax.experimental import pallas as pl
from jax.experimental.pallas import tpu as pltpu
from jax.sharding import PartitionSpec as P

BLOCK = 128
SIDE = 4
CORES = 2
STEP_K = 1024


adapter_scale = 2.0


def ring_step(shift, ring):
    return [
        (z * CORES + c, ((z + shift) % ring) * CORES + c)
        for z in range(ring)
        for c in range(CORES)
    ]


def x_step(shift):
    return [
        (y * SIDE + x, y * SIDE + (x + shift) % SIDE) for y in range(SIDE) for x in range(SIDE)
    ]


def y_step(shift):
    return [
        (y * SIDE + x, ((y + shift) % SIDE) * SIDE + x) for y in range(SIDE) for x in range(SIDE)
    ]


def frozen_kernel(n, place_ref, *refs):
    shards, weight = refs[:n], refs[n]
    out, total, sems = refs[-3:]
    rows = shards[0].shape[0]
    step = pl.program_id(0)
    left = jnp.concatenate([s[...] for s in shards], axis=0)
    part = lax.dot_general(
        left, weight[...], (((1,), (1,)), ((), ())), preferred_element_type=jnp.float32
    )

    @pl.when(step == 0)
    def _():
        total[...] = part

    @pl.when(step > 0)
    def _():
        total[...] += part

    @pl.when(step == pl.num_programs(0) - 1)
    def _():
        copies = [
            pltpu.make_async_copy(
                total.at[pl.ds(i * rows, rows)],
                out.at[pl.ds(pl.multiple_of(place_ref[i] * rows, rows), rows)],
                sems.at[i],
            )
            for i in range(n)
        ]
        for copy in copies:
            copy.start()
        for copy in copies:
            copy.wait()


def frozen_rows(places, shards, weight, all_rows, held=()):
    n = len(shards)
    rows, width = shards[0].shape
    features = weight.shape[0]
    grid_spec = pltpu.PrefetchScalarGridSpec(
        num_scalar_prefetch=1,
        grid=(width // STEP_K,),
        in_specs=[pl.BlockSpec((rows, STEP_K), lambda k, p: (0, k))] * n
        + [
            pl.BlockSpec((features, STEP_K), lambda k, p: (0, k)),
        ]
        + [pl.BlockSpec(memory_space=pl.ANY)] * len(held),
        out_specs=pl.BlockSpec(memory_space=pl.ANY),
        scratch_shapes=[
            pltpu.VMEM((n * rows, features), jnp.float32),
            pltpu.SemaphoreType.DMA((n,)),
        ],
    )
    return pl.pallas_call(
        lambda *refs: frozen_kernel(n, *refs),
        out_shape=jax.ShapeDtypeStruct((all_rows, features), jnp.float32),
        grid_spec=grid_spec,
        input_output_aliases={n + 2: 0} if held else {},
        compiler_params=pltpu.CompilerParams(vmem_limit_bytes=24 * 1024 * 1024),
        cost_estimate=pl.CostEstimate(
            flops=2 * n * rows * width * features,
            bytes_accessed=2 * width * (features + n * rows),
            transcendentals=0,
        ),
    )(jnp.stack(places).astype(jnp.int32), *shards, weight, *held)


def per_device(
    output_cotangent,
    acts,
    output_weight,
    adapter_down_weight,
    adapter_up_weight,
    counts,
    block_tenant_map,
    owner,
):
    f32, bf16 = jnp.float32, jnp.bfloat16
    shard_rows, width = output_cotangent.shape
    features = acts.shape[1]
    held_slots, rank, columns = adapter_up_weight.shape
    nblk_loc = acts.shape[0] // BLOCK
    mp = width // columns
    ring = mp // CORES
    slot_count = owner.shape[0]
    nblocks = block_tenant_map.shape[0]
    group = lax.axis_index("dp")
    member = lax.axis_index("mp")
    z, core = member // CORES, member % CORES
    y, x = group // SIDE, group % SIDE

    def up_ring(v):
        return lax.ppermute(v, "mp", ring_step(1, ring))

    def down_ring(v):
        return lax.ppermute(v, "mp", ring_step(-1, ring))

    def swap(v):
        return lax.ppermute(v, "mp", [(i, i ^ 1) for i in range(mp)])

    own = output_cotangent
    half = shard_rows // 2
    u1, d1 = up_ring(own), down_ring(own)
    u2, d2 = up_ring(u1), down_ring(d1)
    u3, d3 = up_ring(u2), down_ring(d2)
    u4, d4 = up_ring(u3[:half]), down_ring(d3[half:])
    s4 = jnp.concatenate([u4, d4], axis=0)

    tenant_ids = jnp.arange(slot_count, dtype=jnp.int32)
    global_ids = jnp.arange(nblocks, dtype=jnp.int32)
    slot_blk = jnp.sum(
        jnp.where(block_tenant_map[:, None] == tenant_ids[None, :], owner[None, :], 0), axis=1
    )
    first_block = group * nblk_loc
    local_map = lax.dynamic_slice_in_dim(block_tenant_map, first_block, nblk_loc)
    local_ids = first_block + jnp.arange(nblk_loc, dtype=jnp.int32)
    same = (local_map[:, None] == block_tenant_map[None, :]) & (
        global_ids[None, :] < local_ids[:, None]
    )
    before = jnp.sum(same.astype(jnp.int32), axis=1)
    hit = local_map[:, None] == tenant_ids[None, :]
    limit = jnp.sum(jnp.where(hit, counts[None, :], 0), axis=1)
    real = limit - before * BLOCK
    within = jnp.arange(BLOCK, dtype=jnp.int32)
    valid = within[None, :] < real[:, None]
    own_real = lax.dynamic_slice_in_dim(real, z, 1) - core * shard_rows
    own_valid = jnp.arange(shard_rows, dtype=jnp.int32) < own_real
    own_masked = jnp.where(own_valid[:, None], own, jnp.zeros_like(own))

    shifts = (0, 1, -1, 2)

    def x_gather(v):
        return [v] + [lax.ppermute(v, "dp", x_step(s)) for s in shifts[1:]]

    def y_exchange(vs):
        return [vs[0]] + [lax.ppermute(v, "dp", y_step(s)) for s, v in zip(shifts[1:], vs[1:])]

    x_sources = [y * SIDE + (x - s) % SIDE for s in shifts]
    y_targets = [((y + s) % SIDE) * SIDE + x for s in shifts]

    def slots_of(g):
        return g * held_slots + jnp.arange(held_slots, dtype=jnp.int32)

    def blocks_of(g):
        return lax.dynamic_slice_in_dim(slot_blk, g * nblk_loc, nblk_loc)

    mine = jnp.concatenate([jnp.swapaxes(adapter_down_weight, 1, 2), adapter_up_weight], axis=2)
    near = jnp.concatenate(x_gather(mine), axis=0)
    near_slots = jnp.concatenate([slots_of(g) for g in x_sources])
    picked = [
        jnp.einsum(
            "ns,srd->nrd",
            (blocks_of(g)[:, None] == near_slots[None, :]).astype(bf16),
            near,
            preferred_element_type=f32,
        ).astype(bf16)
        for g in y_targets
    ]
    got = y_exchange(picked)
    factors = got[0] + got[1] + got[2] + got[3]
    down_factor, up_factor = factors[:, :, :features], factors[:, :, features:]

    activation_block = acts.reshape(nblk_loc, BLOCK, features)
    low_part = jnp.einsum(
        "nbh,nrh->nrb", activation_block, down_factor, preferred_element_type=f32
    )
    low_high = lax.reduce_precision(low_part, 8, 7)
    low_rest = low_part - low_high
    to_rows = jnp.concatenate([up_factor, low_high.astype(bf16), low_rest.astype(bf16)], axis=2)
    to_rows = jnp.broadcast_to(to_rows[:, None], (ring, CORES) + to_rows.shape[1:])
    to_rows = to_rows.reshape((mp,) + to_rows.shape[2:])
    at_rows = lax.all_to_all(to_rows, "mp", 0, 0, tiled=True)
    low_sum = jnp.sum(
        at_rows[:, :, columns : columns + BLOCK].astype(f32)
        + at_rows[:, :, columns + BLOCK :].astype(f32),
        axis=0,
    ).astype(bf16)
    low_own = lax.dynamic_slice_in_dim(low_sum, core * shard_rows, shard_rows, 1)
    up_whole = jnp.swapaxes(at_rows[:, :, :columns], 0, 1).reshape(rank, width)
    back_own = lax.dot_general(
        up_whole, own_masked, (((1,), (1,)), ((), ())), preferred_element_type=f32
    ).astype(bf16)
    up_rows = (
        adapter_scale
        * lax.dot_general(
            low_own, own_masked, (((1,), (0,)), ((), ())), preferred_element_type=f32
        )
    ).astype(bf16)
    to_columns = jnp.swapaxes(up_rows.reshape(rank, mp, columns), 0, 1)
    back_pad = jnp.pad(back_own, ((0, 0), (0, BLOCK - shard_rows)))
    to_columns = jnp.concatenate(
        [to_columns, jnp.broadcast_to(back_pad[None], (mp, rank, BLOCK))], axis=2
    )
    at_columns = lax.all_to_all(to_columns, "mp", 0, 0, tiled=True)
    up_block = jnp.sum(
        at_columns[:, :, :columns].astype(f32).reshape(ring, CORES, rank, columns), axis=1
    )
    back = at_columns[:, :, columns : columns + shard_rows].reshape(ring, CORES, rank, shard_rows)
    back = jnp.swapaxes(back, 1, 2).reshape(nblk_loc, rank, BLOCK)
    down_block = adapter_scale * jnp.einsum(
        "nrb,nbh->nrh", back, activation_block, preferred_element_type=f32
    )

    grads = jnp.concatenate([down_block, up_block], axis=2).astype(bf16)
    near_grads = jnp.concatenate(x_gather(grads), axis=0)
    near_blocks = jnp.concatenate([blocks_of(g) for g in x_sources])
    summed = [
        jnp.einsum(
            "sn,nrd->srd",
            (slots_of(g)[:, None] == near_blocks[None, :]).astype(bf16),
            near_grads,
            preferred_element_type=f32,
        )
        for g in y_targets
    ]
    arrived = y_exchange([summed[0]] + [s.astype(bf16) for s in summed[1:]])
    total = arrived[0] + (
        arrived[1].astype(f32) + arrived[2].astype(f32) + arrived[3].astype(f32)
    )
    grad_down = jnp.swapaxes(total[:, :, :features], 1, 2)
    grad_up = total[:, :, features:]

    def places(*shifts):
        found = []
        for s in shifts:
            chip = (z + s) % ring
            found += [chip * CORES + core, chip * CORES + 1 - core]
        return found

    steps = [
        (places(0, -1, 1), [own, swap(own), u1, swap(u1), d1, swap(d1)]),
        (places(-2, 2), [u2, swap(u2), d2, swap(d2)]),
        (places(-3, 3), [u3, swap(u3), d3, swap(d3)]),
        (places(4), [s4, swap(s4)]),
    ]
    held = ()
    for where, shards in steps:
        held = (frozen_rows(where, shards, output_weight, nblk_loc * BLOCK, held),)
    frozen = held[0]
    adapter_extra = jnp.einsum(
        "nrb,nrh->nbh", back, down_factor, preferred_element_type=f32
    )
    input_gradient = jnp.where(
        valid[:, :, None],
        frozen.reshape(nblk_loc, BLOCK, features) + adapter_scale * adapter_extra,
        0.0,
    ).astype(bf16)
    return (input_gradient.reshape(nblk_loc * BLOCK, features), grad_down, grad_up)


def solution(mesh):
    in_specs = (
        P(("dp", "mp"), None),
        P("dp", "mp"),
        P("mp", None),
        P("dp", "mp", None),
        P("dp", None, "mp"),
        P(),
        P(),
        P(),
    )
    out_specs = (P("dp", "mp"), P("dp", "mp", None), P("dp", None, "mp"))
    return jax.shard_map(
        per_device, mesh=mesh, in_specs=in_specs, out_specs=out_specs, check_vma=False
    )
```

time: 388 us -> 187 us (0.48)
  waiting for transfers between devices: 273 us -> 62.1 us
  blocking collectives: 56.9 us -> 0 us
  starting transfers between devices: 0.19 us -> 55.6 us
  Pallas kernels: 0 us -> 29.2 us
  matrix products: 38.1 us -> 13.4 us
  between operations: 14.5 us -> 1.89 us
  local copies, waits for them, and re-layouts: 2.97 us -> 15.4 us
  other arithmetic: 1.81 us -> 8.04 us
    all_gather x5 -> x0, waiting for transfers between devices: 271 us -> none  [the longest x1 96 us: per_device(): gathered = lax.all_gather(output_cotangent, 'mp', axis=0, tiled=True)]
    psum x1 -> x0, blocking collectives: 44.4 us -> none  [per_device(): low_sum, back_sum = lax.psum((low_part, back_part), 'mp')]
    ppermute x0 -> x28, starting transfers between devices: none -> 39.1 us  [the longest x4 9 us: down_ring(): return lax.ppermute(v, 'mp', ring_step(-1, ring))]
    ppermute x0 -> x28, waiting for transfers between devices: none -> 34.9 us  [the longest x6 14.4 us: x_gather(): return [v] + [lax.ppermute(v, 'dp', x_step(s)) for s in shifts[1:]]]
    pallas_call x0 -> x4, Pallas kernels: none -> 29.2 us  [frozen_rows(): pl.pallas_call(lambda *refs: frozen_kernel(n, *refs), out_shape=jax.Shape...]
    all_to_all x0 -> x2, waiting for transfers between devices: none -> 27.2 us  [the longest x1 15.6 us: per_device(): at_columns = lax.all_to_all(to_columns, 'mp', 0, 0, tiled=True)]
    dot_general x10 -> x13, matrix products: 38.1 us -> 13.4 us  [the longest x4 5.1 us: per_device(): jnp.einsum('ns,srd->nrd', (blocks_of(g)[:, None] == near_slots[None, :])....]
    all_to_all x0 -> x2, starting transfers between devices: none -> 16.5 us  [the longest x1 10.3 us: per_device(): at_rows = lax.all_to_all(to_rows, 'mp', 0, 0, tiled=True)]
  transfers between devices with their start and end apart: 5 -> 30, of which waited for: 5 -> 10; matrix products, arithmetic and copies ran while one was open for 8% -> 13% of each run, Pallas kernels for 0% -> 13%
where the time goes in v1:
time: 187 us; the launch traced here: 186 us
  waiting for transfers between devices  62.1 us (33%)
  starting transfers between devices  55.6 us (30%)
  Pallas kernels  29.2 us (16%)
  local copies, waits for them, and re-layouts  15.4 us (8%)
  matrix products  13.4 us (7%)
  other arithmetic  8.04 us (4%)
  between operations  1.89 us (1%)
    pallas_call x4, Pallas kernels, frozen_rows(): pl.pallas_call(lambda *refs: frozen_kernel(n, *refs), out_shape=jax.Shape...  29.2 us
    all_to_all x1, waiting for transfers between devices, per_device(): at_columns = lax.all_to_all(to_columns, 'mp', 0, 0, tiled=True)  15.6 us
    ppermute x6, waiting for transfers between devices, x_gather(): return [v] + [lax.ppermute(v, 'dp', x_step(s)) for s in shifts[1:]]  14.4 us
    ppermute x4, waiting for transfers between devices, down_ring(): return lax.ppermute(v, 'mp', ring_step(-1, ring))  13.4 us
    all_to_all x1, waiting for transfers between devices, per_device(): at_rows = lax.all_to_all(to_rows, 'mp', 0, 0, tiled=True)  11.6 us
    unnamed x42, local copies, waits for them, and re-layouts  11.3 us
    all_to_all x1, starting transfers between devices, per_device(): at_rows = lax.all_to_all(to_rows, 'mp', 0, 0, tiled=True)  10.3 us
    ppermute x4, starting transfers between devices, down_ring(): return lax.ppermute(v, 'mp', ring_step(-1, ring))  9 us
  transfers between devices with their start and end apart: 30, of which 10 were waited for; matrix products, arithmetic and copies ran while one was open for 13% of the time, Pallas kernels for 13%

profile of v1, /device:TPU:1, one launch (start us, length us, event | category | flops | bytes accessed | tf_op | source)
XLA Modules:
  0.0 185.7 jit_solution(13524385805358349443)
XLA Ops:
  2.6 2.1 %collective-permute-start.16 = (bf16[4,16,1024]{2,0,1:T(4,128)(2,1)S(1)}, bf16[4,16,1024]{2,0,1:T(4,128)(2,1)S(1)}, u32[]{:S(2)}, u32[]{:S(2)}) collective-permute-start(bf16[4,16,1024]{2,0,1:T(4,128)(2,1)S(1)} %pad_maximum_fusion.5), channel_id=1, source_target_pairs={{0,16},{16,32},{32,48},{48,0},{64,80},{80,96},{96,112},{112,64},{1... | collective-permute-start | bytes 393224 | tf_op jit(solution)/shard_map/ppermute | solution.py:168
  6.1 1.6 collective-permute-start.18
  8.8 3.6 %collective-permute-done.18 = bf16[4,16,1024]{2,0,1:T(4,128)(2,1)S(1)} collective-permute-done((bf16[4,16,1024]{2,0,1:T(4,128)(2,1)S(1)}, bf16[4,16,1024]{2,0,1:T(4,128)(2,1)S(1)}, u32[]{:S(2)}, u32[]{:S(2)}) %collective-permute-start.18) | collective-permute-done | bytes 131104 | tf_op jit(solution)/shard_map/ppermute | solution.py:168
  13.5 2.0 %collective-permute-start.19 = (bf16[8,16,1024]{2,0,1:T(8,128)(2,1)}, bf16[8,16,1024]{2,0,1:T(8,128)(2,1)}, u32[]{:S(2)}, u32[]{:S(2)}) collective-permute-start(bf16[8,16,1024]{2,0,1:T(8,128)(2,1)} %convolution_convert_fusion.2), channel_id=1, source_target_pairs={{0,64},{16,80},{32,96},{48,112},{64,128},{80,144},{96,160},{112,17... | collective-permute-start | bytes 786440 | tf_op jit(solution)/shard_map/ppermute | solution.py:171
  19.3 1.6 collective-permute-start.21
  20.9 1.6 collective-permute-start
  22.5 3.9 %collective-permute-start.4 = (bf16[64,8192]{1,0:T(8,128)(2,1)S(1)}, bf16[64,8192]{1,0:T(8,128)(2,1)}, u32[]{:S(2)}, u32[]{:S(2)}) collective-permute-start(bf16[64,8192]{1,0:T(8,128)(2,1)S(1)} %copy-done.3), channel_id=1, source_target_pairs={{0,14},{1,15},{2,0},{3,1},{4,2},{5,3},{6,4},{7,5},{8,6},{9,7},{10,... | collective-permute-start | bytes 3145736 | tf_op jit(solution)/shard_map/ppermute | solution.py:131
  27.1 2.5 %collective-permute-start.13 = (bf16[64,8192]{1,0:T(8,128)(2,1)S(1)}, bf16[64,8192]{1,0:T(8,128)(2,1)}, u32[]{:S(2)}, u32[]{:S(2)}) collective-permute-start(bf16[64,8192]{1,0:T(8,128)(2,1)S(1)} %copy-done.3), channel_id=1, source_target_pairs={{0,1},{1,0},{2,3},{3,2},{4,5},{5,4},{6,7},{7,6},{8,9},{9,8},{10,11... | collective-permute-start | bytes 3145736 | tf_op jit(solution)/shard_map/ppermute | solution.py:134
  29.5 1.7 fusion.3
  33.2 10.3 %all-to-all-start = ((bf16[16,16,768]{2,1,0:T(8,128)(2,1)}), bf16[16,16,768]{2,1,0:T(8,128)(2,1)S(1)}, u32[]{:S(2)}, u32[]{:S(2)}) async-start(bf16[16,16,768]{2,1,0:T(8,128)(2,1)} %bitcast.76), calls=%async_computation | async-start | bytes 786432 | tf_op jit(solution)/shard_map/all_to_all | solution.py:207
  49.5 11.6 %all-to-all-done = bf16[16,16,768]{2,1,0:T(8,128)(2,1)S(1)} async-done(((bf16[16,16,768]{2,1,0:T(8,128)(2,1)}), bf16[16,16,768]{2,1,0:T(8,128)(2,1)S(1)}, u32[]{:S(2)}, u32[]{:S(2)}) %all-to-all-start) | async-done | bytes 393248 | tf_op jit(solution)/shard_map/all_to_all | solution.py:207
  63.5 6.2 %all-to-all-start.1 = ((bf16[16,16,640]{2,1,0:T(8,128)(2,1)}), bf16[16,16,640]{2,1,0:T(8,128)(2,1)S(1)}, u32[]{:S(2)}, u32[]{:S(2)}) async-start(bf16[16,16,640]{2,1,0:T(8,128)(2,1)} %pad_maximum_fusion.2), calls=%async_computation.1 | async-start | bytes 655360 | tf_op jit(solution)/shard_map/all_to_all | solution.py:229
  69.9 2.6 %collective-permute-start.5 = (bf16[64,8192]{1,0:T(8,128)(2,1)}, bf16[64,8192]{1,0:T(8,128)(2,1)}, u32[]{:S(2)}, u32[]{:S(2)}) collective-permute-start(bf16[64,8192]{1,0:T(8,128)(2,1)} %collective-permute-done.4.refs_5_), channel_id=1, source_target_pairs={{0,14},{1,15},{2,0},{3,1},{4,2},{5,3},{6,4},{7,5},{8,6},{9,7},{10,... | collective-permute-start | bytes 3145736 | tf_op jit(solution)/shard_map/ppermute | solution.py:131
  72.7 15.6 %all-to-all-done.1 = bf16[16,16,640]{2,1,0:T(8,128)(2,1)S(1)} async-done(((bf16[16,16,640]{2,1,0:T(8,128)(2,1)}), bf16[16,16,640]{2,1,0:T(8,128)(2,1)S(1)}, u32[]{:S(2)}, u32[]{:S(2)}) %all-to-all-start.1) | async-done | bytes 327712 | tf_op jit(solution)/shard_map/all_to_all | solution.py:229
  90.0 1.7 collective-permute-start.2
  93.0 2.7 %collective-permute-start.23 = (bf16[8,16,1024]{2,1,0:T(8,128)(2,1)}, bf16[8,16,1024]{2,1,0:T(8,128)(2,1)S(1)}, u32[]{:S(2)}, u32[]{:S(2)}) collective-permute-start(bf16[8,16,1024]{2,1,0:T(8,128)(2,1)} %pad_maximum_fusion.3), channel_id=1, source_target_pairs={{0,48},{16,0},{32,16},{48,32},{64,112},{80,64},{96,80},{112,96},{1... | collective-permute-start | bytes 786440 | tf_op jit(solution)/shard_map/ppermute | solution.py:168
  95.6 5.7 %collective-permute-done.22 = bf16[8,16,1024]{2,1,0:T(8,128)(2,1)} collective-permute-done((bf16[8,16,1024]{2,1,0:T(8,128)(2,1)}, bf16[8,16,1024]{2,1,0:T(8,128)(2,1)}, u32[]{:S(2)}, u32[]{:S(2)}) %collective-permute-start.22) | collective-permute-done | bytes 262176 | tf_op jit(solution)/shard_map/ppermute | solution.py:168
  101.7 1.9 %collective-permute-start.6 = (bf16[64,8192]{1,0:T(8,128)(2,1)}, bf16[64,8192]{1,0:T(8,128)(2,1)S(1)}, u32[]{:S(2)}, u32[]{:S(2)}) collective-permute-start(bf16[64,8192]{1,0:T(8,128)(2,1)} %collective-permute-done.5.refs_3_), channel_id=1, source_target_pairs={{0,14},{1,15},{2,0},{3,1},{4,2},{5,3},{6,4},{7,5},{8,6},{9,7},{10,... | collective-permute-start | bytes 3145736 | tf_op jit(solution)/shard_map/ppermute | solution.py:131
  106.0 5.0 %collective-permute-done.24 = bf16[8,16,1024]{2,1,0:T(8,128)(2,1)S(1)} collective-permute-done((bf16[8,16,1024]{2,1,0:T(8,128)(2,1)}, bf16[8,16,1024]{2,1,0:T(8,128)(2,1)S(1)}, u32[]{:S(2)}, u32[]{:S(2)}) %collective-permute-start.24) | collective-permute-done | bytes 262176 | tf_op jit(solution)/shard_map/ppermute | solution.py:168
  112.5 4.3 %collective-permute-done.2.refs_1_ = bf16[64,8192]{1,0:T(8,128)(2,1)S(1)} collective-permute-done((bf16[64,8192]{1,0:T(8,128)(2,1)}, bf16[64,8192]{1,0:T(8,128)(2,1)S(1)}, u32[]{:S(2)}, u32[]{:S(2)}) %collective-permute-start.2) | collective-permute-done | bytes 1048608 | tf_op jit(solution)/shard_map/ppermute | solution.py:128
  120.6 5.1 %collective-permute-done.6.refs_3_ = bf16[64,8192]{1,0:T(8,128)(2,1)S(1)} collective-permute-done((bf16[64,8192]{1,0:T(8,128)(2,1)}, bf16[64,8192]{1,0:T(8,128)(2,1)S(1)}, u32[]{:S(2)}, u32[]{:S(2)}) %collective-permute-start.6) | collective-permute-done | bytes 1048608 | tf_op jit(solution)/shard_map/ppermute | solution.py:131
  126.8 1.7 collective-permute-start.26
  128.5 2.7 %collective-permute-done.3 = bf16[32,8192]{1,0:T(8,128)(2,1)S(1)} collective-permute-done((bf16[32,8192]{1,0:T(8,128)(2,1)S(1)}, bf16[32,8192]{1,0:T(8,128)(2,1)S(1)}, u32[]{:S(2)}, u32[]{:S(2)}) %collective-permute-start.3) | collective-permute-done | bytes 524320 | tf_op jit(solution)/shard_map/ppermute | solution.py:128
  132.9 2.0 %collective-permute-start.11 = (bf16[64,8192]{1,0:T(8,128)(2,1)}, bf16[64,8192]{1,0:T(8,128)(2,1)S(1)}, u32[]{:S(2)}, u32[]{:S(2)}) collective-permute-start(bf16[64,8192]{1,0:T(8,128)(2,1)} %collective-permute-done.1.refs_1_), channel_id=1, source_target_pairs={{0,1},{1,0},{2,3},{3,2},{4,5},{5,4},{6,7},{7,6},{8,9},{9,8},{10,11... | collective-permute-start | bytes 3145736 | tf_op jit(solution)/shard_map/ppermute | solution.py:134
  135.5 8.0 %collective-permute-done.7 = bf16[32,8192]{1,0:T(8,128)(2,1)S(1)} collective-permute-done((bf16[32,8192]{1,0:T(8,128)(2,1)S(1)}, bf16[32,8192]{1,0:T(8,128)(2,1)S(1)}, u32[]{:S(2)}, u32[]{:S(2)}) %collective-permute-start.7) | collective-permute-done | bytes 524320 | tf_op jit(solution)/shard_map/ppermute | solution.py:131
  143.4 2.2 %collective-permute-start.9 = (bf16[64,8192]{1,0:T(8,128)(2,1)S(1)}, bf16[64,8192]{1,0:T(8,128)(2,1)S(1)}, u32[]{:S(2)}, u32[]{:S(2)}) collective-permute-start(bf16[64,8192]{1,0:T(8,128)(2,1)S(1)} %collective-permute-done.2.refs_1_), channel_id=1, source_target_pairs={{0,1},{1,0},{2,3},{3,2},{4,5},{5,4},{6,7},{7,6},{8,9},{9,8},{10,11... | collective-permute-start | bytes 3145736 | tf_op jit(solution)/shard_map/ppermute | solution.py:134
  145.8 3.4 %copy-done.1 = bf16[512,8192]{1,0:T(8,128)(2,1)S(1)} copy-done((bf16[512,8192]{1,0:T(8,128)(2,1)S(1)}, bf16[512,8192]{1,0:T(8,128)(2,1)}, u32[]{:S(2)}) %copy-start.1) | copy-done | bytes 8388632
  149.1 9.2 %shard_map.103.refs_6_ = f32[1024,512]{1,0:T(8,128)S(1)} custom-call(s32[6]{0:T(128)S(1)} %stack.79.refs_0_, bf16[64,8192]{1,0:T(8,128)(2,1)S(1)} %copy-done.3, bf16[64,8192]{1,0:T(8,128)(2,1)} %collective-permute-done.13.refs_2_, bf16[64,8192]{1,0:T(8,128)(2,1)S(1)} %copy-done.5, bf16[64,8192]{1,0:T(8,128)(2,1)S(1)} %collective-permute-done.14.refs_4_, ...), custom_call_target="tpu_custom_call" | custom-call | flops 3221225472 | bytes 14680064 | tf_op jit(solution)/shard_map/pallas_call | solution.py:89
  161.0 3.4 %copy-done.2 = bf16[512,8192]{1,0:T(8,128)(2,1)S(1)} copy-done((bf16[512,8192]{1,0:T(8,128)(2,1)S(1)}, bf16[512,8192]{1,0:T(8,128)(2,1)}, u32[]{:S(2)}) %copy-start.2) | copy-done | bytes 8388632
  164.3 7.9 %shard_map.104.refs_6_ = f32[1024,512]{1,0:T(8,128)S(1)} custom-call(s32[4]{0:T(128)S(1)} %pad_add_fusion.2.refs_0_, bf16[64,8192]{1,0:T(8,128)(2,1)} %collective-permute-done.1.refs_1_, bf16[64,8192]{1,0:T(8,128)(2,1)S(1)} %collective-permute-done.11.refs_2_, bf16[64,8192]{1,0:T(8,128)(2,1)} %collective-permute-done.5.refs_3_, ...), custom_call_target="tpu_custom_call", output_to_operand_aliasing={{}: (6, {})} | custom-call | flops 2147483648 | bytes 12582912 | tf_op jit(solution)/shard_map/pallas_call | solution.py:89
  172.3 6.4 %shard_map.105.refs_4_ = f32[1024,512]{1,0:T(8,128)S(1)} custom-call(s32[4]{0:T(128)S(1)} %pad_add_fusion.1.refs_0_, bf16[64,8192]{1,0:T(8,128)(2,1)S(1)} %collective-permute-done.2.refs_1_, bf16[64,8192]{1,0:T(8,128)(2,1)S(1)} %collective-permute-done.9.refs_2_, ...), custom_call_target="tpu_custom_call", output_to_operand_aliasing={{}: (6, {})} | custom-call | flops 2147483648 | bytes 12582912 | tf_op jit(solution)/shard_map/pallas_call | solution.py:89
  178.7 5.8 %shard_map.106 = f32[1024,512]{1,0:T(8,128)S(1)} custom-call(s32[2]{0:T(128)S(1)} %pad_add_fusion.refs_0_, bf16[64,8192]{1,0:T(8,128)(2,1)S(1)} %constant_dynamic-update-slice_fusion.refs_1_, bf16[64,8192]{1,0:T(8,128)(2,1)S(1)} %collective-permute-done.8.refs_2_, bf16[512,8192]{1,0:T(8,128)(2,1)S(1)} %copy-done.2, ...), custom_call_target="tpu_custom_call", output_to_operand_aliasing={{}: (4, {})} | custom-call | flops 1073741824 | bytes 10485760 | tf_op jit(solution)/shard_map/pallas_call | solution.py:89
  (132 shorter events, 37.9 us)
Async XLA Ops:
  0.6 30.6 %copy-start = (bf16[1024,512]{1,0:T(8,128)(2,1)S(1)}, bf16[1024,512]{1,0:T(8,128)(2,1)}, u32[]{:S(2)}) copy-start(bf16[1024,512]{1,0:T(8,128)(2,1)} %param.9) | copy-start | bytes 3145732
  2.6 6.2 %collective-permute-start.16 = (bf16[4,16,1024]{2,0,1:T(4,128)(2,1)S(1)}, bf16[4,16,1024]{2,0,1:T(4,128)(2,1)S(1)}, u32[]{:S(2)}, u32[]{:S(2)}) collective-permute-start(bf16[4,16,1024]{2,0,1:T(4,128)(2,1)S(1)} %pad_maximum_fusion.5), channel_id=1, source_target_pairs={{0,16},{16,32},{32,48},{48,0},{64,80},{80,96},{96,112},{112,64},{1... | collective-permute-start | bytes 393224 | tf_op jit(solution)/shard_map/ppermute | solution.py:168
  4.7 4.0 %collective-permute-start.17 = (bf16[4,16,1024]{2,0,1:T(4,128)(2,1)S(1)}, bf16[4,16,1024]{2,0,1:T(4,128)(2,1)S(1)}, u32[]{:S(2)}, u32[]{:S(2)}) collective-permute-start(bf16[4,16,1024]{2,0,1:T(4,128)(2,1)S(1)} %pad_maximum_fusion.5), channel_id=1, source_target_pairs={{0,48},{16,0},{32,16},{48,32},{64,112},{80,64},{96,80},{112,96},{1... | collective-permute-start | bytes 393224 | tf_op jit(solution)/shard_map/ppermute | solution.py:168
  6.1 6.3 %collective-permute-start.18 = (bf16[4,16,1024]{2,0,1:T(4,128)(2,1)S(1)}, bf16[4,16,1024]{2,0,1:T(4,128)(2,1)S(1)}, u32[]{:S(2)}, u32[]{:S(2)}) collective-permute-start(bf16[4,16,1024]{2,0,1:T(4,128)(2,1)S(1)} %pad_maximum_fusion.5), channel_id=1, source_target_pairs={{0,32},{16,48},{32,0},{48,16},{64,96},{80,112},{96,64},{112,80},{1... | collective-permute-start | bytes 393224 | tf_op jit(solution)/shard_map/ppermute | solution.py:168
  13.5 13.6 %collective-permute-start.19 = (bf16[8,16,1024]{2,0,1:T(8,128)(2,1)}, bf16[8,16,1024]{2,0,1:T(8,128)(2,1)}, u32[]{:S(2)}, u32[]{:S(2)}) collective-permute-start(bf16[8,16,1024]{2,0,1:T(8,128)(2,1)} %convolution_convert_fusion.2), channel_id=1, source_target_pairs={{0,64},{16,80},{32,96},{48,112},{64,128},{80,144},{96,160},{112,17... | collective-permute-start | bytes 786440 | tf_op jit(solution)/shard_map/ppermute | solution.py:171
  16.7 12.9 %collective-permute-start.20 = (bf16[8,16,1024]{2,0,1:T(8,128)(2,1)}, bf16[8,16,1024]{2,0,1:T(8,128)(2,1)}, u32[]{:S(2)}, u32[]{:S(2)}) collective-permute-start(bf16[8,16,1024]{2,0,1:T(8,128)(2,1)} %convolution_convert_fusion.1), channel_id=1, source_target_pairs={{0,192},{16,208},{32,224},{48,240},{64,0},{80,16},{96,32},{112,48}... | collective-permute-start | bytes 786440 | tf_op jit(solution)/shard_map/ppermute | solution.py:171
  19.3 10.3 %collective-permute-start.21 = (bf16[8,16,1024]{2,0,1:T(8,128)(2,1)}, bf16[8,16,1024]{2,0,1:T(8,128)(2,1)}, u32[]{:S(2)}, u32[]{:S(2)}) collective-permute-start(bf16[8,16,1024]{2,0,1:T(8,128)(2,1)} %convolution_convert_fusion), channel_id=1, source_target_pairs={{0,128},{16,144},{32,160},{48,176},{64,192},{80,208},{96,224},{112... | collective-permute-start | bytes 786440 | tf_op jit(solution)/shard_map/ppermute | solution.py:171
  20.9 27.2 %collective-permute-start = (bf16[64,8192]{1,0:T(8,128)(2,1)S(1)}, bf16[64,8192]{1,0:T(8,128)(2,1)S(1)}, u32[]{:S(2)}, u32[]{:S(2)}) collective-permute-start(bf16[64,8192]{1,0:T(8,128)(2,1)S(1)} %copy-done.3), channel_id=1, source_target_pairs={{0,2},{1,3},{2,4},{3,5},{4,6},{5,7},{6,8},{7,9},{8,10},{9,11},{10,... | collective-permute-start | bytes 3145736 | tf_op jit(solution)/shard_map/ppermute | solution.py:128
  22.5 47.4 %collective-permute-start.4 = (bf16[64,8192]{1,0:T(8,128)(2,1)S(1)}, bf16[64,8192]{1,0:T(8,128)(2,1)}, u32[]{:S(2)}, u32[]{:S(2)}) collective-permute-start(bf16[64,8192]{1,0:T(8,128)(2,1)S(1)} %copy-done.3), channel_id=1, source_target_pairs={{0,14},{1,15},{2,0},{3,1},{4,2},{5,3},{6,4},{7,5},{8,6},{9,7},{10,... | collective-permute-start | bytes 3145736 | tf_op jit(solution)/shard_map/ppermute | solution.py:131
  27.1 99.8 %collective-permute-start.13 = (bf16[64,8192]{1,0:T(8,128)(2,1)S(1)}, bf16[64,8192]{1,0:T(8,128)(2,1)}, u32[]{:S(2)}, u32[]{:S(2)}) collective-permute-start(bf16[64,8192]{1,0:T(8,128)(2,1)S(1)} %copy-done.3), channel_id=1, source_target_pairs={{0,1},{1,0},{2,3},{3,2},{4,5},{5,4},{6,7},{7,6},{8,9},{9,8},{10,11... | collective-permute-start | bytes 3145736 | tf_op jit(solution)/shard_map/ppermute | solution.py:134
  33.2 27.9 %all-to-all-start = ((bf16[16,16,768]{2,1,0:T(8,128)(2,1)}), bf16[16,16,768]{2,1,0:T(8,128)(2,1)S(1)}, u32[]{:S(2)}, u32[]{:S(2)}) async-start(bf16[16,16,768]{2,1,0:T(8,128)(2,1)} %bitcast.76), calls=%async_computation | async-start | bytes 786432 | tf_op jit(solution)/shard_map/all_to_all | solution.py:207
  48.1 41.9 %collective-permute-start.1 = (bf16[64,8192]{1,0:T(8,128)(2,1)S(1)}, bf16[64,8192]{1,0:T(8,128)(2,1)}, u32[]{:S(2)}, u32[]{:S(2)}) collective-permute-start(bf16[64,8192]{1,0:T(8,128)(2,1)S(1)} %collective-permute-done.refs_3_), channel_id=1, source_target_pairs={{0,2},{1,3},{2,4},{3,5},{4,6},{5,7},{6,8},{7,9},{8,10},{9,11},{10,... | collective-permute-start | bytes 3145736 | tf_op jit(solution)/shard_map/ppermute | solution.py:128
  62.7 30.2 %copy-start.16 = (s32[8]{0:T(128)S(1)}, s32[8]{0:T(128)}, u32[]{:S(2)}) copy-start(s32[8]{0:T(128)} %copy-done.15) | copy-start | bytes 100
  63.5 24.8 %all-to-all-start.1 = ((bf16[16,16,640]{2,1,0:T(8,128)(2,1)}), bf16[16,16,640]{2,1,0:T(8,128)(2,1)S(1)}, u32[]{:S(2)}, u32[]{:S(2)}) async-start(bf16[16,16,640]{2,1,0:T(8,128)(2,1)} %pad_maximum_fusion.2), calls=%async_computation.1 | async-start | bytes 655360 | tf_op jit(solution)/shard_map/all_to_all | solution.py:229
  69.9 31.7 %collective-permute-start.5 = (bf16[64,8192]{1,0:T(8,128)(2,1)}, bf16[64,8192]{1,0:T(8,128)(2,1)}, u32[]{:S(2)}, u32[]{:S(2)}) collective-permute-start(bf16[64,8192]{1,0:T(8,128)(2,1)} %collective-permute-done.4.refs_5_), channel_id=1, source_target_pairs={{0,14},{1,15},{2,0},{3,1},{4,2},{5,3},{6,4},{7,5},{8,6},{9,7},{10,... | collective-permute-start | bytes 3145736 | tf_op jit(solution)/shard_map/ppermute | solution.py:131
  90.0 26.8 %collective-permute-start.2 = (bf16[64,8192]{1,0:T(8,128)(2,1)}, bf16[64,8192]{1,0:T(8,128)(2,1)S(1)}, u32[]{:S(2)}, u32[]{:S(2)}) collective-permute-start(bf16[64,8192]{1,0:T(8,128)(2,1)} %collective-permute-done.1.refs_1_), channel_id=1, source_target_pairs={{0,2},{1,3},{2,4},{3,5},{4,6},{5,7},{6,8},{7,9},{8,10},{9,11},{10,... | collective-permute-start | bytes 3145736 | tf_op jit(solution)/shard_map/ppermute | solution.py:128
  92.7 8.6 %collective-permute-start.22 = (bf16[8,16,1024]{2,1,0:T(8,128)(2,1)}, bf16[8,16,1024]{2,1,0:T(8,128)(2,1)}, u32[]{:S(2)}, u32[]{:S(2)}) collective-permute-start(bf16[8,16,1024]{2,1,0:T(8,128)(2,1)} %pad_maximum_fusion.3), channel_id=1, source_target_pairs={{0,16},{16,32},{32,48},{48,0},{64,80},{80,96},{96,112},{112,64},{1... | collective-permute-start | bytes 786440 | tf_op jit(solution)/shard_map/ppermute | solution.py:168
  93.0 12.0 %collective-permute-start.23 = (bf16[8,16,1024]{2,1,0:T(8,128)(2,1)}, bf16[8,16,1024]{2,1,0:T(8,128)(2,1)S(1)}, u32[]{:S(2)}, u32[]{:S(2)}) collective-permute-start(bf16[8,16,1024]{2,1,0:T(8,128)(2,1)} %pad_maximum_fusion.3), channel_id=1, source_target_pairs={{0,48},{16,0},{32,16},{48,32},{64,112},{80,64},{96,80},{112,96},{1... | collective-permute-start | bytes 786440 | tf_op jit(solution)/shard_map/ppermute | solution.py:168
  101.3 9.7 %collective-permute-start.24 = (bf16[8,16,1024]{2,1,0:T(8,128)(2,1)}, bf16[8,16,1024]{2,1,0:T(8,128)(2,1)S(1)}, u32[]{:S(2)}, u32[]{:S(2)}) collective-permute-start(bf16[8,16,1024]{2,1,0:T(8,128)(2,1)} %pad_maximum_fusion.3), channel_id=1, source_target_pairs={{0,32},{16,48},{32,0},{48,16},{64,96},{80,112},{96,64},{112,80},{1... | collective-permute-start | bytes 786440 | tf_op jit(solution)/shard_map/ppermute | solution.py:168
  101.7 24.0 %collective-permute-start.6 = (bf16[64,8192]{1,0:T(8,128)(2,1)}, bf16[64,8192]{1,0:T(8,128)(2,1)S(1)}, u32[]{:S(2)}, u32[]{:S(2)}) collective-permute-start(bf16[64,8192]{1,0:T(8,128)(2,1)} %collective-permute-done.5.refs_3_), channel_id=1, source_target_pairs={{0,14},{1,15},{2,0},{3,1},{4,2},{5,3},{6,4},{7,5},{8,6},{9,7},{10,... | collective-permute-start | bytes 3145736 | tf_op jit(solution)/shard_map/ppermute | solution.py:131
  105.0 26.9 %collective-permute-start.14 = (bf16[64,8192]{1,0:T(8,128)(2,1)S(1)}, bf16[64,8192]{1,0:T(8,128)(2,1)S(1)}, u32[]{:S(2)}, u32[]{:S(2)}) collective-permute-start(bf16[64,8192]{1,0:T(8,128)(2,1)S(1)} %copy-done.5), channel_id=1, source_target_pairs={{0,1},{1,0},{2,3},{3,2},{4,5},{5,4},{6,7},{7,6},{8,9},{9,8},{10,11... | collective-permute-start | bytes 3145736 | tf_op jit(solution)/shard_map/ppermute | solution.py:134
  111.0 21.9 %collective-permute-start.15 = (bf16[64,8192]{1,0:T(8,128)(2,1)}, bf16[64,8192]{1,0:T(8,128)(2,1)S(1)}, u32[]{:S(2)}, u32[]{:S(2)}) collective-permute-start(bf16[64,8192]{1,0:T(8,128)(2,1)} %collective-permute-done.4.refs_5_), channel_id=1, source_target_pairs={{0,1},{1,0},{2,3},{3,2},{4,5},{5,4},{6,7},{7,6},{8,9},{9,8},{10,11... | collective-permute-start | bytes 3145736 | tf_op jit(solution)/shard_map/ppermute | solution.py:134
  116.9 14.4 %collective-permute-start.3 = (bf16[32,8192]{1,0:T(8,128)(2,1)S(1)}, bf16[32,8192]{1,0:T(8,128)(2,1)S(1)}, u32[]{:S(2)}, u32[]{:S(2)}) collective-permute-start(bf16[32,8192]{1,0:T(8,128)(2,1)S(1)} %slice.44), channel_id=1, source_target_pairs={{0,2},{1,3},{2,4},{3,5},{4,6},{5,7},{6,8},{7,9},{8,10},{9,11},{10,... | collective-permute-start | bytes 1572872 | tf_op jit(solution)/shard_map/ppermute | solution.py:128
  125.7 9.3 %collective-permute-start.25 = (bf16[4,16,1024]{2,0,1:T(4,128)(2,1)S(1)}, bf16[4,16,1024]{2,0,1:T(4,128)(2,1)S(1)}, u32[]{:S(2)}, u32[]{:S(2)}) collective-permute-start(bf16[4,16,1024]{2,0,1:T(4,128)(2,1)S(1)} %convolution_convert_fusion.6), channel_id=1, source_target_pairs={{0,64},{16,80},{32,96},{48,112},{64,128},{80,144},{96,160},{112,17... | collective-permute-start | bytes 393224 | tf_op jit(solution)/shard_map/ppermute | solution.py:171
  126.8 8.2 %collective-permute-start.26 = (bf16[4,16,1024]{2,0,1:T(4,128)(2,1)S(1)}, bf16[4,16,1024]{2,0,1:T(4,128)(2,1)S(1)}, u32[]{:S(2)}, u32[]{:S(2)}) collective-permute-start(bf16[4,16,1024]{2,0,1:T(4,128)(2,1)S(1)} %convolution_convert_fusion.5), channel_id=1, source_target_pairs={{0,192},{16,208},{32,224},{48,240},{64,0},{80,16},{96,32},{112,48}... | collective-permute-start | bytes 393224 | tf_op jit(solution)/shard_map/ppermute | solution.py:171
  131.3 12.2 %collective-permute-start.7 = (bf16[32,8192]{1,0:T(8,128)(2,1)S(1)}, bf16[32,8192]{1,0:T(8,128)(2,1)S(1)}, u32[]{:S(2)}, u32[]{:S(2)}) collective-permute-start(bf16[32,8192]{1,0:T(8,128)(2,1)S(1)} %slice.45), channel_id=1, source_target_pairs={{0,14},{1,15},{2,0},{3,1},{4,2},{5,3},{6,4},{7,5},{8,6},{9,7},{10,... | collective-permute-start | bytes 1572872 | tf_op jit(solution)/shard_map/ppermute | solution.py:131
  131.9 13.8 %collective-permute-start.27 = (bf16[4,16,1024]{2,0,1:T(4,128)(2,1)S(1)}, bf16[4,16,1024]{2,0,1:T(4,128)(2,1)S(1)}, u32[]{:S(2)}, u32[]{:S(2)}) collective-permute-start(bf16[4,16,1024]{2,0,1:T(4,128)(2,1)S(1)} %convolution_convert_fusion.4), channel_id=1, source_target_pairs={{0,128},{16,144},{32,160},{48,176},{64,192},{80,208},{96,224},{112... | collective-permute-start | bytes 393224 | tf_op jit(solution)/shard_map/ppermute | solution.py:171
  132.9 28.0 %collective-permute-start.11 = (bf16[64,8192]{1,0:T(8,128)(2,1)}, bf16[64,8192]{1,0:T(8,128)(2,1)S(1)}, u32[]{:S(2)}, u32[]{:S(2)}) collective-permute-start(bf16[64,8192]{1,0:T(8,128)(2,1)} %collective-permute-done.1.refs_1_), channel_id=1, source_target_pairs={{0,1},{1,0},{2,3},{3,2},{4,5},{5,4},{6,7},{7,6},{8,9},{9,8},{10,11... | collective-permute-start | bytes 3145736 | tf_op jit(solution)/shard_map/ppermute | solution.py:134
  135.0 26.0 %collective-permute-start.12 = (bf16[64,8192]{1,0:T(8,128)(2,1)}, bf16[64,8192]{1,0:T(8,128)(2,1)S(1)}, u32[]{:S(2)}, u32[]{:S(2)}) collective-permute-start(bf16[64,8192]{1,0:T(8,128)(2,1)} %collective-permute-done.5.refs_3_), channel_id=1, source_target_pairs={{0,1},{1,0},{2,3},{3,2},{4,5},{5,4},{6,7},{7,6},{8,9},{9,8},{10,11... | collective-permute-start | bytes 3145736 | tf_op jit(solution)/shard_map/ppermute | solution.py:134
  135.1 37.2 %collective-permute-start.10 = (bf16[64,8192]{1,0:T(8,128)(2,1)S(1)}, bf16[64,8192]{1,0:T(8,128)(2,1)S(1)}, u32[]{:S(2)}, u32[]{:S(2)}) collective-permute-start(bf16[64,8192]{1,0:T(8,128)(2,1)S(1)} %collective-permute-done.6.refs_3_), channel_id=1, source_target_pairs={{0,1},{1,0},{2,3},{3,2},{4,5},{5,4},{6,7},{7,6},{8,9},{9,8},{10,11... | collective-permute-start | bytes 3145736 | tf_op jit(solution)/shard_map/ppermute | solution.py:134
  143.4 28.9 %collective-permute-start.9 = (bf16[64,8192]{1,0:T(8,128)(2,1)S(1)}, bf16[64,8192]{1,0:T(8,128)(2,1)S(1)}, u32[]{:S(2)}, u32[]{:S(2)}) collective-permute-start(bf16[64,8192]{1,0:T(8,128)(2,1)S(1)} %collective-permute-done.2.refs_1_), channel_id=1, source_target_pairs={{0,1},{1,0},{2,3},{3,2},{4,5},{5,4},{6,7},{7,6},{8,9},{9,8},{10,11... | collective-permute-start | bytes 3145736 | tf_op jit(solution)/shard_map/ppermute | solution.py:134
  145.6 33.0 %collective-permute-start.8 = (bf16[64,8192]{1,0:T(8,128)(2,1)S(1)}, bf16[64,8192]{1,0:T(8,128)(2,1)S(1)}, u32[]{:S(2)}, u32[]{:S(2)}) collective-permute-start(bf16[64,8192]{1,0:T(8,128)(2,1)S(1)} %constant_dynamic-update-slice_fusion.refs_1_), channel_id=1, source_target_pairs={{0,1},{1,0},{2,3},{3,2},{4,5},{5,4},{6,7},{7,6},{8,9},{9,8},{10,11... | collective-permute-start | bytes 3145736 | tf_op jit(solution)/shard_map/ppermute | solution.py:134
  (16 other events, 118.3 us)

commit v2 on v0

v2 whole, which is shorter than its diff:
```python
import jax
import jax.numpy as jnp
from jax import lax
from jax.experimental import pallas as pl
from jax.experimental.pallas import tpu as pltpu
from jax.sharding import PartitionSpec as P

BLOCK = 128
SIDE = 4
CORES = 2
SHIFTS = (0, 1, -1, 2)
STEP_K = 2048
VMEM_BYTES = 56 * 1024 * 1024


adapter_scale = 2.0


def ring_step(shift, ring):
    return [
        (z * CORES + c, ((z + (shift if c == 0 else -shift)) % ring) * CORES + c)
        for z in range(ring)
        for c in range(CORES)
    ]


def x_step(shift):
    return [
        (y * SIDE + x, y * SIDE + (x + shift) % SIDE) for y in range(SIDE) for x in range(SIDE)
    ]


def y_step(shift):
    return [
        (y * SIDE + x, ((y + shift) % SIDE) * SIDE + x) for y in range(SIDE) for x in range(SIDE)
    ]


def dot(a, b, dims):
    return lax.dot_general(a, b, (dims, ((), ())), preferred_element_type=jnp.float32)


def local_call(kernel, out_shapes, scalars, arrays, flops=0):
    size = sum(a.size * a.dtype.itemsize for a in arrays)
    size += sum(o.size * o.dtype.itemsize for o in out_shapes)
    return pl.pallas_call(
        kernel,
        out_shape=tuple(out_shapes),
        in_specs=[pl.BlockSpec(memory_space=pltpu.SMEM)] * len(scalars)
        + [pl.BlockSpec(memory_space=pltpu.VMEM)] * len(arrays),
        out_specs=tuple([pl.BlockSpec(memory_space=pltpu.VMEM)] * len(out_shapes)),
        compiler_params=pltpu.CompilerParams(vmem_limit_bytes=16 * 1024 * 1024),
        cost_estimate=pl.CostEstimate(flops=flops, bytes_accessed=size, transcendentals=0),
    )(*scalars, *arrays)


def split_kernel(at_ref, real_ref, own, mine, other):
    z, core = at_ref[2], at_ref[3]
    rows, columns = own.shape[0], own.shape[1] // 16
    limit = real_ref[z] - core * rows
    keep = lax.broadcasted_iota(jnp.int32, (rows, columns), 0) < limit
    for r in range(mine.shape[1] // columns):
        a = own[:, (2 * r) * columns : (2 * r + 1) * columns]
        b = own[:, (2 * r + 1) * columns : (2 * r + 2) * columns]
        a = jnp.where(keep, a, jnp.zeros_like(a))
        b = jnp.where(keep, b, jnp.zeros_like(b))
        here = pl.ds(r * columns, columns)
        mine[:, here] = jnp.where(core == 0, a, b)
        other[:, here] = jnp.where(core == 0, b, a)


def pick_kernel(at_ref, slot_ref, *refs):
    near, picked = refs[:SIDE], refs[SIDE:]
    x, y = at_ref[0], at_ref[1]
    per, held = picked[0].shape[0], near[0].shape[0]
    for shift, out in zip(SHIFTS, picked):
        group = lax.rem(y + shift + SIDE, SIDE) * SIDE + x
        for n in range(per):
            slot = slot_ref[group * per + n]
            owner = slot // held
            away = lax.rem(x - owner % SIDE + SIDE, SIDE)
            here = slot % held
            value = jnp.zeros(out.shape[1:], out.dtype)
            for source, block in zip(SHIFTS, near):
                value = jnp.where(away == source % SIDE, block[here], value)
            out[n] = jnp.where(owner // SIDE == y, value, jnp.zeros_like(value))


def low_kernel(*refs):
    got, (acts, down, to_rows) = refs[:SIDE], refs[SIDE:]
    features = acts.shape[1]
    columns = to_rows.shape[2] - 2 * BLOCK
    for n in range(down.shape[0]):
        mixed = sum(g[n].astype(jnp.float32) for g in got).astype(jnp.bfloat16)
        factor = mixed[:, :features]
        down[n] = factor
        low = dot(factor, acts[pl.ds(n * BLOCK, BLOCK), :], ((1,), (1,)))
        high = low.astype(jnp.bfloat16)
        to_rows[n, :, :columns] = mixed[:, features:]
        to_rows[n, :, columns : columns + BLOCK] = high
        to_rows[n, :, columns + BLOCK :] = (low - high.astype(jnp.float32)).astype(jnp.bfloat16)


def sums_kernel(at_ref, at_rows, mine, other, sums):
    core = at_ref[3]
    ring, rank, size = at_rows.shape
    columns = size - 2 * BLOCK
    low = jnp.zeros((rank, BLOCK), jnp.float32)
    back_mine = jnp.zeros((rank, mine.shape[0]), jnp.float32)
    back_other = jnp.zeros((rank, mine.shape[0]), jnp.float32)
    for r in range(ring):
        low += at_rows[r, :, columns : columns + BLOCK].astype(jnp.float32)
        low += at_rows[r, :, columns + BLOCK :].astype(jnp.float32)
        up = at_rows[r, :, :columns]
        here = pl.ds(r * columns, columns)
        back_mine += dot(up, mine[:, here], ((1,), (1,)))
        back_other += dot(up, other[:, here], ((1,), (1,)))
    first = jnp.where(core == 0, back_mine, back_other)
    second = jnp.where(core == 0, back_other, back_mine)
    sums[:rank] = low
    sums[rank:] = jnp.concatenate([first, second], axis=1)


def columns_kernel(at_ref, sums, more, mine, other, to_columns):
    core = at_ref[3]
    rank, rows = sums.shape[0] // 2, mine.shape[0]
    whole = (sums[...] + more[...]).astype(jnp.bfloat16)
    low, back = whole[:rank], whole[rank:]
    first, second = low[:, :rows], low[:, rows:]
    low_mine = jnp.where(core == 0, first, second)
    low_other = jnp.where(core == 0, second, first)
    columns = to_columns.shape[2] - BLOCK
    for r in range(to_columns.shape[0]):
        here = pl.ds(r * columns, columns)
        value = dot(low_mine, mine[:, here], ((1,), (0,)))
        value += dot(low_other, other[:, here], ((1,), (0,)))
        to_columns[r, :, :columns] = (adapter_scale * value).astype(jnp.bfloat16)
        to_columns[r, :, columns:] = back


def grads_kernel(at_columns, acts, grads):
    features = acts.shape[1]
    columns = at_columns.shape[2] - BLOCK
    count = at_columns.shape[0]
    for n in range(count):
        back = at_columns[n, :, columns:]
        value = adapter_scale * dot(back, acts[pl.ds(n * BLOCK, BLOCK), :], ((1,), (0,)))
        grads[n, :, :features] = value.astype(jnp.bfloat16)
        grads[n, :, features:] = at_columns[n, :, :columns]


def slots_kernel(at_ref, slot_ref, *refs):
    near, summed, total = refs[:SIDE], refs[SIDE:-1], refs[-1]
    x, y = at_ref[0], at_ref[1]
    per, held = near[0].shape[0], summed[0].shape[0]
    total[...] = jnp.zeros_like(total)
    for shift, block in zip(SHIFTS, near):
        group = y * SIDE + lax.rem(x - shift + SIDE, SIDE)
        for n in range(per):
            slot = slot_ref[group * per + n]
            owner = slot // held

            @pl.when(owner % SIDE == x)
            def _():
                here = (owner // SIDE) * held + slot % held
                total[here] = total[here] + block[n].astype(jnp.float32)

    for shift, out in zip(SHIFTS, summed):
        there = lax.rem(y + shift + SIDE, SIDE) * held
        out[...] = total[pl.ds(there, held)].astype(jnp.bfloat16)


def finish_kernel(*refs):
    arrived, (grad_down, grad_up) = refs[:SIDE], refs[SIDE:]
    features = grad_down.shape[2]
    for s in range(grad_down.shape[0]):
        value = sum(a[s].astype(jnp.float32) for a in arrived)
        grad_down[s] = value[:, :features]
        grad_up[s] = value[:, features:]


def early_kernel(n, *refs):
    shards, (weight, total) = refs[:n], refs[n:]
    step = pl.program_id(0)
    left = jnp.concatenate([s[...] for s in shards], axis=0)
    part = dot(left, weight[...], ((1,), (1,)))

    @pl.when(step == 0)
    def _():
        total[...] = part

    @pl.when(step > 0)
    def _():
        total[...] += part


def early_rows(shards, weight):
    n = len(shards)
    rows, width = shards[0].shape
    features = weight.shape[0]
    return pl.pallas_call(
        lambda *refs: early_kernel(n, *refs),
        out_shape=jax.ShapeDtypeStruct((n * rows, features), jnp.float32),
        grid=(width // STEP_K,),
        in_specs=[pl.BlockSpec((rows, STEP_K), lambda k: (0, k))] * n
        + [pl.BlockSpec((features, STEP_K), lambda k: (0, k))],
        out_specs=pl.BlockSpec((n * rows, features), lambda k: (0, 0)),
        compiler_params=pltpu.CompilerParams(vmem_limit_bytes=VMEM_BYTES),
        cost_estimate=pl.CostEstimate(
            flops=2 * n * rows * width * features,
            bytes_accessed=2 * width * (features + n * rows),
            transcendentals=0,
        ),
    )(*shards, weight)


def frozen_kernel(n, early, place_ref, real_ref, *refs):
    shards, weight, at_columns, down = refs[:n], refs[n], refs[n + 1], refs[n + 2]
    before = refs[n + 3 : n + 3 + early]
    out, total, extra, done, sems = refs[-5:]
    rows = shards[0].shape[0]
    step = pl.program_id(0)
    left = jnp.concatenate([s[...] for s in shards], axis=0)
    part = dot(left, weight[...], ((1,), (1,)))

    @pl.when(step == 0)
    def _():
        total[...] = part

    @pl.when(step > 0)
    def _():
        total[...] += part

    @pl.when(step == pl.num_programs(0) - 1)
    def _():
        copies = []
        columns = at_columns.shape[2] - BLOCK
        blocks = [(a, k) for a in (*before, total) for k in range(a.shape[0] // BLOCK)]
        for i, (source, k) in enumerate(blocks):
            block = place_ref[i * CORES] // CORES
            back = at_columns[block][:, columns:]
            extra[...] = dot(back, down[block], ((0,), (0,)))
            for j in range(CORES):
                place = place_ref[i * CORES + j]
                core = place % CORES
                here = pl.ds(i * BLOCK + j * rows, rows)
                value = source[pl.ds(k * BLOCK + j * rows, rows), :]
                value = value + adapter_scale * extra[pl.ds(core * rows, rows), :]
                limit = real_ref[block] - core * rows
                keep = lax.broadcasted_iota(jnp.int32, value.shape, 0) < limit
                done[here, :] = jnp.where(keep, value, 0.0).astype(jnp.bfloat16)
                copy = pltpu.make_async_copy(
                    done.at[here, :],
                    out.at[pl.ds(pl.multiple_of(place * rows, rows), rows), :],
                    sems.at[i * CORES + j],
                )
                copy.start()
                copies.append(copy)
        for copy in copies:
            copy.wait()


def frozen_rows(places, real, shards, weight, at_columns, down, before, held=()):
    n, early, count = len(shards), len(before), len(places)
    rows, width = shards[0].shape
    features = weight.shape[0]
    all_rows = down.shape[0] * BLOCK
    whole = lambda a: pl.BlockSpec(a.shape, lambda k, p, q: (0,) * a.ndim)
    grid_spec = pltpu.PrefetchScalarGridSpec(
        num_scalar_prefetch=2,
        grid=(width // STEP_K,),
        in_specs=[pl.BlockSpec((rows, STEP_K), lambda k, p, q: (0, k))] * n
        + [
            pl.BlockSpec((features, STEP_K), lambda k, p, q: (0, k)),
            whole(at_columns),
            whole(down),
        ]
        + [whole(a) for a in before]
        + [pl.BlockSpec(memory_space=pl.ANY)] * len(held),
        out_specs=pl.BlockSpec(memory_space=pl.ANY),
        scratch_shapes=[
            pltpu.VMEM((n * rows, features), jnp.float32),
            pltpu.VMEM((BLOCK, features), jnp.float32),
            pltpu.VMEM((count * rows, features), jnp.bfloat16),
            pltpu.SemaphoreType.DMA((count,)),
        ],
    )
    return pl.pallas_call(
        lambda *refs: frozen_kernel(n, early, *refs),
        out_shape=jax.ShapeDtypeStruct((all_rows, features), jnp.bfloat16),
        grid_spec=grid_spec,
        input_output_aliases={n + early + 5: 0} if held else {},
        compiler_params=pltpu.CompilerParams(vmem_limit_bytes=VMEM_BYTES),
        cost_estimate=pl.CostEstimate(
            flops=2 * n * rows * width * features,
            bytes_accessed=2 * width * (features + n * rows),
            transcendentals=0,
        ),
    )(
        jnp.stack(places).astype(jnp.int32),
        real,
        *shards,
        weight,
        at_columns,
        down,
        *before,
        *held,
    )


def per_device(
    output_cotangent,
    acts,
    output_weight,
    adapter_down_weight,
    adapter_up_weight,
    counts,
    block_tenant_map,
    owner,
):
    f32, bf16 = jnp.float32, jnp.bfloat16
    shard_rows, width = output_cotangent.shape
    features = acts.shape[1]
    held_slots, rank, columns = adapter_up_weight.shape
    nblk_loc = acts.shape[0] // BLOCK
    mp = width // columns
    ring = mp // CORES
    slot_count = owner.shape[0]
    nblocks = block_tenant_map.shape[0]
    group = lax.axis_index("dp")
    member = lax.axis_index("mp")
    z, core = member // CORES, member % CORES
    y, x = group // SIDE, group % SIDE
    at = jnp.stack([x, y, z, core]).astype(jnp.int32)

    def ring_a(v):
        return lax.ppermute(v, "mp", ring_step(1, ring))

    def ring_b(v):
        return lax.ppermute(v, "mp", ring_step(-1, ring))

    def swap(v):
        return lax.ppermute(v, "mp", [(i, i ^ 1) for i in range(mp)])

    same_core = [[r * CORES + c for r in range(ring)] for c in range(CORES)]

    def x_exchange(v):
        return [v] + [lax.ppermute(v, "dp", x_step(shift)) for shift in SHIFTS[1:]]

    def y_exchange(vs):
        moved = zip(SHIFTS[1:], vs[1:])
        return [vs[0]] + [lax.ppermute(v, "dp", y_step(shift)) for shift, v in moved]

    def z_exchange(v):
        return lax.all_to_all(v, "mp", 0, 0, tiled=True, axis_index_groups=same_core)

    toward = 1 - 2 * core

    def places(*steps):
        found = []
        for s in steps:
            chip = (z - s * toward + ring) % ring
            found += [chip * CORES + core, chip * CORES + 1 - core]
        return found

    def shaped(*shape, dtype=bf16):
        return jax.ShapeDtypeStruct(shape, dtype)

    own = output_cotangent
    a1, b1 = ring_a(own), ring_b(own)

    tenant_ids = jnp.arange(slot_count, dtype=jnp.int32)
    global_ids = jnp.arange(nblocks, dtype=jnp.int32)
    slot_blk = jnp.sum(
        jnp.where(block_tenant_map[:, None] == tenant_ids[None, :], owner[None, :], 0), axis=1
    )
    first_block = group * nblk_loc
    local_map = lax.dynamic_slice_in_dim(block_tenant_map, first_block, nblk_loc)
    local_ids = first_block + jnp.arange(nblk_loc, dtype=jnp.int32)
    same = (local_map[:, None] == block_tenant_map[None, :]) & (
        global_ids[None, :] < local_ids[:, None]
    )
    before = jnp.sum(same.astype(jnp.int32), axis=1)
    hit = local_map[:, None] == tenant_ids[None, :]
    limit = jnp.sum(jnp.where(hit, counts[None, :], 0), axis=1)
    real = limit - before * BLOCK

    held = jnp.concatenate([jnp.swapaxes(adapter_down_weight, 1, 2), adapter_up_weight], axis=2)
    near = x_exchange(held)
    picked = local_call(
        pick_kernel,
        [shaped(nblk_loc, rank, features + columns)] * SIDE,
        [at, slot_blk],
        near,
    )
    got = y_exchange(picked)
    mine_cols, other_cols = local_call(
        split_kernel,
        [shaped(shard_rows, width // CORES)] * CORES,
        [at, real],
        [own],
    )
    other_cols = swap(other_cols)
    a2, b2 = ring_a(a1), ring_b(b1)
    got, mine_cols, other_cols, a1, b1 = lax.optimization_barrier(
        (got, mine_cols, other_cols, a1, b1)
    )
    down_factor, to_rows = local_call(
        low_kernel,
        [shaped(nblk_loc, rank, features), shaped(nblk_loc, rank, columns + 2 * BLOCK)],
        [],
        [*got, acts],
    )
    at_rows = z_exchange(to_rows)
    early = [early_rows([own, swap(own), a1, swap(b1), b1, swap(a1)], output_weight)]
    a3, b3 = ring_a(a2), ring_b(b2)
    at_rows, early, a2, b2 = lax.optimization_barrier((at_rows, early, a2, b2))
    (sums,) = local_call(
        sums_kernel,
        [shaped(2 * rank, BLOCK, dtype=f32)],
        [at],
        [at_rows, mine_cols, other_cols],
    )
    (to_columns,) = local_call(
        columns_kernel,
        [shaped(ring, rank, columns + BLOCK)],
        [at],
        [sums, swap(sums), mine_cols, other_cols],
    )
    at_columns = z_exchange(to_columns)
    early = early + [early_rows([a2, swap(b2), b2, swap(a2)], output_weight)]
    a4 = ring_a(a3)
    at_columns, early, a3, b3 = lax.optimization_barrier((at_columns, early, a3, b3))
    (grads,) = local_call(
        grads_kernel,
        [shaped(nblk_loc, rank, features + columns)],
        [],
        [at_columns, acts],
    )
    near_grads = x_exchange(grads)
    out = frozen_rows(
        places(0, 1, -1, 2, -2, 3, -3),
        real,
        [a3, swap(b3), b3, swap(a3)],
        output_weight,
        at_columns,
        down_factor,
        early,
    )
    near_grads, out, a4 = lax.optimization_barrier((near_grads, out, a4))
    (*summed, _) = local_call(
        slots_kernel,
        [shaped(held_slots, rank, features + columns)] * SIDE
        + [shaped(SIDE * held_slots, rank, features + columns, dtype=f32)],
        [at, slot_blk],
        near_grads,
    )
    arrived = y_exchange(summed)
    input_gradient = frozen_rows(
        places(4), real, [a4, swap(a4)], output_weight, at_columns, down_factor, (), (out,)
    )
    arrived, input_gradient = lax.optimization_barrier((arrived, input_gradient))
    grad_down, grad_up = local_call(
        finish_kernel,
        [shaped(held_slots, rank, features, dtype=f32), shaped(held_slots, rank, columns, dtype=f32)],
        [],
        arrived,
    )
    return (input_gradient, jnp.swapaxes(grad_down, 1, 2), grad_up)


def solution(mesh):
    in_specs = (
        P(("dp", "mp"), None),
        P("dp", "mp"),
        P("mp", None),
        P("dp", "mp", None),
        P("dp", None, "mp"),
        P(),
        P(),
        P(),
    )
    out_specs = (P("dp", "mp"), P("dp", "mp", None), P("dp", None, "mp"))
    return jax.shard_map(
        per_device, mesh=mesh, in_specs=in_specs, out_specs=out_specs, check_vma=False
    )
```

time: 388 us -> 135 us (0.35)
  waiting for transfers between devices: 273 us -> 41.2 us
  blocking collectives: 56.9 us -> 0 us
  Pallas kernels: 0 us -> 42.8 us
  starting transfers between devices: 0.19 us -> 42.3 us
  matrix products: 38.1 us -> 0 us
  between operations: 14.5 us -> 0.81 us
    all_gather x5 -> x0, waiting for transfers between devices: 271 us -> none  [the longest x1 96 us: per_device(): gathered = lax.all_gather(output_cotangent, 'mp', axis=0, tiled=True)]
    psum x1 -> x0, blocking collectives: 44.4 us -> none  [per_device(): low_sum, back_sum = lax.psum((low_part, back_part), 'mp')]
    pallas_call x0 -> x12, Pallas kernels: none -> 42.8 us  [the longest x2 17.4 us: frozen_rows(): pl.pallas_call(lambda *refs: frozen_kernel(n, early, *refs), out_shape=ja...]
    dot_general x10 -> x0, matrix products: 38.1 us -> none  [the longest x1 16 us: per_device(): lax.dot_general(masked_rows.reshape(row_block_values, width), output_weig...]
    ppermute x0 -> x29, starting transfers between devices: none -> 34.6 us  [the longest x6 8.67 us: y_exchange(): lax.ppermute(v, 'dp', y_step(shift))]
    all_to_all x0 -> x2, waiting for transfers between devices: none -> 26.5 us  [z_exchange(): lax.all_to_all(v, 'mp', 0, 0, tiled=True, axis_index_groups=same_core)]
    ppermute x0 -> x29, waiting for transfers between devices: none -> 14.7 us  [the longest x6 5.19 us: y_exchange(): lax.ppermute(v, 'dp', y_step(shift))]
    unnamed x1 -> x0, blocking collectives: 12.5 us -> none
  transfers between devices with their start and end apart: 5 -> 31, of which waited for: 5 -> 9; matrix products, arithmetic and copies ran while one was open for 8% -> 3% of each run, Pallas kernels for 0% -> 31%
where the time goes in v2:
time: 135 us; the launch traced here: 134 us
  Pallas kernels  42.8 us (32%)
  starting transfers between devices  42.3 us (31%)
  waiting for transfers between devices  41.2 us (31%)
  other arithmetic  3.98 us (3%)
  local copies, waits for them, and re-layouts  3.23 us (2%)
    all_to_all x2, waiting for transfers between devices, z_exchange(): lax.all_to_all(v, 'mp', 0, 0, tiled=True, axis_index_groups=same_core)  26.5 us
    pallas_call x2, Pallas kernels, frozen_rows(): pl.pallas_call(lambda *refs: frozen_kernel(n, early, *refs), out_shape=ja...  17.4 us
    pallas_call x2, Pallas kernels, early_rows(): pl.pallas_call(lambda *refs: early_kernel(n, *refs), out_shape=jax.ShapeD...  16 us
    pallas_call x8, Pallas kernels, local_call(): pl.pallas_call(kernel, out_shape=tuple(out_shapes), in_specs=[pl.BlockSpe...  9.45 us
    ppermute x6, starting transfers between devices, y_exchange(): lax.ppermute(v, 'dp', y_step(shift))  8.67 us
    ppermute x4, starting transfers between devices, ring_a(): return lax.ppermute(v, 'mp', ring_step(1, ring))  8.4 us
    ppermute x6, starting transfers between devices, x_exchange(): return [v] + [lax.ppermute(v, 'dp', x_step(shift)) for shift in SHIFTS[1:]]  8.09 us
    ppermute x10, starting transfers between devices, swap(): return lax.ppermute(v, 'mp', [(i, i ^ 1) for i in range(mp)])  7.97 us
  transfers between devices with their start and end apart: 31, of which 9 were waited for; matrix products, arithmetic and copies ran while one was open for 3% of the time, Pallas kernels for 31%

profile of v2, /device:TPU:1, one launch (start us, length us, event | category | flops | bytes accessed | tf_op | source)
XLA Modules:
  0.0 134.3 jit_solution(15010200324471610200)
XLA Ops:
  1.5 2.1 %collective-permute-start = (bf16[4,16,1024]{2,1,0:T(8,128)(2,1)S(1)}, bf16[4,16,1024]{2,1,0:T(8,128)(2,1)S(1)}, u32[]{:S(2)}, u32[]{:S(2)}) collective-permute-start(bf16[4,16,1024]{2,1,0:T(8,128)(2,1)S(1)} %pad_maximum_fusion.refs_0_), channel_id=1, source_target_pairs={{0,16},{16,32},{32,48},{48,0},{64,80},{80,96},{96,112},{112,64},{1... | collective-permute-start | bytes 393224 | tf_op jit(solution)/shard_map/ppermute | solution.py:348
  3.6 1.4 %collective-permute-start.1 = (bf16[4,16,1024]{2,1,0:T(8,128)(2,1)S(1)}, bf16[4,16,1024]{2,1,0:T(8,128)(2,1)S(1)}, u32[]{:S(2)}, u32[]{:S(2)}) collective-permute-start(bf16[4,16,1024]{2,1,0:T(8,128)(2,1)S(1)} %pad_maximum_fusion.refs_0_), channel_id=1, source_target_pairs={{0,48},{16,0},{32,16},{48,32},{64,112},{80,64},{96,80},{112,96},{1... | collective-permute-start | bytes 393224 | tf_op jit(solution)/shard_map/ppermute | solution.py:348
  5.0 1.6 %collective-permute-start.2 = (bf16[4,16,1024]{2,1,0:T(8,128)(2,1)S(1)}, bf16[4,16,1024]{2,1,0:T(8,128)(2,1)S(1)}, u32[]{:S(2)}, u32[]{:S(2)}) collective-permute-start(bf16[4,16,1024]{2,1,0:T(8,128)(2,1)S(1)} %pad_maximum_fusion.refs_0_), channel_id=1, source_target_pairs={{0,32},{16,48},{32,0},{48,16},{64,96},{80,112},{96,64},{112,80},{1... | collective-permute-start | bytes 393224 | tf_op jit(solution)/shard_map/ppermute | solution.py:348
  6.6 5.6 %collective-permute-start.7 = (bf16[64,8192]{1,0:T(8,128)(2,1)}, bf16[64,8192]{1,0:T(8,128)(2,1)}, u32[]{:S(2)}, u32[]{:S(2)}) collective-permute-start(bf16[64,8192]{1,0:T(8,128)(2,1)} %refs_0_.1), channel_id=1, source_target_pairs={{0,2},{1,15},{2,4},{3,1},{4,6},{5,3},{6,8},{7,5},{8,10},{9,7},{10,... | collective-permute-start | bytes 3145736 | tf_op jit(solution)/shard_map/ppermute | solution.py:337
  16.7 1.4 %collective-permute-start.3 = (bf16[8,16,1024]{2,1,0:T(8,128)(2,1)S(1)}, bf16[8,16,1024]{2,1,0:T(8,128)(2,1)S(1)}, u32[]{:S(2)}, u32[]{:S(2)}) collective-permute-start(bf16[8,16,1024]{2,1,0:T(8,128)(2,1)S(1)} %get-tuple-element.46), channel_id=1, source_target_pairs={{0,64},{16,80},{32,96},{48,112},{64,128},{80,144},{96,160},{112,17... | collective-permute-start | bytes 786440 | tf_op jit(solution)/shard_map/ppermute | solution.py:352
  18.0 1.3 shard_map.104
  19.4 2.2 %collective-permute-start.6 = (bf16[64,4096]{1,0:T(8,128)(2,1)S(1)}, bf16[64,4096]{1,0:T(8,128)(2,1)S(1)}, u32[]{:S(2)}, u32[]{:S(2)}) collective-permute-start(bf16[64,4096]{1,0:T(8,128)(2,1)S(1)} %get-tuple-element.50), channel_id=1, source_target_pairs={{0,1},{1,0},{2,3},{3,2},{4,5},{5,4},{6,7},{7,6},{8,9},{9,8},{10,11... | collective-permute-start | bytes 1572872 | tf_op jit(solution)/shard_map/ppermute | solution.py:343
  21.5 1.4 %collective-permute-start.4 = (bf16[8,16,1024]{2,1,0:T(8,128)(2,1)S(1)}, bf16[8,16,1024]{2,1,0:T(8,128)(2,1)S(1)}, u32[]{:S(2)}, u32[]{:S(2)}) collective-permute-start(bf16[8,16,1024]{2,1,0:T(8,128)(2,1)S(1)} %get-tuple-element.47), channel_id=1, source_target_pairs={{0,192},{16,208},{32,224},{48,240},{64,0},{80,16},{96,32},{112,48}... | collective-permute-start | bytes 786440 | tf_op jit(solution)/shard_map/ppermute | solution.py:352
  22.9 1.3 collective-permute-done.3.refs_1_
  24.2 1.6 %collective-permute-start.5 = (bf16[8,16,1024]{2,1,0:T(8,128)(2,1)S(1)}, bf16[8,16,1024]{2,1,0:T(8,128)(2,1)S(1)}, u32[]{:S(2)}, u32[]{:S(2)}) collective-permute-start(bf16[8,16,1024]{2,1,0:T(8,128)(2,1)S(1)} %get-tuple-element.48), channel_id=1, source_target_pairs={{0,128},{16,144},{32,160},{48,176},{64,192},{80,208},{96,224},{112... | collective-permute-start | bytes 786440 | tf_op jit(solution)/shard_map/ppermute | solution.py:352
  25.8 3.7 %collective-permute-done.4.refs_2_ = bf16[8,16,1024]{2,1,0:T(8,128)(2,1)S(1)} collective-permute-done((bf16[8,16,1024]{2,1,0:T(8,128)(2,1)S(1)}, bf16[8,16,1024]{2,1,0:T(8,128)(2,1)S(1)}, u32[]{:S(2)}, u32[]{:S(2)}) %collective-permute-start.4) | collective-permute-done | bytes 262176 | tf_op jit(solution)/shard_map/ppermute | solution.py:352
  29.5 1.2 collective-permute-start.9
  30.9 2.6 %collective-permute-done.7.refs_2_ = bf16[64,8192]{1,0:T(8,128)(2,1)} collective-permute-done((bf16[64,8192]{1,0:T(8,128)(2,1)}, bf16[64,8192]{1,0:T(8,128)(2,1)}, u32[]{:S(2)}, u32[]{:S(2)}) %collective-permute-start.7) | collective-permute-done | bytes 1048608 | tf_op jit(solution)/shard_map/ppermute | solution.py:337
  33.5 4.2 %collective-permute-done.8.refs_4_ = bf16[64,8192]{1,0:T(8,128)(2,1)} collective-permute-done((bf16[64,8192]{1,0:T(8,128)(2,1)}, bf16[64,8192]{1,0:T(8,128)(2,1)}, u32[]{:S(2)}, u32[]{:S(2)}) %collective-permute-start.8) | collective-permute-done | bytes 1048608 | tf_op jit(solution)/shard_map/ppermute | solution.py:340
  39.6 1.2 copy-done
  42.6 3.8 %all-to-all-start = ((bf16[8,16,768]{2,1,0:T(8,128)(2,1)}), bf16[8,16,768]{2,1,0:T(8,128)(2,1)S(1)}, u32[]{:S(2)}, u32[]{:S(2)}) async-start(bf16[8,16,768]{2,1,0:T(8,128)(2,1)} %get-tuple-element.55), calls=%async_computation | async-start | bytes 393216 | tf_op jit(solution)/shard_map/all_to_all | solution.py:355
  46.4 8.6 %shard_map.106.refs_9_ = f32[384,512]{1,0:T(8,128)} custom-call(bf16[64,8192]{1,0:T(8,128)(2,1)} %refs_0_.1, bf16[64,8192]{1,0:T(8,128)(2,1)} %collective-permute-done.9.refs_1_, bf16[64,8192]{1,0:T(8,128)(2,1)} %collective-permute-done.7.refs_2_, bf16[64,8192]{1,0:T(8,128)(2,1)} %collective-permute-done.10.refs_3_, ...), custom_call_target="tpu_custom_call" | custom-call | flops 3221225472 | bytes 14680064 | tf_op jit(solution)/shard_map/pallas_call | solution.py:201
  54.9 14.2 %all-to-all-done.at_rows = bf16[8,16,768]{2,1,0:T(8,128)(2,1)S(1)} async-done(((bf16[8,16,768]{2,1,0:T(8,128)(2,1)}), bf16[8,16,768]{2,1,0:T(8,128)(2,1)S(1)}, u32[]{:S(2)}, u32[]{:S(2)}) %all-to-all-start) | async-done | bytes 196640 | tf_op jit(solution)/shard_map/all_to_all | solution.py:355
  70.3 1.2 collective-permute-start.18
  72.4 1.9 %collective-permute-start.14 = (f32[32,128]{1,0:T(8,128)S(1)}, f32[32,128]{1,0:T(8,128)S(1)}, u32[]{:S(2)}, u32[]{:S(2)}) collective-permute-start(f32[32,128]{1,0:T(8,128)S(1)} %shard_map.107.sums), channel_id=1, source_target_pairs={{0,1},{1,0},{2,3},{3,2},{4,5},{5,4},{6,7},{7,6},{8,9},{9,8},{10,11... | collective-permute-start | bytes 49160 | tf_op jit(solution)/shard_map/ppermute | solution.py:343
  75.2 1.6 %shard_map.108 = bf16[8,16,640]{2,1,0:T(8,128)(2,1)} custom-call(s32[4]{0:T(128)S(1)} %pad_add_fusion.at_ref, f32[32,128]{1,0:T(8,128)S(1)} %shard_map.107.sums, f32[32,128]{1,0:T(8,128)S(1)} %collective-permute-done.14.more, bf16[64,4096]{1,0:T(8,128)(2,1)S(1)} %get-tuple-element.59.mine, bf16[64,4096]{1,0:T(8,128)(2,1)S(1)} %collective-permute-done.6.other), custom_call_target="tpu_custom_call" | custom-call | bytes 1245184 | tf_op jit(solution)/shard_map/pallas_call | solution.py:46
  76.8 3.9 %all-to-all-start.1 = ((bf16[8,16,640]{2,1,0:T(8,128)(2,1)}), bf16[8,16,640]{2,1,0:T(8,128)(2,1)S(1)}, u32[]{:S(2)}, u32[]{:S(2)}) async-start(bf16[8,16,640]{2,1,0:T(8,128)(2,1)} %shard_map.108), calls=%async_computation.1 | async-start | bytes 327680 | tf_op jit(solution)/shard_map/all_to_all | solution.py:355
  80.7 7.4 %shard_map.109.refs_10_ = f32[256,512]{1,0:T(8,128)} custom-call(bf16[64,8192]{1,0:T(8,128)(2,1)} %copy-done.6, bf16[64,8192]{1,0:T(8,128)(2,1)} %collective-permute-done.15.refs_1_, bf16[64,8192]{1,0:T(8,128)(2,1)} %collective-permute-done.13.refs_2_, bf16[64,8192]{1,0:T(8,128)(2,1)} %collective-permute-done.16.refs_3_, bf16[512,8192]{1,0:T(8,128)(2,1)} %refs_4_.5), custom_call_target="tpu_custom_call" | custom-call | flops 2147483648 | bytes 12582912 | tf_op jit(solution)/shard_map/pallas_call | solution.py:201
  88.1 12.2 %all-to-all-done.1.at_columns.refs_7_.refs_5_ = bf16[8,16,640]{2,1,0:T(8,128)(2,1)S(1)} async-done(((bf16[8,16,640]{2,1,0:T(8,128)(2,1)}), bf16[8,16,640]{2,1,0:T(8,128)(2,1)S(1)}, u32[]{:S(2)}, u32[]{:S(2)}) %all-to-all-start.1) | async-done | bytes 163872 | tf_op jit(solution)/shard_map/all_to_all | solution.py:355
  101.0 1.4 %collective-permute-start.24 = (bf16[64,8192]{1,0:T(8,128)(2,1)}, bf16[64,8192]{1,0:T(8,128)(2,1)S(1)}, u32[]{:S(2)}, u32[]{:S(2)}) collective-permute-start(bf16[64,8192]{1,0:T(8,128)(2,1)} %collective-permute-done.17.refs_2_), channel_id=1, source_target_pairs={{0,2},{1,15},{2,4},{3,1},{4,6},{5,3},{6,8},{7,5},{8,10},{9,7},{10,... | collective-permute-start | bytes 3145736 | tf_op jit(solution)/shard_map/ppermute | solution.py:337
  103.0 2.4 %collective-permute-start.20 = (bf16[8,16,1024]{2,1,0:T(8,128)(2,1)S(1)}, bf16[8,16,1024]{2,1,0:T(8,128)(2,1)S(1)}, u32[]{:S(2)}, u32[]{:S(2)}) collective-permute-start(bf16[8,16,1024]{2,1,0:T(8,128)(2,1)S(1)} %shard_map.110.refs_0_), channel_id=1, source_target_pairs={{0,48},{16,0},{32,16},{48,32},{64,112},{80,64},{96,80},{112,96},{1... | collective-permute-start | bytes 786440 | tf_op jit(solution)/shard_map/ppermute | solution.py:348
  106.2 9.4 %shard_map.111.refs_7_ = bf16[1024,512]{1,0:T(8,128)(2,1)} custom-call(s32[14]{0:T(128)} %stack.88.refs_0_, s32[8]{0:T(128)} %copy-done.4, bf16[64,8192]{1,0:T(8,128)(2,1)} %collective-permute-done.17.refs_2_, bf16[64,8192]{1,0:T(8,128)(2,1)} %collective-permute-done.22.refs_3_, bf16[64,8192]{1,0:T(8,128)(2,1)} %collective-permute-done.18.refs_4_, ...), custom_call_target="tpu_custom_call" | custom-call | flops 2147483648 | bytes 12582912 | tf_op jit(solution)/shard_map/pallas_call | solution.py:288
  115.6 1.9 %collective-permute-done.19.refs_1_ = bf16[8,16,1024]{2,1,0:T(8,128)(2,1)S(1)} collective-permute-done((bf16[8,16,1024]{2,1,0:T(8,128)(2,1)S(1)}, bf16[8,16,1024]{2,1,0:T(8,128)(2,1)S(1)}, u32[]{:S(2)}, u32[]{:S(2)}) %collective-permute-start.19) | collective-permute-done | bytes 262176 | tf_op jit(solution)/shard_map/ppermute | solution.py:348
  118.3 2.3 %shard_map.112 = (bf16[4,16,1024]{2,1,0:T(8,128)(2,1)S(1)}, bf16[4,16,1024]{2,1,0:T(8,128)(2,1)S(1)}, bf16[4,16,1024]{2,1,0:T(8,128)(2,1)S(1)}, bf16[4,16,1024]{2,1,0:T(8,128)(2,1)S(1)}, f32[16,16,1024]{2,1,0:T(8,128)}) custom-call(s32[4]{0:T(128)S(1)} %pad_add_fusion.at_ref, s32[128]{0:T(128)S(1)} %select_reduce_fusion.slot_ref, ...), custom_call_target="tpu_custom_call" | custom-call | bytes 2621440 | tf_op jit(solution)/shard_map/pallas_call | solution.py:46
  121.4 2.0 %collective-permute-start.26 = (bf16[4,16,1024]{2,1,0:T(8,128)(2,1)S(1)}, bf16[4,16,1024]{2,1,0:T(8,128)(2,1)S(1)}, u32[]{:S(2)}, u32[]{:S(2)}) collective-permute-start(bf16[4,16,1024]{2,1,0:T(8,128)(2,1)S(1)} %get-tuple-element.76), channel_id=1, source_target_pairs={{0,192},{16,208},{32,224},{48,240},{64,0},{80,16},{96,32},{112,48}... | collective-permute-start | bytes 393224 | tf_op jit(solution)/shard_map/ppermute | solution.py:352
  123.4 1.5 %collective-permute-start.27 = (bf16[4,16,1024]{2,1,0:T(8,128)(2,1)S(1)}, bf16[4,16,1024]{2,1,0:T(8,128)(2,1)S(1)}, u32[]{:S(2)}, u32[]{:S(2)}) collective-permute-start(bf16[4,16,1024]{2,1,0:T(8,128)(2,1)S(1)} %get-tuple-element.77), channel_id=1, source_target_pairs={{0,128},{16,144},{32,160},{48,176},{64,192},{80,208},{96,224},{112... | collective-permute-start | bytes 393224 | tf_op jit(solution)/shard_map/ppermute | solution.py:352
  125.6 8.0 %shard_map.113 = bf16[1024,512]{1,0:T(8,128)(2,1)} custom-call(s32[2]{0:T(128)} %pad_add_fusion.1.refs_0_, s32[8]{0:T(128)} %copy-done.4, bf16[64,8192]{1,0:T(8,128)(2,1)} %copy-done.5, bf16[64,8192]{1,0:T(8,128)(2,1)} %collective-permute-done.28.refs_3_, bf16[512,8192]{1,0:T(8,128)(2,1)} %refs_4_.5, ...), custom_call_target="tpu_custom_call", output_to_operand_aliasing={{}: (7, {})} | custom-call | flops 1073741824 | bytes 10485760 | tf_op jit(solution)/shard_map/pallas_call | solution.py:288
  (66 shorter events, 17.1 us)
Async XLA Ops:
  1.5 14.0 %collective-permute-start = (bf16[4,16,1024]{2,1,0:T(8,128)(2,1)S(1)}, bf16[4,16,1024]{2,1,0:T(8,128)(2,1)S(1)}, u32[]{:S(2)}, u32[]{:S(2)}) collective-permute-start(bf16[4,16,1024]{2,1,0:T(8,128)(2,1)S(1)} %pad_maximum_fusion.refs_0_), channel_id=1, source_target_pairs={{0,16},{16,32},{32,48},{48,0},{64,80},{80,96},{96,112},{112,64},{1... | collective-permute-start | bytes 393224 | tf_op jit(solution)/shard_map/ppermute | solution.py:348
  3.6 11.8 %collective-permute-start.1 = (bf16[4,16,1024]{2,1,0:T(8,128)(2,1)S(1)}, bf16[4,16,1024]{2,1,0:T(8,128)(2,1)S(1)}, u32[]{:S(2)}, u32[]{:S(2)}) collective-permute-start(bf16[4,16,1024]{2,1,0:T(8,128)(2,1)S(1)} %pad_maximum_fusion.refs_0_), channel_id=1, source_target_pairs={{0,48},{16,0},{32,16},{48,32},{64,112},{80,64},{96,80},{112,96},{1... | collective-permute-start | bytes 393224 | tf_op jit(solution)/shard_map/ppermute | solution.py:348
  5.0 10.5 %collective-permute-start.2 = (bf16[4,16,1024]{2,1,0:T(8,128)(2,1)S(1)}, bf16[4,16,1024]{2,1,0:T(8,128)(2,1)S(1)}, u32[]{:S(2)}, u32[]{:S(2)}) collective-permute-start(bf16[4,16,1024]{2,1,0:T(8,128)(2,1)S(1)} %pad_maximum_fusion.refs_0_), channel_id=1, source_target_pairs={{0,32},{16,48},{32,0},{48,16},{64,96},{80,112},{96,64},{112,80},{1... | collective-permute-start | bytes 393224 | tf_op jit(solution)/shard_map/ppermute | solution.py:348
  6.6 26.8 %collective-permute-start.7 = (bf16[64,8192]{1,0:T(8,128)(2,1)}, bf16[64,8192]{1,0:T(8,128)(2,1)}, u32[]{:S(2)}, u32[]{:S(2)}) collective-permute-start(bf16[64,8192]{1,0:T(8,128)(2,1)} %refs_0_.1), channel_id=1, source_target_pairs={{0,2},{1,15},{2,4},{3,1},{4,6},{5,3},{6,8},{7,5},{8,10},{9,7},{10,... | collective-permute-start | bytes 3145736 | tf_op jit(solution)/shard_map/ppermute | solution.py:337
  12.2 25.4 %collective-permute-start.8 = (bf16[64,8192]{1,0:T(8,128)(2,1)}, bf16[64,8192]{1,0:T(8,128)(2,1)}, u32[]{:S(2)}, u32[]{:S(2)}) collective-permute-start(bf16[64,8192]{1,0:T(8,128)(2,1)} %refs_0_.1), channel_id=1, source_target_pairs={{0,14},{1,3},{2,0},{3,5},{4,2},{5,7},{6,4},{7,9},{8,6},{9,11},{10,... | collective-permute-start | bytes 3145736 | tf_op jit(solution)/shard_map/ppermute | solution.py:340
  16.7 7.5 %collective-permute-start.3 = (bf16[8,16,1024]{2,1,0:T(8,128)(2,1)S(1)}, bf16[8,16,1024]{2,1,0:T(8,128)(2,1)S(1)}, u32[]{:S(2)}, u32[]{:S(2)}) collective-permute-start(bf16[8,16,1024]{2,1,0:T(8,128)(2,1)S(1)} %get-tuple-element.46), channel_id=1, source_target_pairs={{0,64},{16,80},{32,96},{48,112},{64,128},{80,144},{96,160},{112,17... | collective-permute-start | bytes 786440 | tf_op jit(solution)/shard_map/ppermute | solution.py:352
  19.4 11.5 %collective-permute-start.6 = (bf16[64,4096]{1,0:T(8,128)(2,1)S(1)}, bf16[64,4096]{1,0:T(8,128)(2,1)S(1)}, u32[]{:S(2)}, u32[]{:S(2)}) collective-permute-start(bf16[64,4096]{1,0:T(8,128)(2,1)S(1)} %get-tuple-element.50), channel_id=1, source_target_pairs={{0,1},{1,0},{2,3},{3,2},{4,5},{5,4},{6,7},{7,6},{8,9},{9,8},{10,11... | collective-permute-start | bytes 1572872 | tf_op jit(solution)/shard_map/ppermute | solution.py:343
  21.5 8.0 %collective-permute-start.4 = (bf16[8,16,1024]{2,1,0:T(8,128)(2,1)S(1)}, bf16[8,16,1024]{2,1,0:T(8,128)(2,1)S(1)}, u32[]{:S(2)}, u32[]{:S(2)}) collective-permute-start(bf16[8,16,1024]{2,1,0:T(8,128)(2,1)S(1)} %get-tuple-element.47), channel_id=1, source_target_pairs={{0,192},{16,208},{32,224},{48,240},{64,0},{80,16},{96,32},{112,48}... | collective-permute-start | bytes 786440 | tf_op jit(solution)/shard_map/ppermute | solution.py:352
  24.2 6.7 %collective-permute-start.5 = (bf16[8,16,1024]{2,1,0:T(8,128)(2,1)S(1)}, bf16[8,16,1024]{2,1,0:T(8,128)(2,1)S(1)}, u32[]{:S(2)}, u32[]{:S(2)}) collective-permute-start(bf16[8,16,1024]{2,1,0:T(8,128)(2,1)S(1)} %get-tuple-element.48), channel_id=1, source_target_pairs={{0,128},{16,144},{32,160},{48,176},{64,192},{80,208},{96,224},{112... | collective-permute-start | bytes 786440 | tf_op jit(solution)/shard_map/ppermute | solution.py:352
  29.5 16.9 %collective-permute-start.9 = (bf16[64,8192]{1,0:T(8,128)(2,1)}, bf16[64,8192]{1,0:T(8,128)(2,1)}, u32[]{:S(2)}, u32[]{:S(2)}) collective-permute-start(bf16[64,8192]{1,0:T(8,128)(2,1)} %refs_0_.1), channel_id=1, source_target_pairs={{0,1},{1,0},{2,3},{3,2},{4,5},{5,4},{6,7},{7,6},{8,9},{9,8},{10,11... | collective-permute-start | bytes 3145736 | tf_op jit(solution)/shard_map/ppermute | solution.py:343
  37.6 8.7 %collective-permute-start.10 = (bf16[64,8192]{1,0:T(8,128)(2,1)}, bf16[64,8192]{1,0:T(8,128)(2,1)}, u32[]{:S(2)}, u32[]{:S(2)}) collective-permute-start(bf16[64,8192]{1,0:T(8,128)(2,1)} %collective-permute-done.8.refs_4_), channel_id=1, source_target_pairs={{0,1},{1,0},{2,3},{3,2},{4,5},{5,4},{6,7},{7,6},{8,9},{9,8},{10,11... | collective-permute-start | bytes 3145736 | tf_op jit(solution)/shard_map/ppermute | solution.py:343
  37.6 8.7 %collective-permute-start.11 = (bf16[64,8192]{1,0:T(8,128)(2,1)}, bf16[64,8192]{1,0:T(8,128)(2,1)}, u32[]{:S(2)}, u32[]{:S(2)}) collective-permute-start(bf16[64,8192]{1,0:T(8,128)(2,1)} %collective-permute-done.7.refs_2_), channel_id=1, source_target_pairs={{0,1},{1,0},{2,3},{3,2},{4,5},{5,4},{6,7},{7,6},{8,9},{9,8},{10,11... | collective-permute-start | bytes 3145736 | tf_op jit(solution)/shard_map/ppermute | solution.py:343
  38.2 31.0 %collective-permute-start.12 = (bf16[64,8192]{1,0:T(8,128)(2,1)}, bf16[64,8192]{1,0:T(8,128)(2,1)S(1)}, u32[]{:S(2)}, u32[]{:S(2)}) collective-permute-start(bf16[64,8192]{1,0:T(8,128)(2,1)} %collective-permute-done.7.refs_2_), channel_id=1, source_target_pairs={{0,2},{1,15},{2,4},{3,1},{4,6},{5,3},{6,8},{7,5},{8,10},{9,7},{10,... | collective-permute-start | bytes 3145736 | tf_op jit(solution)/shard_map/ppermute | solution.py:337
  39.3 29.9 %collective-permute-start.13 = (bf16[64,8192]{1,0:T(8,128)(2,1)}, bf16[64,8192]{1,0:T(8,128)(2,1)}, u32[]{:S(2)}, u32[]{:S(2)}) collective-permute-start(bf16[64,8192]{1,0:T(8,128)(2,1)} %collective-permute-done.8.refs_4_), channel_id=1, source_target_pairs={{0,14},{1,3},{2,0},{3,5},{4,2},{5,7},{6,4},{7,9},{8,6},{9,11},{10,... | collective-permute-start | bytes 3145736 | tf_op jit(solution)/shard_map/ppermute | solution.py:340
  42.6 26.6 %all-to-all-start = ((bf16[8,16,768]{2,1,0:T(8,128)(2,1)}), bf16[8,16,768]{2,1,0:T(8,128)(2,1)S(1)}, u32[]{:S(2)}, u32[]{:S(2)}) async-start(bf16[8,16,768]{2,1,0:T(8,128)(2,1)} %get-tuple-element.55), calls=%async_computation | async-start | bytes 393216 | tf_op jit(solution)/shard_map/all_to_all | solution.py:355
  54.9 47.4 %copy-start.1 = (bf16[1024,512]{1,0:T(8,128)(2,1)S(1)}, bf16[1024,512]{1,0:T(8,128)(2,1)}, u32[]{:S(2)}) copy-start(bf16[1024,512]{1,0:T(8,128)(2,1)} %acts.1) | copy-start | bytes 3145732
  69.2 11.4 %collective-permute-start.15 = (bf16[64,8192]{1,0:T(8,128)(2,1)}, bf16[64,8192]{1,0:T(8,128)(2,1)}, u32[]{:S(2)}, u32[]{:S(2)}) collective-permute-start(bf16[64,8192]{1,0:T(8,128)(2,1)} %collective-permute-done.13.refs_2_), channel_id=1, source_target_pairs={{0,1},{1,0},{2,3},{3,2},{4,5},{5,4},{6,7},{7,6},{8,9},{9,8},{10,11... | collective-permute-start | bytes 3145736 | tf_op jit(solution)/shard_map/ppermute | solution.py:343
  69.5 11.1 %collective-permute-start.16 = (bf16[64,8192]{1,0:T(8,128)(2,1)S(1)}, bf16[64,8192]{1,0:T(8,128)(2,1)}, u32[]{:S(2)}, u32[]{:S(2)}) collective-permute-start(bf16[64,8192]{1,0:T(8,128)(2,1)S(1)} %collective-permute-done.12.refs_0_), channel_id=1, source_target_pairs={{0,1},{1,0},{2,3},{3,2},{4,5},{5,4},{6,7},{7,6},{8,9},{9,8},{10,11... | collective-permute-start | bytes 3145736 | tf_op jit(solution)/shard_map/ppermute | solution.py:343
  70.0 30.3 %collective-permute-start.17 = (bf16[64,8192]{1,0:T(8,128)(2,1)S(1)}, bf16[64,8192]{1,0:T(8,128)(2,1)}, u32[]{:S(2)}, u32[]{:S(2)}) collective-permute-start(bf16[64,8192]{1,0:T(8,128)(2,1)S(1)} %collective-permute-done.12.refs_0_), channel_id=1, source_target_pairs={{0,2},{1,15},{2,4},{3,1},{4,6},{5,3},{6,8},{7,5},{8,10},{9,7},{10,... | collective-permute-start | bytes 3145736 | tf_op jit(solution)/shard_map/ppermute | solution.py:337
  70.3 30.0 %collective-permute-start.18 = (bf16[64,8192]{1,0:T(8,128)(2,1)}, bf16[64,8192]{1,0:T(8,128)(2,1)}, u32[]{:S(2)}, u32[]{:S(2)}) collective-permute-start(bf16[64,8192]{1,0:T(8,128)(2,1)} %collective-permute-done.13.refs_2_), channel_id=1, source_target_pairs={{0,14},{1,3},{2,0},{3,5},{4,2},{5,7},{6,4},{7,9},{8,6},{9,11},{10,... | collective-permute-start | bytes 3145736 | tf_op jit(solution)/shard_map/ppermute | solution.py:340
  72.4 2.7 %collective-permute-start.14 = (f32[32,128]{1,0:T(8,128)S(1)}, f32[32,128]{1,0:T(8,128)S(1)}, u32[]{:S(2)}, u32[]{:S(2)}) collective-permute-start(f32[32,128]{1,0:T(8,128)S(1)} %shard_map.107.sums), channel_id=1, source_target_pairs={{0,1},{1,0},{2,3},{3,2},{4,5},{5,4},{6,7},{7,6},{8,9},{9,8},{10,11... | collective-permute-start | bytes 49160 | tf_op jit(solution)/shard_map/ppermute | solution.py:343
  76.8 23.5 %all-to-all-start.1 = ((bf16[8,16,640]{2,1,0:T(8,128)(2,1)}), bf16[8,16,640]{2,1,0:T(8,128)(2,1)S(1)}, u32[]{:S(2)}, u32[]{:S(2)}) async-start(bf16[8,16,640]{2,1,0:T(8,128)(2,1)} %shard_map.108), calls=%async_computation.1 | async-start | bytes 327680 | tf_op jit(solution)/shard_map/all_to_all | solution.py:355
  100.3 5.0 %collective-permute-start.22 = (bf16[64,8192]{1,0:T(8,128)(2,1)}, bf16[64,8192]{1,0:T(8,128)(2,1)}, u32[]{:S(2)}, u32[]{:S(2)}) collective-permute-start(bf16[64,8192]{1,0:T(8,128)(2,1)} %collective-permute-done.18.refs_4_), channel_id=1, source_target_pairs={{0,1},{1,0},{2,3},{3,2},{4,5},{5,4},{6,7},{7,6},{8,9},{9,8},{10,11... | collective-permute-start | bytes 3145736 | tf_op jit(solution)/shard_map/ppermute | solution.py:343
  100.9 5.3 %collective-permute-start.23 = (bf16[64,8192]{1,0:T(8,128)(2,1)}, bf16[64,8192]{1,0:T(8,128)(2,1)}, u32[]{:S(2)}, u32[]{:S(2)}) collective-permute-start(bf16[64,8192]{1,0:T(8,128)(2,1)} %collective-permute-done.17.refs_2_), channel_id=1, source_target_pairs={{0,1},{1,0},{2,3},{3,2},{4,5},{5,4},{6,7},{7,6},{8,9},{9,8},{10,11... | collective-permute-start | bytes 3145736 | tf_op jit(solution)/shard_map/ppermute | solution.py:343
  101.0 16.6 %collective-permute-start.24 = (bf16[64,8192]{1,0:T(8,128)(2,1)}, bf16[64,8192]{1,0:T(8,128)(2,1)S(1)}, u32[]{:S(2)}, u32[]{:S(2)}) collective-permute-start(bf16[64,8192]{1,0:T(8,128)(2,1)} %collective-permute-done.17.refs_2_), channel_id=1, source_target_pairs={{0,2},{1,15},{2,4},{3,1},{4,6},{5,3},{6,8},{7,5},{8,10},{9,7},{10,... | collective-permute-start | bytes 3145736 | tf_op jit(solution)/shard_map/ppermute | solution.py:337
  102.6 15.0 %collective-permute-start.19 = (bf16[8,16,1024]{2,1,0:T(8,128)(2,1)S(1)}, bf16[8,16,1024]{2,1,0:T(8,128)(2,1)S(1)}, u32[]{:S(2)}, u32[]{:S(2)}) collective-permute-start(bf16[8,16,1024]{2,1,0:T(8,128)(2,1)S(1)} %shard_map.110.refs_0_), channel_id=1, source_target_pairs={{0,16},{16,32},{32,48},{48,0},{64,80},{80,96},{96,112},{112,64},{1... | collective-permute-start | bytes 786440 | tf_op jit(solution)/shard_map/ppermute | solution.py:348
  103.0 14.6 %collective-permute-start.20 = (bf16[8,16,1024]{2,1,0:T(8,128)(2,1)S(1)}, bf16[8,16,1024]{2,1,0:T(8,128)(2,1)S(1)}, u32[]{:S(2)}, u32[]{:S(2)}) collective-permute-start(bf16[8,16,1024]{2,1,0:T(8,128)(2,1)S(1)} %shard_map.110.refs_0_), channel_id=1, source_target_pairs={{0,48},{16,0},{32,16},{48,32},{64,112},{80,64},{96,80},{112,96},{1... | collective-permute-start | bytes 786440 | tf_op jit(solution)/shard_map/ppermute | solution.py:348
  105.4 12.2 %collective-permute-start.21 = (bf16[8,16,1024]{2,1,0:T(8,128)(2,1)S(1)}, bf16[8,16,1024]{2,1,0:T(8,128)(2,1)S(1)}, u32[]{:S(2)}, u32[]{:S(2)}) collective-permute-start(bf16[8,16,1024]{2,1,0:T(8,128)(2,1)S(1)} %shard_map.110.refs_0_), channel_id=1, source_target_pairs={{0,32},{16,48},{32,0},{48,16},{64,96},{80,112},{96,64},{112,80},{1... | collective-permute-start | bytes 786440 | tf_op jit(solution)/shard_map/ppermute | solution.py:348
  117.6 8.0 %collective-permute-start.28 = (bf16[64,8192]{1,0:T(8,128)(2,1)S(1)}, bf16[64,8192]{1,0:T(8,128)(2,1)}, u32[]{:S(2)}, u32[]{:S(2)}) collective-permute-start(bf16[64,8192]{1,0:T(8,128)(2,1)S(1)} %collective-permute-done.24.refs_2_), channel_id=1, source_target_pairs={{0,1},{1,0},{2,3},{3,2},{4,5},{5,4},{6,7},{7,6},{8,9},{9,8},{10,11... | collective-permute-start | bytes 3145736 | tf_op jit(solution)/shard_map/ppermute | solution.py:343
  120.7 12.9 %collective-permute-start.25 = (bf16[4,16,1024]{2,1,0:T(8,128)(2,1)S(1)}, bf16[4,16,1024]{2,1,0:T(8,128)(2,1)S(1)}, u32[]{:S(2)}, u32[]{:S(2)}) collective-permute-start(bf16[4,16,1024]{2,1,0:T(8,128)(2,1)S(1)} %get-tuple-element.75), channel_id=1, source_target_pairs={{0,64},{16,80},{32,96},{48,112},{64,128},{80,144},{96,160},{112,17... | collective-permute-start | bytes 393224 | tf_op jit(solution)/shard_map/ppermute | solution.py:352
  121.4 12.2 %collective-permute-start.26 = (bf16[4,16,1024]{2,1,0:T(8,128)(2,1)S(1)}, bf16[4,16,1024]{2,1,0:T(8,128)(2,1)S(1)}, u32[]{:S(2)}, u32[]{:S(2)}) collective-permute-start(bf16[4,16,1024]{2,1,0:T(8,128)(2,1)S(1)} %get-tuple-element.76), channel_id=1, source_target_pairs={{0,192},{16,208},{32,224},{48,240},{64,0},{80,16},{96,32},{112,48}... | collective-permute-start | bytes 393224 | tf_op jit(solution)/shard_map/ppermute | solution.py:352
  123.4 10.1 %collective-permute-start.27 = (bf16[4,16,1024]{2,1,0:T(8,128)(2,1)S(1)}, bf16[4,16,1024]{2,1,0:T(8,128)(2,1)S(1)}, u32[]{:S(2)}, u32[]{:S(2)}) collective-permute-start(bf16[4,16,1024]{2,1,0:T(8,128)(2,1)S(1)} %get-tuple-element.77), channel_id=1, source_target_pairs={{0,128},{16,144},{32,160},{48,176},{64,192},{80,208},{96,224},{112... | collective-permute-start | bytes 393224 | tf_op jit(solution)/shard_map/ppermute | solution.py:352
  (6 other events, 64.1 us)

commit v3 on v2

--- a/solution.py
+++ b/solution.py
@@ -402,9 +402,6 @@
     )
     other_cols = swap(other_cols)
     a2, b2 = ring_a(a1), ring_b(b1)
-    got, mine_cols, other_cols, a1, b1 = lax.optimization_barrier(
-        (got, mine_cols, other_cols, a1, b1)
-    )
     down_factor, to_rows = local_call(
         low_kernel,
         [shaped(nblk_loc, rank, features), shaped(nblk_loc, rank, columns + 2 * BLOCK)],
@@ -414,7 +411,9 @@
     at_rows = z_exchange(to_rows)
     early = [early_rows([own, swap(own), a1, swap(b1), b1, swap(a1)], output_weight)]
     a3, b3 = ring_a(a2), ring_b(b2)
-    at_rows, early, a2, b2 = lax.optimization_barrier((at_rows, early, a2, b2))
+    at_rows, early, a2, b2, mine_cols, other_cols = lax.optimization_barrier(
+        (at_rows, early, a2, b2, mine_cols, other_cols)
+    )
     (sums,) = local_call(
         sums_kernel,
         [shaped(2 * rank, BLOCK, dtype=f32)],

time: 135 us -> 132 us (0.978)
  waiting for transfers between devices: 41.2 us -> 26.5 us
  starting transfers between devices: 42.3 us -> 52.4 us
  local copies, waits for them, and re-layouts: 3.23 us -> 5.41 us
    all_to_all x2, waiting for transfers between devices: 26.5 us -> 15.5 us  [z_exchange(): lax.all_to_all(v, 'mp', 0, 0, tiled=True, axis_index_groups=same_core)]
    ppermute x10, starting transfers between devices: 7.97 us -> 12.8 us  [swap(): return lax.ppermute(v, 'mp', [(i, i ^ 1) for i in range(mp)])]
    ppermute x4, starting transfers between devices: 8.4 us -> 12.3 us  [ring_a(): return lax.ppermute(v, 'mp', ring_step(1, ring))]
    ppermute x3, waiting for transfers between devices: 4.19 us -> 1.08 us  [ring_b(): return lax.ppermute(v, 'mp', ring_step(-1, ring))]
    ppermute x6, waiting for transfers between devices: 1.94 us -> 4.75 us  [x_exchange(): return [v] + [lax.ppermute(v, 'dp', x_step(shift)) for shift in SHIFTS[1:]]]
    unnamed x14 -> x16, local copies, waits for them, and re-layouts: 1.9 us -> 4.07 us
    ppermute x6, waiting for transfers between devices: 5.19 us -> 3.08 us  [y_exchange(): lax.ppermute(v, 'dp', y_step(shift))]
    ppermute x6, starting transfers between devices: 8.67 us -> 10.2 us  [y_exchange(): lax.ppermute(v, 'dp', y_step(shift))]
  transfers between devices with their start and end apart: 31 -> 31, of which waited for: 9 -> 9; matrix products, arithmetic and copies ran while one was open for 3% -> 4% of each run, Pallas kernels for 31% -> 32%
where the time goes in v3:
time: 132 us
  starting transfers between devices  52.4 us (40%)
  Pallas kernels  42.4 us (32%)
  waiting for transfers between devices  26.5 us (20%)
  local copies, waits for them, and re-layouts  5.41 us (4%)
  other arithmetic  4.05 us (3%)
    pallas_call x2, Pallas kernels, frozen_rows(): pl.pallas_call(lambda *refs: frozen_kernel(n, early, *refs), out_shape=ja...  17.4 us
    pallas_call x2, Pallas kernels, early_rows(): pl.pallas_call(lambda *refs: early_kernel(n, *refs), out_shape=jax.ShapeD...  16 us
    all_to_all x2, waiting for transfers between devices, z_exchange(): lax.all_to_all(v, 'mp', 0, 0, tiled=True, axis_index_groups=same_core)  15.5 us
    ppermute x10, starting transfers between devices, swap(): return lax.ppermute(v, 'mp', [(i, i ^ 1) for i in range(mp)])  12.8 us
    ppermute x4, starting transfers between devices, ring_a(): return lax.ppermute(v, 'mp', ring_step(1, ring))  12.3 us
    ppermute x6, starting transfers between devices, y_exchange(): lax.ppermute(v, 'dp', y_step(shift))  10.2 us
    pallas_call x8, Pallas kernels, local_call(): pl.pallas_call(kernel, out_shape=tuple(out_shapes), in_specs=[pl.BlockSpe...  8.95 us
    ppermute x6, starting transfers between devices, x_exchange(): return [v] + [lax.ppermute(v, 'dp', x_step(shift)) for shift in SHIFTS[1:]]  8.31 us
  transfers between devices with their start and end apart: 31, of which 9 were waited for; matrix products, arithmetic and copies ran while one was open for 4% of the time, Pallas kernels for 32%

profile of v3, /device:TPU:1, one launch (start us, length us, event | category | flops | bytes accessed | tf_op | source)
XLA Modules:
  0.0 131.6 jit_solution(14387611370014668485)
XLA Ops:
  0.6 6.5 %collective-permute-start.7 = (bf16[64,8192]{1,0:T(8,128)(2,1)}, bf16[64,8192]{1,0:T(8,128)(2,1)}, u32[]{:S(2)}, u32[]{:S(2)}) collective-permute-start(bf16[64,8192]{1,0:T(8,128)(2,1)} %own.1), channel_id=1, source_target_pairs={{0,2},{1,15},{2,4},{3,1},{4,6},{5,3},{6,8},{7,5},{8,10},{9,7},{10,... | collective-permute-start | bytes 3145736 | tf_op jit(solution)/shard_map/ppermute | solution.py:337
  8.0 1.3 collective-permute-start
  9.3 1.5 %collective-permute-start.1 = (bf16[4,16,1024]{2,1,0:T(8,128)(2,1)S(1)}, bf16[4,16,1024]{2,1,0:T(8,128)(2,1)S(1)}, u32[]{:S(2)}, u32[]{:S(2)}) collective-permute-start(bf16[4,16,1024]{2,1,0:T(8,128)(2,1)S(1)} %pad_maximum_fusion.refs_0_), channel_id=1, source_target_pairs={{0,48},{16,0},{32,16},{48,32},{64,112},{80,64},{96,80},{112,96},{1... | collective-permute-start | bytes 393224 | tf_op jit(solution)/shard_map/ppermute | solution.py:348
  10.8 1.5 %collective-permute-start.2 = (bf16[4,16,1024]{2,1,0:T(8,128)(2,1)S(1)}, bf16[4,16,1024]{2,1,0:T(8,128)(2,1)S(1)}, u32[]{:S(2)}, u32[]{:S(2)}) collective-permute-start(bf16[4,16,1024]{2,1,0:T(8,128)(2,1)S(1)} %pad_maximum_fusion.refs_0_), channel_id=1, source_target_pairs={{0,32},{16,48},{32,0},{48,16},{64,96},{80,112},{96,64},{112,80},{1... | collective-permute-start | bytes 393224 | tf_op jit(solution)/shard_map/ppermute | solution.py:348
  13.5 4.0 %collective-permute-done.2.refs_3_ = bf16[4,16,1024]{2,1,0:T(8,128)(2,1)S(1)} collective-permute-done((bf16[4,16,1024]{2,1,0:T(8,128)(2,1)S(1)}, bf16[4,16,1024]{2,1,0:T(8,128)(2,1)S(1)}, u32[]{:S(2)}, u32[]{:S(2)}) %collective-permute-start.2) | collective-permute-done | bytes 131104 | tf_op jit(solution)/shard_map/ppermute | solution.py:348
  18.6 1.4 %collective-permute-start.3 = (bf16[8,16,1024]{2,1,0:T(8,128)(2,1)S(1)}, bf16[8,16,1024]{2,1,0:T(8,128)(2,1)S(1)}, u32[]{:S(2)}, u32[]{:S(2)}) collective-permute-start(bf16[8,16,1024]{2,1,0:T(8,128)(2,1)S(1)} %get-tuple-element.40), channel_id=1, source_target_pairs={{0,64},{16,80},{32,96},{48,112},{64,128},{80,144},{96,160},{112,17... | collective-permute-start | bytes 786440 | tf_op jit(solution)/shard_map/ppermute | solution.py:352
  20.0 1.9 %collective-permute-start.6 = (bf16[64,8192]{1,0:T(8,128)(2,1)}, bf16[64,8192]{1,0:T(8,128)(2,1)}, u32[]{:S(2)}, u32[]{:S(2)}) collective-permute-start(bf16[64,8192]{1,0:T(8,128)(2,1)} %own.1), channel_id=1, source_target_pairs={{0,1},{1,0},{2,3},{3,2},{4,5},{5,4},{6,7},{7,6},{8,9},{9,8},{10,11... | collective-permute-start | bytes 3145736 | tf_op jit(solution)/shard_map/ppermute | solution.py:343
  21.9 1.4 %collective-permute-start.4 = (bf16[8,16,1024]{2,1,0:T(8,128)(2,1)S(1)}, bf16[8,16,1024]{2,1,0:T(8,128)(2,1)S(1)}, u32[]{:S(2)}, u32[]{:S(2)}) collective-permute-start(bf16[8,16,1024]{2,1,0:T(8,128)(2,1)S(1)} %get-tuple-element.41), channel_id=1, source_target_pairs={{0,192},{16,208},{32,224},{48,240},{64,0},{80,16},{96,32},{112,48}... | collective-permute-start | bytes 786440 | tf_op jit(solution)/shard_map/ppermute | solution.py:352
  23.3 3.1 %collective-permute-done.3.refs_1_ = bf16[8,16,1024]{2,1,0:T(8,128)(2,1)S(1)} collective-permute-done((bf16[8,16,1024]{2,1,0:T(8,128)(2,1)S(1)}, bf16[8,16,1024]{2,1,0:T(8,128)(2,1)S(1)}, u32[]{:S(2)}, u32[]{:S(2)}) %collective-permute-start.3) | collective-permute-done | bytes 262176 | tf_op jit(solution)/shard_map/ppermute | solution.py:352
  26.4 1.6 %collective-permute-start.5 = (bf16[8,16,1024]{2,1,0:T(8,128)(2,1)S(1)}, bf16[8,16,1024]{2,1,0:T(8,128)(2,1)S(1)}, u32[]{:S(2)}, u32[]{:S(2)}) collective-permute-start(bf16[8,16,1024]{2,1,0:T(8,128)(2,1)S(1)} %get-tuple-element.42), channel_id=1, source_target_pairs={{0,128},{16,144},{32,160},{48,176},{64,192},{80,208},{96,224},{112... | collective-permute-start | bytes 786440 | tf_op jit(solution)/shard_map/ppermute | solution.py:352
  27.9 1.2 collective-permute-done.7.refs_2_
  29.2 1.5 %collective-permute-start.10 = (bf16[64,8192]{1,0:T(8,128)(2,1)}, bf16[64,8192]{1,0:T(8,128)(2,1)}, u32[]{:S(2)}, u32[]{:S(2)}) collective-permute-start(bf16[64,8192]{1,0:T(8,128)(2,1)} %collective-permute-done.7.refs_2_), channel_id=1, source_target_pairs={{0,1},{1,0},{2,3},{3,2},{4,5},{5,4},{6,7},{7,6},{8,9},{9,8},{10,11... | collective-permute-start | bytes 3145736 | tf_op jit(solution)/shard_map/ppermute | solution.py:343
  32.4 2.5 %collective-permute-start.11 = (bf16[64,8192]{1,0:T(8,128)(2,1)}, bf16[64,8192]{1,0:T(8,128)(2,1)}, u32[]{:S(2)}, u32[]{:S(2)}) collective-permute-start(bf16[64,8192]{1,0:T(8,128)(2,1)} %collective-permute-done.7.refs_2_), channel_id=1, source_target_pairs={{0,2},{1,15},{2,4},{3,1},{4,6},{5,3},{6,8},{7,5},{8,10},{9,7},{10,... | collective-permute-start | bytes 3145736 | tf_op jit(solution)/shard_map/ppermute | solution.py:337
  36.7 1.2 copy-done.2
  38.5 6.2 %collective-permute-start.13 = (bf16[64,4096]{1,0:T(8,128)(2,1)S(1)}, bf16[64,4096]{1,0:T(8,128)(2,1)S(1)}, u32[]{:S(2)}, u32[]{:S(2)}) collective-permute-start(bf16[64,4096]{1,0:T(8,128)(2,1)S(1)} %get-tuple-element.45), channel_id=1, source_target_pairs={{0,1},{1,0},{2,3},{3,2},{4,5},{5,4},{6,7},{7,6},{8,9},{9,8},{10,11... | collective-permute-start | bytes 1572872 | tf_op jit(solution)/shard_map/ppermute | solution.py:343
  44.7 1.2 copy-done
  47.7 3.4 %all-to-all-start = ((bf16[8,16,768]{2,1,0:T(8,128)(2,1)}), bf16[8,16,768]{2,1,0:T(8,128)(2,1)S(1)}, u32[]{:S(2)}, u32[]{:S(2)}) async-start(bf16[8,16,768]{2,1,0:T(8,128)(2,1)} %get-tuple-element.43), calls=%async_computation | async-start | bytes 393216 | tf_op jit(solution)/shard_map/all_to_all | solution.py:355
  51.1 8.6 %shard_map.105.refs_9_ = f32[384,512]{1,0:T(8,128)} custom-call(bf16[64,8192]{1,0:T(8,128)(2,1)} %own.1, bf16[64,8192]{1,0:T(8,128)(2,1)} %collective-permute-done.6.refs_1_, bf16[64,8192]{1,0:T(8,128)(2,1)} %collective-permute-done.7.refs_2_, bf16[64,8192]{1,0:T(8,128)(2,1)} %collective-permute-done.9.refs_3_, ...), custom_call_target="tpu_custom_call" | custom-call | flops 3221225472 | bytes 14680064 | tf_op jit(solution)/shard_map/pallas_call | solution.py:201
  59.8 4.5 %all-to-all-done.at_rows = bf16[8,16,768]{2,1,0:T(8,128)(2,1)S(1)} async-done(((bf16[8,16,768]{2,1,0:T(8,128)(2,1)}), bf16[8,16,768]{2,1,0:T(8,128)(2,1)S(1)}, u32[]{:S(2)}, u32[]{:S(2)}) %all-to-all-start) | async-done | bytes 196640 | tf_op jit(solution)/shard_map/all_to_all | solution.py:355
  67.5 1.6 %collective-permute-start.14 = (f32[32,128]{1,0:T(8,128)S(1)}, f32[32,128]{1,0:T(8,128)S(1)}, u32[]{:S(2)}, u32[]{:S(2)}) collective-permute-start(f32[32,128]{1,0:T(8,128)S(1)} %shard_map.107.sums), channel_id=1, source_target_pairs={{0,1},{1,0},{2,3},{3,2},{4,5},{5,4},{6,7},{7,6},{8,9},{9,8},{10,11... | collective-permute-start | bytes 49160 | tf_op jit(solution)/shard_map/ppermute | solution.py:343
  69.9 1.6 %shard_map.108 = bf16[8,16,640]{2,1,0:T(8,128)(2,1)} custom-call(s32[4]{0:T(128)S(1)} %pad_add_fusion.at_ref, f32[32,128]{1,0:T(8,128)S(1)} %shard_map.107.sums, f32[32,128]{1,0:T(8,128)S(1)} %collective-permute-done.14.more, bf16[64,4096]{1,0:T(8,128)(2,1)S(1)} %get-tuple-element.47.mine, bf16[64,4096]{1,0:T(8,128)(2,1)S(1)} %collective-permute-done.13.other), custom_call_target="tpu_custom_call" | custom-call | bytes 1245184 | tf_op jit(solution)/shard_map/pallas_call | solution.py:46
  71.5 4.7 %all-to-all-start.1 = ((bf16[8,16,640]{2,1,0:T(8,128)(2,1)}), bf16[8,16,640]{2,1,0:T(8,128)(2,1)S(1)}, u32[]{:S(2)}, u32[]{:S(2)}) async-start(bf16[8,16,640]{2,1,0:T(8,128)(2,1)} %shard_map.108), calls=%async_computation.1 | async-start | bytes 327680 | tf_op jit(solution)/shard_map/all_to_all | solution.py:355
  77.1 7.4 %shard_map.109.refs_10_ = f32[256,512]{1,0:T(8,128)} custom-call(bf16[64,8192]{1,0:T(8,128)(2,1)} %collective-permute-done.11.refs_0_, bf16[64,8192]{1,0:T(8,128)(2,1)} %copy-done.7, bf16[64,8192]{1,0:T(8,128)(2,1)} %collective-permute-done.12.refs_2_, bf16[64,8192]{1,0:T(8,128)(2,1)} %collective-permute-done.16.refs_3_, bf16[512,8192]{1,0:T(8,128)(2,1)} %refs_4_.5), custom_call_target="tpu_custom_call" | custom-call | flops 2147483648 | bytes 12582912 | tf_op jit(solution)/shard_map/pallas_call | solution.py:201
  84.5 11.0 %all-to-all-done.1.at_columns.refs_7_.refs_5_ = bf16[8,16,640]{2,1,0:T(8,128)(2,1)S(1)} async-done(((bf16[8,16,640]{2,1,0:T(8,128)(2,1)}), bf16[8,16,640]{2,1,0:T(8,128)(2,1)S(1)}, u32[]{:S(2)}, u32[]{:S(2)}) %all-to-all-start.1) | async-done | bytes 163872 | tf_op jit(solution)/shard_map/all_to_all | solution.py:355
  96.6 2.3 %collective-permute-start.24 = (bf16[64,8192]{1,0:T(8,128)(2,1)}, bf16[64,8192]{1,0:T(8,128)(2,1)S(1)}, u32[]{:S(2)}, u32[]{:S(2)}) collective-permute-start(bf16[64,8192]{1,0:T(8,128)(2,1)} %collective-permute-done.17.refs_2_), channel_id=1, source_target_pairs={{0,2},{1,15},{2,4},{3,1},{4,6},{5,3},{6,8},{7,5},{8,10},{9,7},{10,... | collective-permute-start | bytes 3145736 | tf_op jit(solution)/shard_map/ppermute | solution.py:337
  100.2 1.7 %collective-permute-start.20 = (bf16[8,16,1024]{2,1,0:T(8,128)(2,1)S(1)}, bf16[8,16,1024]{2,1,0:T(8,128)(2,1)S(1)}, u32[]{:S(2)}, u32[]{:S(2)}) collective-permute-start(bf16[8,16,1024]{2,1,0:T(8,128)(2,1)S(1)} %shard_map.110.refs_0_), channel_id=1, source_target_pairs={{0,48},{16,0},{32,16},{48,32},{64,112},{80,64},{96,80},{112,96},{1... | collective-permute-start | bytes 786440 | tf_op jit(solution)/shard_map/ppermute | solution.py:348
  102.0 1.3 collective-permute-start.21
  103.9 9.4 %shard_map.111.refs_7_ = bf16[1024,512]{1,0:T(8,128)(2,1)} custom-call(s32[14]{0:T(128)} %stack.88.refs_0_, s32[8]{0:T(128)} %copy-done.5, bf16[64,8192]{1,0:T(8,128)(2,1)} %collective-permute-done.17.refs_2_, bf16[64,8192]{1,0:T(8,128)(2,1)} %collective-permute-done.22.refs_3_, bf16[64,8192]{1,0:T(8,128)(2,1)} %collective-permute-done.18.refs_4_, ...), custom_call_target="tpu_custom_call" | custom-call | flops 2147483648 | bytes 12582912 | tf_op jit(solution)/shard_map/pallas_call | solution.py:288
  113.8 2.5 %shard_map.112 = (bf16[4,16,1024]{2,1,0:T(8,128)(2,1)S(1)}, bf16[4,16,1024]{2,1,0:T(8,128)(2,1)S(1)}, bf16[4,16,1024]{2,1,0:T(8,128)(2,1)S(1)}, bf16[4,16,1024]{2,1,0:T(8,128)(2,1)S(1)}, f32[16,16,1024]{2,1,0:T(8,128)}) custom-call(s32[4]{0:T(128)S(1)} %pad_add_fusion.at_ref, s32[128]{0:T(128)S(1)} %select_reduce_fusion.slot_ref, ...), custom_call_target="tpu_custom_call" | custom-call | bytes 2621440 | tf_op jit(solution)/shard_map/pallas_call | solution.py:46
  116.3 2.4 %collective-permute-start.25 = (bf16[4,16,1024]{2,1,0:T(8,128)(2,1)S(1)}, bf16[4,16,1024]{2,1,0:T(8,128)(2,1)S(1)}, u32[]{:S(2)}, u32[]{:S(2)}) collective-permute-start(bf16[4,16,1024]{2,1,0:T(8,128)(2,1)S(1)} %get-tuple-element.63), channel_id=1, source_target_pairs={{0,64},{16,80},{32,96},{48,112},{64,128},{80,144},{96,160},{112,17... | collective-permute-start | bytes 393224 | tf_op jit(solution)/shard_map/ppermute | solution.py:352
  118.7 2.2 %collective-permute-start.26 = (bf16[4,16,1024]{2,1,0:T(8,128)(2,1)S(1)}, bf16[4,16,1024]{2,1,0:T(8,128)(2,1)S(1)}, u32[]{:S(2)}, u32[]{:S(2)}) collective-permute-start(bf16[4,16,1024]{2,1,0:T(8,128)(2,1)S(1)} %get-tuple-element.64), channel_id=1, source_target_pairs={{0,192},{16,208},{32,224},{48,240},{64,0},{80,16},{96,32},{112,48}... | collective-permute-start | bytes 393224 | tf_op jit(solution)/shard_map/ppermute | solution.py:352
  122.8 8.0 %shard_map.113 = bf16[1024,512]{1,0:T(8,128)(2,1)} custom-call(s32[2]{0:T(128)} %pad_add_fusion.1.refs_0_, s32[8]{0:T(128)} %copy-done.5, bf16[64,8192]{1,0:T(8,128)(2,1)} %copy-done.6, bf16[64,8192]{1,0:T(8,128)(2,1)} %collective-permute-done.28.refs_3_, bf16[512,8192]{1,0:T(8,128)(2,1)} %refs_4_.5, ...), custom_call_target="tpu_custom_call", output_to_operand_aliasing={{}: (7, {})} | custom-call | flops 1073741824 | bytes 10485760 | tf_op jit(solution)/shard_map/pallas_call | solution.py:288
  (68 shorter events, 20.1 us)
Async XLA Ops:
  0.6 28.5 %collective-permute-start.7 = (bf16[64,8192]{1,0:T(8,128)(2,1)}, bf16[64,8192]{1,0:T(8,128)(2,1)}, u32[]{:S(2)}, u32[]{:S(2)}) collective-permute-start(bf16[64,8192]{1,0:T(8,128)(2,1)} %own.1), channel_id=1, source_target_pairs={{0,2},{1,15},{2,4},{3,1},{4,6},{5,3},{6,8},{7,5},{8,10},{9,7},{10,... | collective-permute-start | bytes 3145736 | tf_op jit(solution)/shard_map/ppermute | solution.py:337
  7.1 24.6 %collective-permute-start.8 = (bf16[64,8192]{1,0:T(8,128)(2,1)}, bf16[64,8192]{1,0:T(8,128)(2,1)}, u32[]{:S(2)}, u32[]{:S(2)}) collective-permute-start(bf16[64,8192]{1,0:T(8,128)(2,1)} %own.1), channel_id=1, source_target_pairs={{0,14},{1,3},{2,0},{3,5},{4,2},{5,7},{6,4},{7,9},{8,6},{9,11},{10,... | collective-permute-start | bytes 3145736 | tf_op jit(solution)/shard_map/ppermute | solution.py:340
  8.0 5.5 %collective-permute-start = (bf16[4,16,1024]{2,1,0:T(8,128)(2,1)S(1)}, bf16[4,16,1024]{2,1,0:T(8,128)(2,1)S(1)}, u32[]{:S(2)}, u32[]{:S(2)}) collective-permute-start(bf16[4,16,1024]{2,1,0:T(8,128)(2,1)S(1)} %pad_maximum_fusion.refs_0_), channel_id=1, source_target_pairs={{0,16},{16,32},{32,48},{48,0},{64,80},{80,96},{96,112},{112,64},{1... | collective-permute-start | bytes 393224 | tf_op jit(solution)/shard_map/ppermute | solution.py:348
  9.3 4.2 %collective-permute-start.1 = (bf16[4,16,1024]{2,1,0:T(8,128)(2,1)S(1)}, bf16[4,16,1024]{2,1,0:T(8,128)(2,1)S(1)}, u32[]{:S(2)}, u32[]{:S(2)}) collective-permute-start(bf16[4,16,1024]{2,1,0:T(8,128)(2,1)S(1)} %pad_maximum_fusion.refs_0_), channel_id=1, source_target_pairs={{0,48},{16,0},{32,16},{48,32},{64,112},{80,64},{96,80},{112,96},{1... | collective-permute-start | bytes 393224 | tf_op jit(solution)/shard_map/ppermute | solution.py:348
  10.8 6.7 %collective-permute-start.2 = (bf16[4,16,1024]{2,1,0:T(8,128)(2,1)S(1)}, bf16[4,16,1024]{2,1,0:T(8,128)(2,1)S(1)}, u32[]{:S(2)}, u32[]{:S(2)}) collective-permute-start(bf16[4,16,1024]{2,1,0:T(8,128)(2,1)S(1)} %pad_maximum_fusion.refs_0_), channel_id=1, source_target_pairs={{0,32},{16,48},{32,0},{48,16},{64,96},{80,112},{96,64},{112,80},{1... | collective-permute-start | bytes 393224 | tf_op jit(solution)/shard_map/ppermute | solution.py:348
  18.6 7.7 %collective-permute-start.3 = (bf16[8,16,1024]{2,1,0:T(8,128)(2,1)S(1)}, bf16[8,16,1024]{2,1,0:T(8,128)(2,1)S(1)}, u32[]{:S(2)}, u32[]{:S(2)}) collective-permute-start(bf16[8,16,1024]{2,1,0:T(8,128)(2,1)S(1)} %get-tuple-element.40), channel_id=1, source_target_pairs={{0,64},{16,80},{32,96},{48,112},{64,128},{80,144},{96,160},{112,17... | collective-permute-start | bytes 786440 | tf_op jit(solution)/shard_map/ppermute | solution.py:352
  20.0 18.5 %collective-permute-start.6 = (bf16[64,8192]{1,0:T(8,128)(2,1)}, bf16[64,8192]{1,0:T(8,128)(2,1)}, u32[]{:S(2)}, u32[]{:S(2)}) collective-permute-start(bf16[64,8192]{1,0:T(8,128)(2,1)} %own.1), channel_id=1, source_target_pairs={{0,1},{1,0},{2,3},{3,2},{4,5},{5,4},{6,7},{7,6},{8,9},{9,8},{10,11... | collective-permute-start | bytes 3145736 | tf_op jit(solution)/shard_map/ppermute | solution.py:343
  21.9 10.5 %collective-permute-start.4 = (bf16[8,16,1024]{2,1,0:T(8,128)(2,1)S(1)}, bf16[8,16,1024]{2,1,0:T(8,128)(2,1)S(1)}, u32[]{:S(2)}, u32[]{:S(2)}) collective-permute-start(bf16[8,16,1024]{2,1,0:T(8,128)(2,1)S(1)} %get-tuple-element.41), channel_id=1, source_target_pairs={{0,192},{16,208},{32,224},{48,240},{64,0},{80,16},{96,32},{112,48}... | collective-permute-start | bytes 786440 | tf_op jit(solution)/shard_map/ppermute | solution.py:352
  26.4 8.6 %collective-permute-start.5 = (bf16[8,16,1024]{2,1,0:T(8,128)(2,1)S(1)}, bf16[8,16,1024]{2,1,0:T(8,128)(2,1)S(1)}, u32[]{:S(2)}, u32[]{:S(2)}) collective-permute-start(bf16[8,16,1024]{2,1,0:T(8,128)(2,1)S(1)} %get-tuple-element.42), channel_id=1, source_target_pairs={{0,128},{16,144},{32,160},{48,176},{64,192},{80,208},{96,224},{112... | collective-permute-start | bytes 786440 | tf_op jit(solution)/shard_map/ppermute | solution.py:352
  29.2 21.9 %collective-permute-start.10 = (bf16[64,8192]{1,0:T(8,128)(2,1)}, bf16[64,8192]{1,0:T(8,128)(2,1)}, u32[]{:S(2)}, u32[]{:S(2)}) collective-permute-start(bf16[64,8192]{1,0:T(8,128)(2,1)} %collective-permute-done.7.refs_2_), channel_id=1, source_target_pairs={{0,1},{1,0},{2,3},{3,2},{4,5},{5,4},{6,7},{7,6},{8,9},{9,8},{10,11... | collective-permute-start | bytes 3145736 | tf_op jit(solution)/shard_map/ppermute | solution.py:343
  31.7 19.4 %collective-permute-start.9 = (bf16[64,8192]{1,0:T(8,128)(2,1)}, bf16[64,8192]{1,0:T(8,128)(2,1)}, u32[]{:S(2)}, u32[]{:S(2)}) collective-permute-start(bf16[64,8192]{1,0:T(8,128)(2,1)} %collective-permute-done.8.refs_4_), channel_id=1, source_target_pairs={{0,1},{1,0},{2,3},{3,2},{4,5},{5,4},{6,7},{7,6},{8,9},{9,8},{10,11... | collective-permute-start | bytes 3145736 | tf_op jit(solution)/shard_map/ppermute | solution.py:343
  32.4 31.8 %collective-permute-start.11 = (bf16[64,8192]{1,0:T(8,128)(2,1)}, bf16[64,8192]{1,0:T(8,128)(2,1)}, u32[]{:S(2)}, u32[]{:S(2)}) collective-permute-start(bf16[64,8192]{1,0:T(8,128)(2,1)} %collective-permute-done.7.refs_2_), channel_id=1, source_target_pairs={{0,2},{1,15},{2,4},{3,1},{4,6},{5,3},{6,8},{7,5},{8,10},{9,7},{10,... | collective-permute-start | bytes 3145736 | tf_op jit(solution)/shard_map/ppermute | solution.py:337
  35.0 29.3 %collective-permute-start.12 = (bf16[64,8192]{1,0:T(8,128)(2,1)}, bf16[64,8192]{1,0:T(8,128)(2,1)}, u32[]{:S(2)}, u32[]{:S(2)}) collective-permute-start(bf16[64,8192]{1,0:T(8,128)(2,1)} %collective-permute-done.8.refs_4_), channel_id=1, source_target_pairs={{0,14},{1,3},{2,0},{3,5},{4,2},{5,7},{6,4},{7,9},{8,6},{9,11},{10,... | collective-permute-start | bytes 3145736 | tf_op jit(solution)/shard_map/ppermute | solution.py:340
  38.5 21.2 %collective-permute-start.13 = (bf16[64,4096]{1,0:T(8,128)(2,1)S(1)}, bf16[64,4096]{1,0:T(8,128)(2,1)S(1)}, u32[]{:S(2)}, u32[]{:S(2)}) collective-permute-start(bf16[64,4096]{1,0:T(8,128)(2,1)S(1)} %get-tuple-element.45), channel_id=1, source_target_pairs={{0,1},{1,0},{2,3},{3,2},{4,5},{5,4},{6,7},{7,6},{8,9},{9,8},{10,11... | collective-permute-start | bytes 1572872 | tf_op jit(solution)/shard_map/ppermute | solution.py:343
  47.7 16.6 %all-to-all-start = ((bf16[8,16,768]{2,1,0:T(8,128)(2,1)}), bf16[8,16,768]{2,1,0:T(8,128)(2,1)S(1)}, u32[]{:S(2)}, u32[]{:S(2)}) async-start(bf16[8,16,768]{2,1,0:T(8,128)(2,1)} %get-tuple-element.43), calls=%async_computation | async-start | bytes 393216 | tf_op jit(solution)/shard_map/all_to_all | solution.py:355
  59.7 39.2 %copy-start.1 = (bf16[1024,512]{1,0:T(8,128)(2,1)S(1)}, bf16[1024,512]{1,0:T(8,128)(2,1)}, u32[]{:S(2)}) copy-start(bf16[1024,512]{1,0:T(8,128)(2,1)} %acts.1) | copy-start | bytes 3145732
  64.2 11.9 %collective-permute-start.15 = (bf16[64,8192]{1,0:T(8,128)(2,1)}, bf16[64,8192]{1,0:T(8,128)(2,1)S(1)}, u32[]{:S(2)}, u32[]{:S(2)}) collective-permute-start(bf16[64,8192]{1,0:T(8,128)(2,1)} %collective-permute-done.12.refs_2_), channel_id=1, source_target_pairs={{0,1},{1,0},{2,3},{3,2},{4,5},{5,4},{6,7},{7,6},{8,9},{9,8},{10,11... | collective-permute-start | bytes 3145736 | tf_op jit(solution)/shard_map/ppermute | solution.py:343
  64.2 11.9 %collective-permute-start.16 = (bf16[64,8192]{1,0:T(8,128)(2,1)}, bf16[64,8192]{1,0:T(8,128)(2,1)}, u32[]{:S(2)}, u32[]{:S(2)}) collective-permute-start(bf16[64,8192]{1,0:T(8,128)(2,1)} %collective-permute-done.11.refs_0_), channel_id=1, source_target_pairs={{0,1},{1,0},{2,3},{3,2},{4,5},{5,4},{6,7},{7,6},{8,9},{9,8},{10,11... | collective-permute-start | bytes 3145736 | tf_op jit(solution)/shard_map/ppermute | solution.py:343
  64.7 30.8 %collective-permute-start.17 = (bf16[64,8192]{1,0:T(8,128)(2,1)}, bf16[64,8192]{1,0:T(8,128)(2,1)}, u32[]{:S(2)}, u32[]{:S(2)}) collective-permute-start(bf16[64,8192]{1,0:T(8,128)(2,1)} %collective-permute-done.11.refs_0_), channel_id=1, source_target_pairs={{0,2},{1,15},{2,4},{3,1},{4,6},{5,3},{6,8},{7,5},{8,10},{9,7},{10,... | collective-permute-start | bytes 3145736 | tf_op jit(solution)/shard_map/ppermute | solution.py:337
  65.7 29.8 %collective-permute-start.18 = (bf16[64,8192]{1,0:T(8,128)(2,1)}, bf16[64,8192]{1,0:T(8,128)(2,1)}, u32[]{:S(2)}, u32[]{:S(2)}) collective-permute-start(bf16[64,8192]{1,0:T(8,128)(2,1)} %collective-permute-done.12.refs_2_), channel_id=1, source_target_pairs={{0,14},{1,3},{2,0},{3,5},{4,2},{5,7},{6,4},{7,9},{8,6},{9,11},{10,... | collective-permute-start | bytes 3145736 | tf_op jit(solution)/shard_map/ppermute | solution.py:340
  67.5 2.4 %collective-permute-start.14 = (f32[32,128]{1,0:T(8,128)S(1)}, f32[32,128]{1,0:T(8,128)S(1)}, u32[]{:S(2)}, u32[]{:S(2)}) collective-permute-start(f32[32,128]{1,0:T(8,128)S(1)} %shard_map.107.sums), channel_id=1, source_target_pairs={{0,1},{1,0},{2,3},{3,2},{4,5},{5,4},{6,7},{7,6},{8,9},{9,8},{10,11... | collective-permute-start | bytes 49160 | tf_op jit(solution)/shard_map/ppermute | solution.py:343
  71.5 24.0 %all-to-all-start.1 = ((bf16[8,16,640]{2,1,0:T(8,128)(2,1)}), bf16[8,16,640]{2,1,0:T(8,128)(2,1)S(1)}, u32[]{:S(2)}, u32[]{:S(2)}) async-start(bf16[8,16,640]{2,1,0:T(8,128)(2,1)} %shard_map.108), calls=%async_computation.1 | async-start | bytes 327680 | tf_op jit(solution)/shard_map/all_to_all | solution.py:355
  95.5 6.5 %collective-permute-start.22 = (bf16[64,8192]{1,0:T(8,128)(2,1)}, bf16[64,8192]{1,0:T(8,128)(2,1)}, u32[]{:S(2)}, u32[]{:S(2)}) collective-permute-start(bf16[64,8192]{1,0:T(8,128)(2,1)} %collective-permute-done.18.refs_4_), channel_id=1, source_target_pairs={{0,1},{1,0},{2,3},{3,2},{4,5},{5,4},{6,7},{7,6},{8,9},{9,8},{10,11... | collective-permute-start | bytes 3145736 | tf_op jit(solution)/shard_map/ppermute | solution.py:343
  96.5 7.3 %collective-permute-start.23 = (bf16[64,8192]{1,0:T(8,128)(2,1)}, bf16[64,8192]{1,0:T(8,128)(2,1)}, u32[]{:S(2)}, u32[]{:S(2)}) collective-permute-start(bf16[64,8192]{1,0:T(8,128)(2,1)} %collective-permute-done.17.refs_2_), channel_id=1, source_target_pairs={{0,1},{1,0},{2,3},{3,2},{4,5},{5,4},{6,7},{7,6},{8,9},{9,8},{10,11... | collective-permute-start | bytes 3145736 | tf_op jit(solution)/shard_map/ppermute | solution.py:343
  96.6 17.1 %collective-permute-start.24 = (bf16[64,8192]{1,0:T(8,128)(2,1)}, bf16[64,8192]{1,0:T(8,128)(2,1)S(1)}, u32[]{:S(2)}, u32[]{:S(2)}) collective-permute-start(bf16[64,8192]{1,0:T(8,128)(2,1)} %collective-permute-done.17.refs_2_), channel_id=1, source_target_pairs={{0,2},{1,15},{2,4},{3,1},{4,6},{5,3},{6,8},{7,5},{8,10},{9,7},{10,... | collective-permute-start | bytes 3145736 | tf_op jit(solution)/shard_map/ppermute | solution.py:337
  99.2 14.1 %collective-permute-start.19 = (bf16[8,16,1024]{2,1,0:T(8,128)(2,1)S(1)}, bf16[8,16,1024]{2,1,0:T(8,128)(2,1)S(1)}, u32[]{:S(2)}, u32[]{:S(2)}) collective-permute-start(bf16[8,16,1024]{2,1,0:T(8,128)(2,1)S(1)} %shard_map.110.refs_0_), channel_id=1, source_target_pairs={{0,16},{16,32},{32,48},{48,0},{64,80},{80,96},{96,112},{112,64},{1... | collective-permute-start | bytes 786440 | tf_op jit(solution)/shard_map/ppermute | solution.py:348
  100.2 13.1 %collective-permute-start.20 = (bf16[8,16,1024]{2,1,0:T(8,128)(2,1)S(1)}, bf16[8,16,1024]{2,1,0:T(8,128)(2,1)S(1)}, u32[]{:S(2)}, u32[]{:S(2)}) collective-permute-start(bf16[8,16,1024]{2,1,0:T(8,128)(2,1)S(1)} %shard_map.110.refs_0_), channel_id=1, source_target_pairs={{0,48},{16,0},{32,16},{48,32},{64,112},{80,64},{96,80},{112,96},{1... | collective-permute-start | bytes 786440 | tf_op jit(solution)/shard_map/ppermute | solution.py:348
  102.0 11.8 %collective-permute-start.21 = (bf16[8,16,1024]{2,1,0:T(8,128)(2,1)S(1)}, bf16[8,16,1024]{2,1,0:T(8,128)(2,1)S(1)}, u32[]{:S(2)}, u32[]{:S(2)}) collective-permute-start(bf16[8,16,1024]{2,1,0:T(8,128)(2,1)S(1)} %shard_map.110.refs_0_), channel_id=1, source_target_pairs={{0,32},{16,48},{32,0},{48,16},{64,96},{80,112},{96,64},{112,80},{1... | collective-permute-start | bytes 786440 | tf_op jit(solution)/shard_map/ppermute | solution.py:348
  113.7 9.1 %collective-permute-start.28 = (bf16[64,8192]{1,0:T(8,128)(2,1)S(1)}, bf16[64,8192]{1,0:T(8,128)(2,1)}, u32[]{:S(2)}, u32[]{:S(2)}) collective-permute-start(bf16[64,8192]{1,0:T(8,128)(2,1)S(1)} %collective-permute-done.24.refs_2_), channel_id=1, source_target_pairs={{0,1},{1,0},{2,3},{3,2},{4,5},{5,4},{6,7},{7,6},{8,9},{9,8},{10,11... | collective-permute-start | bytes 3145736 | tf_op jit(solution)/shard_map/ppermute | solution.py:343
  116.3 14.5 %collective-permute-start.25 = (bf16[4,16,1024]{2,1,0:T(8,128)(2,1)S(1)}, bf16[4,16,1024]{2,1,0:T(8,128)(2,1)S(1)}, u32[]{:S(2)}, u32[]{:S(2)}) collective-permute-start(bf16[4,16,1024]{2,1,0:T(8,128)(2,1)S(1)} %get-tuple-element.63), channel_id=1, source_target_pairs={{0,64},{16,80},{32,96},{48,112},{64,128},{80,144},{96,160},{112,17... | collective-permute-start | bytes 393224 | tf_op jit(solution)/shard_map/ppermute | solution.py:352
  118.7 12.0 %collective-permute-start.26 = (bf16[4,16,1024]{2,1,0:T(8,128)(2,1)S(1)}, bf16[4,16,1024]{2,1,0:T(8,128)(2,1)S(1)}, u32[]{:S(2)}, u32[]{:S(2)}) collective-permute-start(bf16[4,16,1024]{2,1,0:T(8,128)(2,1)S(1)} %get-tuple-element.64), channel_id=1, source_target_pairs={{0,192},{16,208},{32,224},{48,240},{64,0},{80,16},{96,32},{112,48}... | collective-permute-start | bytes 393224 | tf_op jit(solution)/shard_map/ppermute | solution.py:352
  121.0 9.8 %collective-permute-start.27 = (bf16[4,16,1024]{2,1,0:T(8,128)(2,1)S(1)}, bf16[4,16,1024]{2,1,0:T(8,128)(2,1)S(1)}, u32[]{:S(2)}, u32[]{:S(2)}) collective-permute-start(bf16[4,16,1024]{2,1,0:T(8,128)(2,1)S(1)} %get-tuple-element.65), channel_id=1, source_target_pairs={{0,128},{16,144},{32,160},{48,176},{64,192},{80,208},{96,224},{112... | collective-permute-start | bytes 393224 | tf_op jit(solution)/shard_map/ppermute | solution.py:352
  (7 other events, 43.4 us)

commit v4 on v3

--- a/solution.py
+++ b/solution.py
@@ -40,7 +40,7 @@
     return lax.dot_general(a, b, (dims, ((), ())), preferred_element_type=jnp.float32)
 
 
-def local_call(kernel, out_shapes, scalars, arrays, flops=0):
+def local_call(kernel, out_shapes, scalars, arrays, flops=0, scratch=()):
     size = sum(a.size * a.dtype.itemsize for a in arrays)
     size += sum(o.size * o.dtype.itemsize for o in out_shapes)
     return pl.pallas_call(
@@ -49,6 +49,7 @@
         in_specs=[pl.BlockSpec(memory_space=pltpu.SMEM)] * len(scalars)
         + [pl.BlockSpec(memory_space=pltpu.VMEM)] * len(arrays),
         out_specs=tuple([pl.BlockSpec(memory_space=pltpu.VMEM)] * len(out_shapes)),
+        scratch_shapes=list(scratch),
         compiler_params=pltpu.CompilerParams(vmem_limit_bytes=16 * 1024 * 1024),
         cost_estimate=pl.CostEstimate(flops=flops, bytes_accessed=size, transcendentals=0),
     )(*scalars, *arrays)
@@ -214,7 +215,7 @@
     )(*shards, weight)
 
 
-def frozen_kernel(n, early, place_ref, real_ref, *refs):
+def frozen_kernel(n, early, first, place_ref, real_ref, *refs):
     shards, weight, at_columns, down = refs[:n], refs[n], refs[n + 1], refs[n + 2]
     before = refs[n + 3 : n + 3 + early]
     out, total, extra, done, sems = refs[-5:]
@@ -237,11 +238,11 @@
         columns = at_columns.shape[2] - BLOCK
         blocks = [(a, k) for a in (*before, total) for k in range(a.shape[0] // BLOCK)]
         for i, (source, k) in enumerate(blocks):
-            block = place_ref[i * CORES] // CORES
+            block = place_ref[first + i * CORES] // CORES
             back = at_columns[block][:, columns:]
             extra[...] = dot(back, down[block], ((0,), (0,)))
             for j in range(CORES):
-                place = place_ref[i * CORES + j]
+                place = place_ref[first + i * CORES + j]
                 core = place % CORES
                 here = pl.ds(i * BLOCK + j * rows, rows)
                 value = source[pl.ds(k * BLOCK + j * rows, rows), :]
@@ -260,8 +261,8 @@
             copy.wait()
 
 
-def frozen_rows(places, real, shards, weight, at_columns, down, before, held=()):
-    n, early, count = len(shards), len(before), len(places)
+def frozen_rows(places, first, count, real, shards, weight, at_columns, down, before, held=()):
+    n, early = len(shards), len(before)
     rows, width = shards[0].shape
     features = weight.shape[0]
     all_rows = down.shape[0] * BLOCK
@@ -286,7 +287,7 @@
         ],
     )
     return pl.pallas_call(
-        lambda *refs: frozen_kernel(n, early, *refs),
+        lambda *refs: frozen_kernel(n, early, first, *refs),
         out_shape=jax.ShapeDtypeStruct((all_rows, features), jnp.bfloat16),
         grid_spec=grid_spec,
         input_output_aliases={n + early + 5: 0} if held else {},
@@ -297,7 +298,7 @@
             transcendentals=0,
         ),
     )(
-        jnp.stack(places).astype(jnp.int32),
+        places,
         real,
         *shards,
         weight,
@@ -437,8 +438,11 @@
         [at_columns, acts],
     )
     near_grads = x_exchange(grads)
+    all_places = jnp.stack(places(0, 1, -1, 2, -2, 3, -3, 4)).astype(jnp.int32)
     out = frozen_rows(
-        places(0, 1, -1, 2, -2, 3, -3),
+        all_places,
+        0,
+        7 * CORES,
         real,
         [a3, swap(b3), b3, swap(a3)],
         output_weight,
@@ -447,16 +451,17 @@
         early,
     )
     near_grads, out, a4 = lax.optimization_barrier((near_grads, out, a4))
-    (*summed, _) = local_call(
+    summed = local_call(
         slots_kernel,
-        [shaped(held_slots, rank, features + columns)] * SIDE
-        + [shaped(SIDE * held_slots, rank, features + columns, dtype=f32)],
+        [shaped(held_slots, rank, features + columns)] * SIDE,
         [at, slot_blk],
         near_grads,
+        0,
+        [pltpu.VMEM((SIDE * held_slots, rank, features + columns), f32)],
     )
     arrived = y_exchange(summed)
     input_gradient = frozen_rows(
-        places(4), real, [a4, swap(a4)], output_weight, at_columns, down_factor, (), (out,)
+        all_places, 7 * CORES, CORES, real, [a4, swap(a4)], output_weight, at_columns, down_factor, (), (out,)
     )
     arrived, input_gradient = lax.optimization_barrier((arrived, input_gradient))
     grad_down, grad_up = local_call(

time: 132 us -> 131 us (level)
    unnamed x16 -> x18, local copies, waits for them, and re-layouts: 4.07 us -> 5.05 us
  transfers between devices with their start and end apart: 31 -> 31, of which waited for: 9 -> 9; matrix products, arithmetic and copies ran while one was open for 4% -> 4% of each run, Pallas kernels for 32% -> 31%
where the time goes in v4:
time: 131 us
  starting transfers between devices  52.7 us (40%)
  Pallas kernels  41.2 us (31%)
  waiting for transfers between devices  26.4 us (20%)
  local copies, waits for them, and re-layouts  6.45 us (5%)
  other arithmetic  3.41 us (3%)
    pallas_call x2, Pallas kernels, frozen_rows(): pl.pallas_call(lambda *refs: frozen_kernel(n, early, first, *refs), out_s...  17.4 us
    pallas_call x2, Pallas kernels, early_rows(): pl.pallas_call(lambda *refs: early_kernel(n, *refs), out_shape=jax.ShapeD...  16 us
    all_to_all x2, waiting for transfers between devices, z_exchange(): lax.all_to_all(v, 'mp', 0, 0, tiled=True, axis_index_groups=same_core)  15.4 us
    ppermute x10, starting transfers between devices, swap(): return lax.ppermute(v, 'mp', [(i, i ^ 1) for i in range(mp)])  12.8 us
    ppermute x4, starting transfers between devices, ring_a(): return lax.ppermute(v, 'mp', ring_step(1, ring))  12.3 us
    ppermute x6, starting transfers between devices, y_exchange(): lax.ppermute(v, 'dp', y_step(shift))  10.4 us
    ppermute x6, starting transfers between devices, x_exchange(): return [v] + [lax.ppermute(v, 'dp', x_step(shift)) for shift in SHIFTS[1:]]  8.31 us
    all_to_all x2, starting transfers between devices, z_exchange(): lax.all_to_all(v, 'mp', 0, 0, tiled=True, axis_index_groups=same_core)  8.05 us
  transfers between devices with their start and end apart: 31, of which 9 were waited for; matrix products, arithmetic and copies ran while one was open for 4% of the time, Pallas kernels for 31%

profile of v4, /device:TPU:1, one launch (start us, length us, event | category | flops | bytes accessed | tf_op | source)
XLA Modules:
  0.0 131.0 jit_solution(5397283463278599039)
XLA Ops:
  0.6 6.5 %collective-permute-start.7 = (bf16[64,8192]{1,0:T(8,128)(2,1)}, bf16[64,8192]{1,0:T(8,128)(2,1)}, u32[]{:S(2)}, u32[]{:S(2)}) collective-permute-start(bf16[64,8192]{1,0:T(8,128)(2,1)} %own.1), channel_id=1, source_target_pairs={{0,2},{1,15},{2,4},{3,1},{4,6},{5,3},{6,8},{7,5},{8,10},{9,7},{10,... | collective-permute-start | bytes 3145736 | tf_op jit(solution)/shard_map/ppermute | solution.py:338
  8.0 1.3 collective-permute-start
  9.3 1.5 %collective-permute-start.1 = (bf16[4,16,1024]{2,1,0:T(8,128)(2,1)S(1)}, bf16[4,16,1024]{2,1,0:T(8,128)(2,1)S(1)}, u32[]{:S(2)}, u32[]{:S(2)}) collective-permute-start(bf16[4,16,1024]{2,1,0:T(8,128)(2,1)S(1)} %pad_maximum_fusion.refs_0_), channel_id=1, source_target_pairs={{0,48},{16,0},{32,16},{48,32},{64,112},{80,64},{96,80},{112,96},{1... | collective-permute-start | bytes 393224 | tf_op jit(solution)/shard_map/ppermute | solution.py:349
  10.8 1.5 %collective-permute-start.2 = (bf16[4,16,1024]{2,1,0:T(8,128)(2,1)S(1)}, bf16[4,16,1024]{2,1,0:T(8,128)(2,1)S(1)}, u32[]{:S(2)}, u32[]{:S(2)}) collective-permute-start(bf16[4,16,1024]{2,1,0:T(8,128)(2,1)S(1)} %pad_maximum_fusion.refs_0_), channel_id=1, source_target_pairs={{0,32},{16,48},{32,0},{48,16},{64,96},{80,112},{96,64},{112,80},{1... | collective-permute-start | bytes 393224 | tf_op jit(solution)/shard_map/ppermute | solution.py:349
  13.5 4.0 %collective-permute-done.2.refs_3_ = bf16[4,16,1024]{2,1,0:T(8,128)(2,1)S(1)} collective-permute-done((bf16[4,16,1024]{2,1,0:T(8,128)(2,1)S(1)}, bf16[4,16,1024]{2,1,0:T(8,128)(2,1)S(1)}, u32[]{:S(2)}, u32[]{:S(2)}) %collective-permute-start.2) | collective-permute-done | bytes 131104 | tf_op jit(solution)/shard_map/ppermute | solution.py:349
  18.6 1.4 %collective-permute-start.3 = (bf16[8,16,1024]{2,1,0:T(8,128)(2,1)S(1)}, bf16[8,16,1024]{2,1,0:T(8,128)(2,1)S(1)}, u32[]{:S(2)}, u32[]{:S(2)}) collective-permute-start(bf16[8,16,1024]{2,1,0:T(8,128)(2,1)S(1)} %get-tuple-element.40), channel_id=1, source_target_pairs={{0,64},{16,80},{32,96},{48,112},{64,128},{80,144},{96,160},{112,17... | collective-permute-start | bytes 786440 | tf_op jit(solution)/shard_map/ppermute | solution.py:353
  20.0 1.9 %collective-permute-start.6 = (bf16[64,8192]{1,0:T(8,128)(2,1)}, bf16[64,8192]{1,0:T(8,128)(2,1)}, u32[]{:S(2)}, u32[]{:S(2)}) collective-permute-start(bf16[64,8192]{1,0:T(8,128)(2,1)} %own.1), channel_id=1, source_target_pairs={{0,1},{1,0},{2,3},{3,2},{4,5},{5,4},{6,7},{7,6},{8,9},{9,8},{10,11... | collective-permute-start | bytes 3145736 | tf_op jit(solution)/shard_map/ppermute | solution.py:344
  21.9 1.4 %collective-permute-start.4 = (bf16[8,16,1024]{2,1,0:T(8,128)(2,1)S(1)}, bf16[8,16,1024]{2,1,0:T(8,128)(2,1)S(1)}, u32[]{:S(2)}, u32[]{:S(2)}) collective-permute-start(bf16[8,16,1024]{2,1,0:T(8,128)(2,1)S(1)} %get-tuple-element.41), channel_id=1, source_target_pairs={{0,192},{16,208},{32,224},{48,240},{64,0},{80,16},{96,32},{112,48}... | collective-permute-start | bytes 786440 | tf_op jit(solution)/shard_map/ppermute | solution.py:353
  23.3 3.1 %collective-permute-done.3.refs_1_ = bf16[8,16,1024]{2,1,0:T(8,128)(2,1)S(1)} collective-permute-done((bf16[8,16,1024]{2,1,0:T(8,128)(2,1)S(1)}, bf16[8,16,1024]{2,1,0:T(8,128)(2,1)S(1)}, u32[]{:S(2)}, u32[]{:S(2)}) %collective-permute-start.3) | collective-permute-done | bytes 262176 | tf_op jit(solution)/shard_map/ppermute | solution.py:353
  26.4 1.6 %collective-permute-start.5 = (bf16[8,16,1024]{2,1,0:T(8,128)(2,1)S(1)}, bf16[8,16,1024]{2,1,0:T(8,128)(2,1)S(1)}, u32[]{:S(2)}, u32[]{:S(2)}) collective-permute-start(bf16[8,16,1024]{2,1,0:T(8,128)(2,1)S(1)} %get-tuple-element.42), channel_id=1, source_target_pairs={{0,128},{16,144},{32,160},{48,176},{64,192},{80,208},{96,224},{112... | collective-permute-start | bytes 786440 | tf_op jit(solution)/shard_map/ppermute | solution.py:353
  27.9 1.2 collective-permute-done.7.refs_2_
  29.2 1.5 %collective-permute-start.10 = (bf16[64,8192]{1,0:T(8,128)(2,1)}, bf16[64,8192]{1,0:T(8,128)(2,1)}, u32[]{:S(2)}, u32[]{:S(2)}) collective-permute-start(bf16[64,8192]{1,0:T(8,128)(2,1)} %collective-permute-done.7.refs_2_), channel_id=1, source_target_pairs={{0,1},{1,0},{2,3},{3,2},{4,5},{5,4},{6,7},{7,6},{8,9},{9,8},{10,11... | collective-permute-start | bytes 3145736 | tf_op jit(solution)/shard_map/ppermute | solution.py:344
  32.4 2.5 %collective-permute-start.11 = (bf16[64,8192]{1,0:T(8,128)(2,1)}, bf16[64,8192]{1,0:T(8,128)(2,1)}, u32[]{:S(2)}, u32[]{:S(2)}) collective-permute-start(bf16[64,8192]{1,0:T(8,128)(2,1)} %collective-permute-done.7.refs_2_), channel_id=1, source_target_pairs={{0,2},{1,15},{2,4},{3,1},{4,6},{5,3},{6,8},{7,5},{8,10},{9,7},{10,... | collective-permute-start | bytes 3145736 | tf_op jit(solution)/shard_map/ppermute | solution.py:338
  36.7 1.2 copy-done.2
  38.5 6.2 %collective-permute-start.13 = (bf16[64,4096]{1,0:T(8,128)(2,1)S(1)}, bf16[64,4096]{1,0:T(8,128)(2,1)S(1)}, u32[]{:S(2)}, u32[]{:S(2)}) collective-permute-start(bf16[64,4096]{1,0:T(8,128)(2,1)S(1)} %get-tuple-element.45), channel_id=1, source_target_pairs={{0,1},{1,0},{2,3},{3,2},{4,5},{5,4},{6,7},{7,6},{8,9},{9,8},{10,11... | collective-permute-start | bytes 1572872 | tf_op jit(solution)/shard_map/ppermute | solution.py:344
  44.7 1.2 copy-done
  47.7 3.4 %all-to-all-start = ((bf16[8,16,768]{2,1,0:T(8,128)(2,1)}), bf16[8,16,768]{2,1,0:T(8,128)(2,1)S(1)}, u32[]{:S(2)}, u32[]{:S(2)}) async-start(bf16[8,16,768]{2,1,0:T(8,128)(2,1)} %get-tuple-element.43), calls=%async_computation | async-start | bytes 393216 | tf_op jit(solution)/shard_map/all_to_all | solution.py:356
  51.1 8.6 %shard_map.105.refs_9_ = f32[384,512]{1,0:T(8,128)} custom-call(bf16[64,8192]{1,0:T(8,128)(2,1)} %own.1, bf16[64,8192]{1,0:T(8,128)(2,1)} %collective-permute-done.6.refs_1_, bf16[64,8192]{1,0:T(8,128)(2,1)} %collective-permute-done.7.refs_2_, bf16[64,8192]{1,0:T(8,128)(2,1)} %collective-permute-done.9.refs_3_, ...), custom_call_target="tpu_custom_call" | custom-call | flops 3221225472 | bytes 14680064 | tf_op jit(solution)/shard_map/pallas_call | solution.py:202
  59.7 4.5 %all-to-all-done.at_rows = bf16[8,16,768]{2,1,0:T(8,128)(2,1)S(1)} async-done(((bf16[8,16,768]{2,1,0:T(8,128)(2,1)}), bf16[8,16,768]{2,1,0:T(8,128)(2,1)S(1)}, u32[]{:S(2)}, u32[]{:S(2)}) %all-to-all-start) | async-done | bytes 196640 | tf_op jit(solution)/shard_map/all_to_all | solution.py:356
  67.5 1.6 %collective-permute-start.14 = (f32[32,128]{1,0:T(8,128)S(1)}, f32[32,128]{1,0:T(8,128)S(1)}, u32[]{:S(2)}, u32[]{:S(2)}) collective-permute-start(f32[32,128]{1,0:T(8,128)S(1)} %shard_map.107.sums), channel_id=1, source_target_pairs={{0,1},{1,0},{2,3},{3,2},{4,5},{5,4},{6,7},{7,6},{8,9},{9,8},{10,11... | collective-permute-start | bytes 49160 | tf_op jit(solution)/shard_map/ppermute | solution.py:344
  69.9 1.6 %shard_map.108 = bf16[8,16,640]{2,1,0:T(8,128)(2,1)} custom-call(s32[4]{0:T(128)S(1)} %pad_add_fusion.at_ref, f32[32,128]{1,0:T(8,128)S(1)} %shard_map.107.sums, f32[32,128]{1,0:T(8,128)S(1)} %collective-permute-done.14.more, bf16[64,4096]{1,0:T(8,128)(2,1)S(1)} %get-tuple-element.47.mine, bf16[64,4096]{1,0:T(8,128)(2,1)S(1)} %collective-permute-done.13.other), custom_call_target="tpu_custom_call" | custom-call | bytes 1245184 | tf_op jit(solution)/shard_map/pallas_call | solution.py:46
  71.5 4.7 %all-to-all-start.1 = ((bf16[8,16,640]{2,1,0:T(8,128)(2,1)}), bf16[8,16,640]{2,1,0:T(8,128)(2,1)S(1)}, u32[]{:S(2)}, u32[]{:S(2)}) async-start(bf16[8,16,640]{2,1,0:T(8,128)(2,1)} %shard_map.108), calls=%async_computation.1 | async-start | bytes 327680 | tf_op jit(solution)/shard_map/all_to_all | solution.py:356
  77.2 7.4 %shard_map.109.refs_10_ = f32[256,512]{1,0:T(8,128)} custom-call(bf16[64,8192]{1,0:T(8,128)(2,1)} %collective-permute-done.11.refs_0_, bf16[64,8192]{1,0:T(8,128)(2,1)} %copy-done.7, bf16[64,8192]{1,0:T(8,128)(2,1)} %collective-permute-done.12.refs_2_, bf16[64,8192]{1,0:T(8,128)(2,1)} %collective-permute-done.16.refs_3_, bf16[512,8192]{1,0:T(8,128)(2,1)} %refs_4_.5), custom_call_target="tpu_custom_call" | custom-call | flops 2147483648 | bytes 12582912 | tf_op jit(solution)/shard_map/pallas_call | solution.py:202
  84.5 11.0 %all-to-all-done.1.at_columns.refs_7_.refs_5_ = bf16[8,16,640]{2,1,0:T(8,128)(2,1)S(1)} async-done(((bf16[8,16,640]{2,1,0:T(8,128)(2,1)}), bf16[8,16,640]{2,1,0:T(8,128)(2,1)S(1)}, u32[]{:S(2)}, u32[]{:S(2)}) %all-to-all-start.1) | async-done | bytes 163872 | tf_op jit(solution)/shard_map/all_to_all | solution.py:356
  96.6 2.3 %collective-permute-start.24 = (bf16[64,8192]{1,0:T(8,128)(2,1)}, bf16[64,8192]{1,0:T(8,128)(2,1)S(1)}, u32[]{:S(2)}, u32[]{:S(2)}) collective-permute-start(bf16[64,8192]{1,0:T(8,128)(2,1)} %collective-permute-done.17.refs_2_), channel_id=1, source_target_pairs={{0,2},{1,15},{2,4},{3,1},{4,6},{5,3},{6,8},{7,5},{8,10},{9,7},{10,... | collective-permute-start | bytes 3145736 | tf_op jit(solution)/shard_map/ppermute | solution.py:338
  100.2 1.7 %collective-permute-start.20 = (bf16[8,16,1024]{2,1,0:T(8,128)(2,1)S(1)}, bf16[8,16,1024]{2,1,0:T(8,128)(2,1)S(1)}, u32[]{:S(2)}, u32[]{:S(2)}) collective-permute-start(bf16[8,16,1024]{2,1,0:T(8,128)(2,1)S(1)} %shard_map.110.refs_0_), channel_id=1, source_target_pairs={{0,48},{16,0},{32,16},{48,32},{64,112},{80,64},{96,80},{112,96},{1... | collective-permute-start | bytes 786440 | tf_op jit(solution)/shard_map/ppermute | solution.py:349
  102.0 1.3 collective-permute-start.21
  103.9 9.4 %shard_map.111.refs_7_ = bf16[1024,512]{1,0:T(8,128)(2,1)} custom-call(s32[16]{0:T(128)} %stack.87.refs_0_, s32[8]{0:T(128)} %copy-done.5, bf16[64,8192]{1,0:T(8,128)(2,1)} %collective-permute-done.17.refs_2_, bf16[64,8192]{1,0:T(8,128)(2,1)} %collective-permute-done.22.refs_3_, bf16[64,8192]{1,0:T(8,128)(2,1)} %collective-permute-done.18.refs_4_, ...), custom_call_target="tpu_custom_call" | custom-call | flops 2147483648 | bytes 12582912 | tf_op jit(solution)/shard_map/pallas_call | solution.py:289
  113.7 1.4 %shard_map.112 = (bf16[4,16,1024]{2,1,0:T(8,128)(2,1)S(1)}, bf16[4,16,1024]{2,1,0:T(8,128)(2,1)S(1)}, bf16[4,16,1024]{2,1,0:T(8,128)(2,1)S(1)}, bf16[4,16,1024]{2,1,0:T(8,128)(2,1)S(1)}) custom-call(s32[4]{0:T(128)S(1)} %pad_add_fusion.at_ref, s32[128]{0:T(128)S(1)} %select_reduce_fusion.slot_ref, bf16[8,16,1024]{2,1,0:T(8,128)(2,1)S(1)} %shard_map.110.refs_0_, ...), custom_call_target="tpu_custom_call" | custom-call | bytes 1572864 | tf_op jit(solution)/shard_map/pallas_call | solution.py:46
  115.1 2.9 %collective-permute-start.25 = (bf16[4,16,1024]{2,1,0:T(8,128)(2,1)S(1)}, bf16[4,16,1024]{2,1,0:T(8,128)(2,1)S(1)}, u32[]{:S(2)}, u32[]{:S(2)}) collective-permute-start(bf16[4,16,1024]{2,1,0:T(8,128)(2,1)S(1)} %get-tuple-element.63), channel_id=1, source_target_pairs={{0,64},{16,80},{32,96},{48,112},{64,128},{80,144},{96,160},{112,17... | collective-permute-start | bytes 393224 | tf_op jit(solution)/shard_map/ppermute | solution.py:353
  118.0 2.1 %collective-permute-start.26 = (bf16[4,16,1024]{2,1,0:T(8,128)(2,1)S(1)}, bf16[4,16,1024]{2,1,0:T(8,128)(2,1)S(1)}, u32[]{:S(2)}, u32[]{:S(2)}) collective-permute-start(bf16[4,16,1024]{2,1,0:T(8,128)(2,1)S(1)} %get-tuple-element.64), channel_id=1, source_target_pairs={{0,192},{16,208},{32,224},{48,240},{64,0},{80,16},{96,32},{112,48}... | collective-permute-start | bytes 393224 | tf_op jit(solution)/shard_map/ppermute | solution.py:353
  122.2 8.0 %shard_map.113 = bf16[1024,512]{1,0:T(8,128)(2,1)} custom-call(s32[16]{0:T(128)} %stack.87.refs_0_, s32[8]{0:T(128)} %copy-done.5, bf16[64,8192]{1,0:T(8,128)(2,1)} %copy-done.6, bf16[64,8192]{1,0:T(8,128)(2,1)} %copy-done.8, bf16[512,8192]{1,0:T(8,128)(2,1)} %refs_4_.5, bf16[8,16,640]{2,1,0:T(8,128)(2,1)} %copy-done.3, ...), custom_call_target="tpu_custom_call", output_to_operand_aliasing={{}: (7, {})} | custom-call | flops 1073741824 | bytes 10485760 | tf_op jit(solution)/shard_map/pallas_call | solution.py:289
  (69 shorter events, 20.4 us)
Async XLA Ops:
  0.6 28.5 %collective-permute-start.7 = (bf16[64,8192]{1,0:T(8,128)(2,1)}, bf16[64,8192]{1,0:T(8,128)(2,1)}, u32[]{:S(2)}, u32[]{:S(2)}) collective-permute-start(bf16[64,8192]{1,0:T(8,128)(2,1)} %own.1), channel_id=1, source_target_pairs={{0,2},{1,15},{2,4},{3,1},{4,6},{5,3},{6,8},{7,5},{8,10},{9,7},{10,... | collective-permute-start | bytes 3145736 | tf_op jit(solution)/shard_map/ppermute | solution.py:338
  7.1 24.6 %collective-permute-start.8 = (bf16[64,8192]{1,0:T(8,128)(2,1)}, bf16[64,8192]{1,0:T(8,128)(2,1)}, u32[]{:S(2)}, u32[]{:S(2)}) collective-permute-start(bf16[64,8192]{1,0:T(8,128)(2,1)} %own.1), channel_id=1, source_target_pairs={{0,14},{1,3},{2,0},{3,5},{4,2},{5,7},{6,4},{7,9},{8,6},{9,11},{10,... | collective-permute-start | bytes 3145736 | tf_op jit(solution)/shard_map/ppermute | solution.py:341
  8.0 5.5 %collective-permute-start = (bf16[4,16,1024]{2,1,0:T(8,128)(2,1)S(1)}, bf16[4,16,1024]{2,1,0:T(8,128)(2,1)S(1)}, u32[]{:S(2)}, u32[]{:S(2)}) collective-permute-start(bf16[4,16,1024]{2,1,0:T(8,128)(2,1)S(1)} %pad_maximum_fusion.refs_0_), channel_id=1, source_target_pairs={{0,16},{16,32},{32,48},{48,0},{64,80},{80,96},{96,112},{112,64},{1... | collective-permute-start | bytes 393224 | tf_op jit(solution)/shard_map/ppermute | solution.py:349
  9.3 4.2 %collective-permute-start.1 = (bf16[4,16,1024]{2,1,0:T(8,128)(2,1)S(1)}, bf16[4,16,1024]{2,1,0:T(8,128)(2,1)S(1)}, u32[]{:S(2)}, u32[]{:S(2)}) collective-permute-start(bf16[4,16,1024]{2,1,0:T(8,128)(2,1)S(1)} %pad_maximum_fusion.refs_0_), channel_id=1, source_target_pairs={{0,48},{16,0},{32,16},{48,32},{64,112},{80,64},{96,80},{112,96},{1... | collective-permute-start | bytes 393224 | tf_op jit(solution)/shard_map/ppermute | solution.py:349
  10.8 6.7 %collective-permute-start.2 = (bf16[4,16,1024]{2,1,0:T(8,128)(2,1)S(1)}, bf16[4,16,1024]{2,1,0:T(8,128)(2,1)S(1)}, u32[]{:S(2)}, u32[]{:S(2)}) collective-permute-start(bf16[4,16,1024]{2,1,0:T(8,128)(2,1)S(1)} %pad_maximum_fusion.refs_0_), channel_id=1, source_target_pairs={{0,32},{16,48},{32,0},{48,16},{64,96},{80,112},{96,64},{112,80},{1... | collective-permute-start | bytes 393224 | tf_op jit(solution)/shard_map/ppermute | solution.py:349
  18.6 7.7 %collective-permute-start.3 = (bf16[8,16,1024]{2,1,0:T(8,128)(2,1)S(1)}, bf16[8,16,1024]{2,1,0:T(8,128)(2,1)S(1)}, u32[]{:S(2)}, u32[]{:S(2)}) collective-permute-start(bf16[8,16,1024]{2,1,0:T(8,128)(2,1)S(1)} %get-tuple-element.40), channel_id=1, source_target_pairs={{0,64},{16,80},{32,96},{48,112},{64,128},{80,144},{96,160},{112,17... | collective-permute-start | bytes 786440 | tf_op jit(solution)/shard_map/ppermute | solution.py:353
  20.0 18.5 %collective-permute-start.6 = (bf16[64,8192]{1,0:T(8,128)(2,1)}, bf16[64,8192]{1,0:T(8,128)(2,1)}, u32[]{:S(2)}, u32[]{:S(2)}) collective-permute-start(bf16[64,8192]{1,0:T(8,128)(2,1)} %own.1), channel_id=1, source_target_pairs={{0,1},{1,0},{2,3},{3,2},{4,5},{5,4},{6,7},{7,6},{8,9},{9,8},{10,11... | collective-permute-start | bytes 3145736 | tf_op jit(solution)/shard_map/ppermute | solution.py:344
  21.9 10.5 %collective-permute-start.4 = (bf16[8,16,1024]{2,1,0:T(8,128)(2,1)S(1)}, bf16[8,16,1024]{2,1,0:T(8,128)(2,1)S(1)}, u32[]{:S(2)}, u32[]{:S(2)}) collective-permute-start(bf16[8,16,1024]{2,1,0:T(8,128)(2,1)S(1)} %get-tuple-element.41), channel_id=1, source_target_pairs={{0,192},{16,208},{32,224},{48,240},{64,0},{80,16},{96,32},{112,48}... | collective-permute-start | bytes 786440 | tf_op jit(solution)/shard_map/ppermute | solution.py:353
  26.4 8.6 %collective-permute-start.5 = (bf16[8,16,1024]{2,1,0:T(8,128)(2,1)S(1)}, bf16[8,16,1024]{2,1,0:T(8,128)(2,1)S(1)}, u32[]{:S(2)}, u32[]{:S(2)}) collective-permute-start(bf16[8,16,1024]{2,1,0:T(8,128)(2,1)S(1)} %get-tuple-element.42), channel_id=1, source_target_pairs={{0,128},{16,144},{32,160},{48,176},{64,192},{80,208},{96,224},{112... | collective-permute-start | bytes 786440 | tf_op jit(solution)/shard_map/ppermute | solution.py:353
  29.2 21.9 %collective-permute-start.10 = (bf16[64,8192]{1,0:T(8,128)(2,1)}, bf16[64,8192]{1,0:T(8,128)(2,1)}, u32[]{:S(2)}, u32[]{:S(2)}) collective-permute-start(bf16[64,8192]{1,0:T(8,128)(2,1)} %collective-permute-done.7.refs_2_), channel_id=1, source_target_pairs={{0,1},{1,0},{2,3},{3,2},{4,5},{5,4},{6,7},{7,6},{8,9},{9,8},{10,11... | collective-permute-start | bytes 3145736 | tf_op jit(solution)/shard_map/ppermute | solution.py:344
  31.7 19.4 %collective-permute-start.9 = (bf16[64,8192]{1,0:T(8,128)(2,1)}, bf16[64,8192]{1,0:T(8,128)(2,1)}, u32[]{:S(2)}, u32[]{:S(2)}) collective-permute-start(bf16[64,8192]{1,0:T(8,128)(2,1)} %collective-permute-done.8.refs_4_), channel_id=1, source_target_pairs={{0,1},{1,0},{2,3},{3,2},{4,5},{5,4},{6,7},{7,6},{8,9},{9,8},{10,11... | collective-permute-start | bytes 3145736 | tf_op jit(solution)/shard_map/ppermute | solution.py:344
  32.4 31.8 %collective-permute-start.11 = (bf16[64,8192]{1,0:T(8,128)(2,1)}, bf16[64,8192]{1,0:T(8,128)(2,1)}, u32[]{:S(2)}, u32[]{:S(2)}) collective-permute-start(bf16[64,8192]{1,0:T(8,128)(2,1)} %collective-permute-done.7.refs_2_), channel_id=1, source_target_pairs={{0,2},{1,15},{2,4},{3,1},{4,6},{5,3},{6,8},{7,5},{8,10},{9,7},{10,... | collective-permute-start | bytes 3145736 | tf_op jit(solution)/shard_map/ppermute | solution.py:338
  35.0 29.3 %collective-permute-start.12 = (bf16[64,8192]{1,0:T(8,128)(2,1)}, bf16[64,8192]{1,0:T(8,128)(2,1)}, u32[]{:S(2)}, u32[]{:S(2)}) collective-permute-start(bf16[64,8192]{1,0:T(8,128)(2,1)} %collective-permute-done.8.refs_4_), channel_id=1, source_target_pairs={{0,14},{1,3},{2,0},{3,5},{4,2},{5,7},{6,4},{7,9},{8,6},{9,11},{10,... | collective-permute-start | bytes 3145736 | tf_op jit(solution)/shard_map/ppermute | solution.py:341
  38.5 21.2 %collective-permute-start.13 = (bf16[64,4096]{1,0:T(8,128)(2,1)S(1)}, bf16[64,4096]{1,0:T(8,128)(2,1)S(1)}, u32[]{:S(2)}, u32[]{:S(2)}) collective-permute-start(bf16[64,4096]{1,0:T(8,128)(2,1)S(1)} %get-tuple-element.45), channel_id=1, source_target_pairs={{0,1},{1,0},{2,3},{3,2},{4,5},{5,4},{6,7},{7,6},{8,9},{9,8},{10,11... | collective-permute-start | bytes 1572872 | tf_op jit(solution)/shard_map/ppermute | solution.py:344
  47.7 16.6 %all-to-all-start = ((bf16[8,16,768]{2,1,0:T(8,128)(2,1)}), bf16[8,16,768]{2,1,0:T(8,128)(2,1)S(1)}, u32[]{:S(2)}, u32[]{:S(2)}) async-start(bf16[8,16,768]{2,1,0:T(8,128)(2,1)} %get-tuple-element.43), calls=%async_computation | async-start | bytes 393216 | tf_op jit(solution)/shard_map/all_to_all | solution.py:356
  59.7 39.2 %copy-start.1 = (bf16[1024,512]{1,0:T(8,128)(2,1)S(1)}, bf16[1024,512]{1,0:T(8,128)(2,1)}, u32[]{:S(2)}) copy-start(bf16[1024,512]{1,0:T(8,128)(2,1)} %acts.1) | copy-start | bytes 3145732
  64.2 12.0 %collective-permute-start.15 = (bf16[64,8192]{1,0:T(8,128)(2,1)}, bf16[64,8192]{1,0:T(8,128)(2,1)S(1)}, u32[]{:S(2)}, u32[]{:S(2)}) collective-permute-start(bf16[64,8192]{1,0:T(8,128)(2,1)} %collective-permute-done.12.refs_2_), channel_id=1, source_target_pairs={{0,1},{1,0},{2,3},{3,2},{4,5},{5,4},{6,7},{7,6},{8,9},{9,8},{10,11... | collective-permute-start | bytes 3145736 | tf_op jit(solution)/shard_map/ppermute | solution.py:344
  64.2 12.0 %collective-permute-start.16 = (bf16[64,8192]{1,0:T(8,128)(2,1)}, bf16[64,8192]{1,0:T(8,128)(2,1)}, u32[]{:S(2)}, u32[]{:S(2)}) collective-permute-start(bf16[64,8192]{1,0:T(8,128)(2,1)} %collective-permute-done.11.refs_0_), channel_id=1, source_target_pairs={{0,1},{1,0},{2,3},{3,2},{4,5},{5,4},{6,7},{7,6},{8,9},{9,8},{10,11... | collective-permute-start | bytes 3145736 | tf_op jit(solution)/shard_map/ppermute | solution.py:344
  64.7 30.8 %collective-permute-start.17 = (bf16[64,8192]{1,0:T(8,128)(2,1)}, bf16[64,8192]{1,0:T(8,128)(2,1)}, u32[]{:S(2)}, u32[]{:S(2)}) collective-permute-start(bf16[64,8192]{1,0:T(8,128)(2,1)} %collective-permute-done.11.refs_0_), channel_id=1, source_target_pairs={{0,2},{1,15},{2,4},{3,1},{4,6},{5,3},{6,8},{7,5},{8,10},{9,7},{10,... | collective-permute-start | bytes 3145736 | tf_op jit(solution)/shard_map/ppermute | solution.py:338
  65.7 29.8 %collective-permute-start.18 = (bf16[64,8192]{1,0:T(8,128)(2,1)}, bf16[64,8192]{1,0:T(8,128)(2,1)}, u32[]{:S(2)}, u32[]{:S(2)}) collective-permute-start(bf16[64,8192]{1,0:T(8,128)(2,1)} %collective-permute-done.12.refs_2_), channel_id=1, source_target_pairs={{0,14},{1,3},{2,0},{3,5},{4,2},{5,7},{6,4},{7,9},{8,6},{9,11},{10,... | collective-permute-start | bytes 3145736 | tf_op jit(solution)/shard_map/ppermute | solution.py:341
  67.5 2.4 %collective-permute-start.14 = (f32[32,128]{1,0:T(8,128)S(1)}, f32[32,128]{1,0:T(8,128)S(1)}, u32[]{:S(2)}, u32[]{:S(2)}) collective-permute-start(f32[32,128]{1,0:T(8,128)S(1)} %shard_map.107.sums), channel_id=1, source_target_pairs={{0,1},{1,0},{2,3},{3,2},{4,5},{5,4},{6,7},{7,6},{8,9},{9,8},{10,11... | collective-permute-start | bytes 49160 | tf_op jit(solution)/shard_map/ppermute | solution.py:344
  71.5 24.0 %all-to-all-start.1 = ((bf16[8,16,640]{2,1,0:T(8,128)(2,1)}), bf16[8,16,640]{2,1,0:T(8,128)(2,1)S(1)}, u32[]{:S(2)}, u32[]{:S(2)}) async-start(bf16[8,16,640]{2,1,0:T(8,128)(2,1)} %shard_map.108), calls=%async_computation.1 | async-start | bytes 327680 | tf_op jit(solution)/shard_map/all_to_all | solution.py:356
  95.5 6.5 %collective-permute-start.22 = (bf16[64,8192]{1,0:T(8,128)(2,1)}, bf16[64,8192]{1,0:T(8,128)(2,1)}, u32[]{:S(2)}, u32[]{:S(2)}) collective-permute-start(bf16[64,8192]{1,0:T(8,128)(2,1)} %collective-permute-done.18.refs_4_), channel_id=1, source_target_pairs={{0,1},{1,0},{2,3},{3,2},{4,5},{5,4},{6,7},{7,6},{8,9},{9,8},{10,11... | collective-permute-start | bytes 3145736 | tf_op jit(solution)/shard_map/ppermute | solution.py:344
  96.5 7.4 %collective-permute-start.23 = (bf16[64,8192]{1,0:T(8,128)(2,1)}, bf16[64,8192]{1,0:T(8,128)(2,1)}, u32[]{:S(2)}, u32[]{:S(2)}) collective-permute-start(bf16[64,8192]{1,0:T(8,128)(2,1)} %collective-permute-done.17.refs_2_), channel_id=1, source_target_pairs={{0,1},{1,0},{2,3},{3,2},{4,5},{5,4},{6,7},{7,6},{8,9},{9,8},{10,11... | collective-permute-start | bytes 3145736 | tf_op jit(solution)/shard_map/ppermute | solution.py:344
  96.6 17.1 %collective-permute-start.24 = (bf16[64,8192]{1,0:T(8,128)(2,1)}, bf16[64,8192]{1,0:T(8,128)(2,1)S(1)}, u32[]{:S(2)}, u32[]{:S(2)}) collective-permute-start(bf16[64,8192]{1,0:T(8,128)(2,1)} %collective-permute-done.17.refs_2_), channel_id=1, source_target_pairs={{0,2},{1,15},{2,4},{3,1},{4,6},{5,3},{6,8},{7,5},{8,10},{9,7},{10,... | collective-permute-start | bytes 3145736 | tf_op jit(solution)/shard_map/ppermute | solution.py:338
  99.2 14.2 %collective-permute-start.19 = (bf16[8,16,1024]{2,1,0:T(8,128)(2,1)S(1)}, bf16[8,16,1024]{2,1,0:T(8,128)(2,1)S(1)}, u32[]{:S(2)}, u32[]{:S(2)}) collective-permute-start(bf16[8,16,1024]{2,1,0:T(8,128)(2,1)S(1)} %shard_map.110.refs_0_), channel_id=1, source_target_pairs={{0,16},{16,32},{32,48},{48,0},{64,80},{80,96},{96,112},{112,64},{1... | collective-permute-start | bytes 786440 | tf_op jit(solution)/shard_map/ppermute | solution.py:349
  100.2 13.2 %collective-permute-start.20 = (bf16[8,16,1024]{2,1,0:T(8,128)(2,1)S(1)}, bf16[8,16,1024]{2,1,0:T(8,128)(2,1)S(1)}, u32[]{:S(2)}, u32[]{:S(2)}) collective-permute-start(bf16[8,16,1024]{2,1,0:T(8,128)(2,1)S(1)} %shard_map.110.refs_0_), channel_id=1, source_target_pairs={{0,48},{16,0},{32,16},{48,32},{64,112},{80,64},{96,80},{112,96},{1... | collective-permute-start | bytes 786440 | tf_op jit(solution)/shard_map/ppermute | solution.py:349
  102.0 11.8 %collective-permute-start.21 = (bf16[8,16,1024]{2,1,0:T(8,128)(2,1)S(1)}, bf16[8,16,1024]{2,1,0:T(8,128)(2,1)S(1)}, u32[]{:S(2)}, u32[]{:S(2)}) collective-permute-start(bf16[8,16,1024]{2,1,0:T(8,128)(2,1)S(1)} %shard_map.110.refs_0_), channel_id=1, source_target_pairs={{0,32},{16,48},{32,0},{48,16},{64,96},{80,112},{96,64},{112,80},{1... | collective-permute-start | bytes 786440 | tf_op jit(solution)/shard_map/ppermute | solution.py:349
  113.7 7.5 %collective-permute-start.28 = (bf16[64,8192]{1,0:T(8,128)(2,1)S(1)}, bf16[64,8192]{1,0:T(8,128)(2,1)S(1)}, u32[]{:S(2)}, u32[]{:S(2)}) collective-permute-start(bf16[64,8192]{1,0:T(8,128)(2,1)S(1)} %collective-permute-done.24.refs_2_), channel_id=1, source_target_pairs={{0,1},{1,0},{2,3},{3,2},{4,5},{5,4},{6,7},{7,6},{8,9},{9,8},{10,11... | collective-permute-start | bytes 3145736 | tf_op jit(solution)/shard_map/ppermute | solution.py:344
  115.1 15.1 %collective-permute-start.25 = (bf16[4,16,1024]{2,1,0:T(8,128)(2,1)S(1)}, bf16[4,16,1024]{2,1,0:T(8,128)(2,1)S(1)}, u32[]{:S(2)}, u32[]{:S(2)}) collective-permute-start(bf16[4,16,1024]{2,1,0:T(8,128)(2,1)S(1)} %get-tuple-element.63), channel_id=1, source_target_pairs={{0,64},{16,80},{32,96},{48,112},{64,128},{80,144},{96,160},{112,17... | collective-permute-start | bytes 393224 | tf_op jit(solution)/shard_map/ppermute | solution.py:353
  118.0 12.2 %collective-permute-start.26 = (bf16[4,16,1024]{2,1,0:T(8,128)(2,1)S(1)}, bf16[4,16,1024]{2,1,0:T(8,128)(2,1)S(1)}, u32[]{:S(2)}, u32[]{:S(2)}) collective-permute-start(bf16[4,16,1024]{2,1,0:T(8,128)(2,1)S(1)} %get-tuple-element.64), channel_id=1, source_target_pairs={{0,192},{16,208},{32,224},{48,240},{64,0},{80,16},{96,32},{112,48}... | collective-permute-start | bytes 393224 | tf_op jit(solution)/shard_map/ppermute | solution.py:353
  120.1 10.1 %collective-permute-start.27 = (bf16[4,16,1024]{2,1,0:T(8,128)(2,1)S(1)}, bf16[4,16,1024]{2,1,0:T(8,128)(2,1)S(1)}, u32[]{:S(2)}, u32[]{:S(2)}) collective-permute-start(bf16[4,16,1024]{2,1,0:T(8,128)(2,1)S(1)} %get-tuple-element.65), channel_id=1, source_target_pairs={{0,128},{16,144},{32,160},{48,176},{64,192},{80,208},{96,224},{112... | collective-permute-start | bytes 393224 | tf_op jit(solution)/shard_map/ppermute | solution.py:353
  (8 other events, 42.8 us)
